TPU v7x, 32 devices: a whole 2x2x4 slice. The times are simulated.
32 devices in a mesh: section: 2 (over x), row: 4 (over z), col: 4 (over y, core).
Axes of the slice: x: 2, y: 2, z: 4, core: 2. Of those that a mesh axis runs over, the one named last changes fastest.
Arguments:
- x_in: bfloat16 [2, 4, 768, 1024], P(None, 'row', None, 'col'), may hold values from -6 to 6
- targets: bfloat16 [2, 4, 768, 1024], P(None, 'row', None, 'col'), may hold values from -6 to 6
- w_query: bfloat16 [2, 1024, 1024], P('section', 'row', 'col'), may hold values from -0.1875 to 0.1875
- w_key: bfloat16 [2, 1024, 512], P('section', 'row', 'col'), may hold values from -0.1875 to 0.1875
- w_value: bfloat16 [2, 1024, 512], P('section', 'row', 'col'), may hold values from -0.1875 to 0.1875
- w_out: bfloat16 [2, 1024, 1024], P('section', 'col', 'row'), may hold values from -0.75 to 0.75
- w_gate: bfloat16 [2, 32, 1024, 512], P('section', 'col', 'row'), may hold values from -0.1875 to 0.1875
- w_up: bfloat16 [2, 32, 1024, 512], P('section', 'col', 'row'), may hold values from -0.1875 to 0.1875
- w_down: bfloat16 [2, 32, 512, 1024], P('section', 'col', None, 'row'), may hold values from -0.75 to 0.75
- gain_attn: bfloat16 [2, 1024], P('section'), may hold values from 0.5 to 1.5
- gain_ffn: bfloat16 [2, 1024], P('section'), may hold values from 0.5 to 1.5
- expert_ids: int32 [2, 2, 4, 768, 8], P('section', None, 'row'), may hold values from 0 to 31, all different within a row; in each aligned block of 768 rows (0 to 767, 768 to 1535, ..., all dimensions but the last counted through in order) at most 384 rows name the same one
- gates: float32 [2, 2, 4, 768, 8], P('section', None, 'row'), may hold values from 0.06 to 0.2
- lengths: int32 [2, 4], replicated, may hold values from 1 to 512, 1536 in all within a row
Outputs:
- outputs: bfloat16 [2, 2, 4, 768, 1024], P('section', None, 'row', None, 'col')
- loss: float32 [], replicated
- input_grads: bfloat16 [2, 2, 4, 768, 1024], P('section', None, 'row', None, 'col')
- grad_query: float32 [2, 1024, 1024], P('section', 'row', 'col')
- grad_key: float32 [2, 1024, 512], P('section', 'row', 'col')
- grad_value: float32 [2, 1024, 512], P('section', 'row', 'col')
- grad_out: float32 [2, 1024, 1024], P('section', 'col', 'row')
- grad_gate: float32 [2, 32, 1024, 512], P('section', 'col', 'row')
- grad_up: float32 [2, 32, 1024, 512], P('section', 'col', 'row')
- grad_down: float32 [2, 32, 512, 1024], P('section', 'col', None, 'row')
- grad_gain_attn: float32 [2, 1024], P('section', 'col')
- grad_gain_ffn: float32 [2, 1024], P('section', 'col')
Inputs may be any that keep to these rules, and one draw needn't show every extreme that they name: `expert_ids`: in each aligned block of 768 rows (one group of one micro-batch at one section) a row names 8 different experts, no expert is named by more than 384 rows, a bound that some block reaches. Each micro-batch's lengths sum to 1536, and its largest is exactly 512.
All inputs are finite; a program needn't handle non-finite values.
Results may differ from a plain program's by a relative error of at most 0.02.
Values may be sent and summed in bfloat16 or wider, within the bound.
No kernel may reach another device: no remote copies, remote signals or barrier semaphores. Data moves between devices by JAX's collectives and lax.ppermute only.
A program may use at most 384 MiB of HBM per device.

v0:
```python
import jax
import jax.numpy as jnp
from jax import lax
from jax.sharding import PartitionSpec as P

HEAD = 64
HIDDEN_SIZE = 512
CONT_LEN = 512
CAP = 384


EPS = 1e-06
THETA = 10000.0
NEG = -1e30


def from_behind(value, axis, steps):
    count = lax.axis_size(axis)
    initial, last = (max(0, -steps), min(count, count - steps))
    return lax.ppermute(value, axis, [(source, source + steps) for source in range(initial, last)])


def tables(positions, head_size):
    freqs = THETA ** (-(jnp.arange(head_size // 2).astype(jnp.float32) * 2.0) / head_size)
    angles = positions.astype(jnp.float32)[:, None] * freqs[None, :]
    return (jnp.cos(angles)[:, None, :], jnp.sin(angles)[:, None, :])


def rotate(value, cosine, sine):
    half = value.shape[-1] // 2
    first = value[..., :half]
    second = value[..., half:]
    return jnp.concatenate(
        [first * cosine - second * sine, second * cosine + first * sine], axis=-1
    )


def spread(value):
    return lax.all_gather(value, "col", axis=1, tiled=True)


def collect(value):
    return lax.psum_scatter(
        value.astype(jnp.bfloat16), "col", scatter_dimension=1, tiled=True
    ).astype(jnp.float32)


def spread_grad(value):
    return lax.all_gather(value, "col", axis=1, tiled=True)


def collect_grad(value):
    return lax.psum_scatter(value, "col", scatter_dimension=1, tiled=True)


def norm_total(value):
    return lax.psum(value, "col")


def contract_last(left, right):
    return lax.dot_general(
        left, right, (((1,), (1,)), ((), ())), preferred_element_type=jnp.float32
    )


def contract_first(left, right):
    return lax.dot_general(
        left, right, (((0,), (0,)), ((), ())), preferred_element_type=jnp.float32
    )


def fetch(w_query, w_key, w_value, w_out, w_gate, w_up, w_down):
    full_query, full_key, full_value, full_out, full_gate, full_up, full_down = (
        lax.all_gather(w_query[0], "row", axis=0, tiled=True),
        lax.all_gather(w_key[0], "row", axis=0, tiled=True),
        lax.all_gather(w_value[0], "row", axis=0, tiled=True),
        lax.all_gather(w_out[0], "row", axis=1, tiled=True),
        lax.all_gather(w_gate[0], "row", axis=1, tiled=True),
        lax.all_gather(w_up[0], "row", axis=1, tiled=True),
        lax.all_gather(w_down[0], "row", axis=2, tiled=True),
    )
    return {
        "qkv": jnp.concatenate([full_query, full_key, full_value], axis=1),
        "out": full_out,
        "gate_up": jnp.concatenate([full_gate, full_up], axis=2),
        "down": full_down,
    }


def attention_scores(grouped, keys, allowed):
    scores = jnp.einsum(
        "tgrd,kgd->grtk", grouped, keys, preferred_element_type=jnp.float32
    ) * grouped.shape[-1] ** (-0.5)
    return jnp.where(allowed[None, None], scores, NEG)


def forward_layer(
    layer_in, fetched, gain_first, gain_second, routes, weights_in, row_rank, col_rank
):
    tokens = layer_in.shape[0]
    prompt_rows = tokens - CONT_LEN
    prompt_len = prompt_rows * lax.axis_size("row")
    width = fetched["qkv"].shape[0]
    query_cols = fetched["out"].shape[0]
    kv_cols = (fetched["qkv"].shape[1] - query_cols) // 2
    kv_heads = kv_cols // HEAD
    repeat = query_cols // kv_cols
    residual = layer_in.astype(jnp.float32)
    whole = spread(layer_in).astype(jnp.float32)
    scale_first = lax.rsqrt(jnp.mean(whole * whole, axis=1, keepdims=True) + EPS)
    normed = (whole * scale_first * gain_first).astype(jnp.bfloat16)
    projected = jnp.dot(normed, fetched["qkv"], preferred_element_type=jnp.float32)
    positions = jnp.concatenate(
        [
            row_rank * prompt_rows + jnp.arange(prompt_rows, dtype=jnp.int32),
            prompt_len + jnp.arange(CONT_LEN, dtype=jnp.int32),
        ]
    )
    cosine, sine = tables(positions, HEAD)
    queries = rotate(projected[:, :query_cols].reshape(tokens, -1, HEAD), cosine, sine).astype(
        jnp.bfloat16
    )
    keys_own = rotate(
        projected[:, query_cols : query_cols + kv_cols].reshape(tokens, kv_heads, HEAD),
        cosine,
        sine,
    ).astype(jnp.bfloat16)
    values_own = (
        projected[:, query_cols + kv_cols :].reshape(tokens, kv_heads, HEAD).astype(jnp.bfloat16)
    )
    prompt_keys, prompt_values = (
        lax.all_gather(keys_own[:prompt_rows], "row", axis=0, tiled=True),
        lax.all_gather(values_own[:prompt_rows], "row", axis=0, tiled=True),
    )
    keys = jnp.concatenate([prompt_keys, keys_own[prompt_rows:]], axis=0)
    values = jnp.concatenate([prompt_values, values_own[prompt_rows:]], axis=0)
    key_pos = jnp.concatenate(
        [
            jnp.arange(prompt_len, dtype=jnp.int32),
            prompt_len + jnp.arange(CONT_LEN, dtype=jnp.int32),
        ]
    )
    allowed = key_pos[None, :] <= positions[:, None]
    grouped = queries.reshape(tokens, kv_heads, repeat, HEAD)
    scores = attention_scores(grouped, keys, allowed)
    top = jnp.max(scores, axis=-1, keepdims=True)
    logsum = top + jnp.log(jnp.sum(jnp.exp(scores - top), axis=-1, keepdims=True))
    probs = jnp.exp(scores - logsum).astype(jnp.bfloat16)
    mixed = (
        jnp.einsum("grtk,kgd->tgrd", probs, values, preferred_element_type=jnp.float32)
        .reshape(tokens, query_cols)
        .astype(jnp.bfloat16)
    )
    second = residual + collect(jnp.dot(mixed, fetched["out"], preferred_element_type=jnp.float32))
    second_b = second.astype(jnp.bfloat16)
    whole_second = spread(second_b).astype(jnp.float32)
    scale_second = lax.rsqrt(jnp.mean(whole_second * whole_second, axis=1, keepdims=True) + EPS)
    normed_second = (whole_second * scale_second * gain_second).astype(jnp.bfloat16)
    local_experts = fetched["down"].shape[0]
    first_expert = col_rank * local_experts
    match = (
        routes[:, :, None]
        == (first_expert + jnp.arange(local_experts, dtype=jnp.int32))[None, None, :]
    )
    member = jnp.any(match, axis=1)
    weight = jnp.sum(jnp.where(match, weights_in[:, :, None], 0.0), axis=1)
    place = jnp.cumsum(member.astype(jnp.int32), axis=0) - 1
    slot = jnp.where(member, place, CAP)
    index = (
        jnp.zeros((local_experts, CAP + 1), jnp.int32)
        .at[jnp.arange(local_experts, dtype=jnp.int32)[None, :], slot]
        .set(jnp.arange(tokens, dtype=jnp.int32)[:, None])[:, :CAP]
    )
    counts = jnp.sum(member.astype(jnp.int32), axis=0)
    live = jnp.arange(CAP, dtype=jnp.int32)[None, :] < counts[:, None]
    slot_gate = jnp.where(live, jnp.take_along_axis(weight.T, index, axis=1), 0.0)
    chosen = normed_second[index]
    gate_up = jnp.einsum(
        "ecd,edh->ech", chosen, fetched["gate_up"], preferred_element_type=jnp.float32
    )
    gate = gate_up[..., :HIDDEN_SIZE]
    up_part = gate_up[..., HIDDEN_SIZE:]
    activated = (jax.nn.silu(gate) * up_part).astype(jnp.bfloat16)
    expert_out = jnp.einsum(
        "ech,ehd->ecd", activated, fetched["down"], preferred_element_type=jnp.float32
    )
    combined = jax.ops.segment_sum(
        (expert_out * slot_gate[..., None]).reshape(-1, width),
        index.reshape(-1),
        num_segments=tokens,
    )
    result = second + collect(combined)
    keep = {
        "layer_in": layer_in,
        "scale_first": scale_first,
        "normed": normed,
        "cosine": cosine,
        "sine": sine,
        "grouped": grouped,
        "keys": keys,
        "values": values,
        "allowed": allowed,
        "logsum": logsum,
        "mixed": mixed,
        "second_b": second_b,
        "scale_second": scale_second,
        "index": index,
        "slot_gate": slot_gate,
        "chosen": chosen,
        "gate": gate,
        "up_part": up_part,
        "activated": activated,
        "result": result,
    }
    return (result, keep)


def norm_backward(grad_local, value_local, scale, gain_local, width):
    scaled = grad_local * gain_local
    inner = norm_total(jnp.sum(scaled * value_local, axis=1))
    grad_value = scale * scaled - value_local * (scale * scale * scale) * inner[:, None] / width
    grad_gain = jnp.sum(grad_local * value_local * scale, axis=0)
    return (grad_value, grad_gain)


def backward_layer(grad_result, keep, fetched, gain_first, gain_second, col_rank):
    tokens, shard = grad_result.shape
    width = fetched["qkv"].shape[0]
    index = keep["index"]
    grad_whole = spread_grad(grad_result.astype(jnp.bfloat16))
    grad_expert = (grad_whole[index].astype(jnp.float32) * keep["slot_gate"][..., None]).astype(
        jnp.bfloat16
    )
    grad_act = jnp.einsum(
        "ecd,ehd->ech", grad_expert, fetched["down"], preferred_element_type=jnp.float32
    )
    grad_down = jnp.einsum(
        "ech,ecd->ehd", keep["activated"], grad_expert, preferred_element_type=jnp.float32
    )
    gate = keep["gate"]
    sigmoid = jax.nn.sigmoid(gate)
    grad_gate = grad_act * keep["up_part"] * sigmoid * (1.0 + gate * (1.0 - sigmoid))
    grad_up = grad_act * gate * sigmoid
    grad_gate_up = jnp.concatenate([grad_gate, grad_up], axis=2).astype(jnp.bfloat16)
    grad_chosen = jnp.einsum(
        "ech,edh->ecd", grad_gate_up, fetched["gate_up"], preferred_element_type=jnp.float32
    )
    grad_gate_up_weight = jnp.einsum(
        "ecd,ech->edh", keep["chosen"], grad_gate_up, preferred_element_type=jnp.float32
    )
    grad_normed_second = collect_grad(
        jax.ops.segment_sum(grad_chosen.reshape(-1, width), index.reshape(-1), num_segments=tokens)
    )
    second_local = keep["second_b"].astype(jnp.float32)
    gain_second_local = lax.dynamic_slice_in_dim(gain_second, col_rank * shard, shard)
    grad_norm_second, grad_gain_second = norm_backward(
        grad_normed_second, second_local, keep["scale_second"], gain_second_local, width
    )
    grad_second = grad_result + grad_norm_second
    grad_branch = spread_grad(grad_second.astype(jnp.bfloat16))
    grad_mixed = contract_last(grad_branch, fetched["out"])
    grad_out_weight = contract_first(keep["mixed"], grad_branch)
    grouped = keep["grouped"]
    keys = keep["keys"]
    values = keep["values"]
    grad_mixed_b = grad_mixed.astype(jnp.bfloat16).reshape(grouped.shape)
    scores = attention_scores(grouped, keys, keep["allowed"])
    probs = jnp.exp(scores - keep["logsum"])
    probs_b = probs.astype(jnp.bfloat16)
    grad_probs = jnp.einsum(
        "tgrd,kgd->grtk", grad_mixed_b, values, preferred_element_type=jnp.float32
    )
    delta = jnp.sum(probs * grad_probs, axis=-1, keepdims=True)
    grad_scores = (probs * (grad_probs - delta)).astype(jnp.bfloat16)
    factor = HEAD ** (-0.5)
    grad_queries = (
        jnp.einsum("grtk,kgd->tgrd", grad_scores, keys, preferred_element_type=jnp.float32) * factor
    )
    grad_keys = (
        jnp.einsum("grtk,tgrd->kgd", grad_scores, grouped, preferred_element_type=jnp.float32)
        * factor
    )
    grad_values = jnp.einsum(
        "grtk,tgrd->kgd", probs_b, grad_mixed_b, preferred_element_type=jnp.float32
    )
    prompt_len = keys.shape[0] - CONT_LEN
    prompt_key_grad, prompt_value_grad = (
        lax.psum_scatter(grad_keys[:prompt_len], "row", scatter_dimension=0, tiled=True),
        lax.psum_scatter(grad_values[:prompt_len], "row", scatter_dimension=0, tiled=True),
    )
    grad_keys_own = jnp.concatenate([prompt_key_grad, grad_keys[prompt_len:]], axis=0)
    grad_values_own = jnp.concatenate([prompt_value_grad, grad_values[prompt_len:]], axis=0)
    cosine = keep["cosine"]
    sine = keep["sine"]
    grad_query_raw = rotate(grad_queries.reshape(tokens, -1, HEAD), cosine, -sine)
    grad_key_raw = rotate(grad_keys_own, cosine, -sine)
    grad_projected = jnp.concatenate(
        [
            grad_query_raw.reshape(tokens, -1),
            grad_key_raw.reshape(tokens, -1),
            grad_values_own.reshape(tokens, -1),
        ],
        axis=1,
    ).astype(jnp.bfloat16)
    grad_normed = collect_grad(contract_last(grad_projected, fetched["qkv"]))
    grad_qkv_weight = contract_first(keep["normed"], grad_projected)
    input_local = keep["layer_in"].astype(jnp.float32)
    gain_first_local = lax.dynamic_slice_in_dim(gain_first, col_rank * shard, shard)
    grad_norm_first, grad_gain_first = norm_backward(
        grad_normed, input_local, keep["scale_first"], gain_first_local, width
    )
    grad_input = grad_second + grad_norm_first
    return (
        grad_input,
        {
            "qkv": grad_qkv_weight,
            "out": grad_out_weight,
            "gate_up": grad_gate_up_weight,
            "down": grad_down,
            "gain_first": grad_gain_first,
            "gain_second": grad_gain_second,
        },
    )


def on_device(
    x_in,
    targets,
    w_query,
    w_key,
    w_value,
    w_out,
    w_gate,
    w_up,
    w_down,
    gain_attn,
    gain_ffn,
    expert_ids,
    gates,
    lengths,
):
    section_rank = lax.axis_index("section")
    row_rank = lax.axis_index("row")
    col_rank = lax.axis_index("col")
    micro = x_in.shape[0]
    tokens = x_in.shape[2]
    shard = x_in.shape[3]
    prompt_rows = tokens - CONT_LEN
    prompt_len = prompt_rows * lax.axis_size("row")
    first_section = section_rank == 0
    gain_first = gain_attn[0].astype(jnp.float32)
    gain_second = gain_ffn[0].astype(jnp.float32)
    count = (micro * prompt_len + jnp.sum(lengths)).astype(jnp.float32)
    received = jnp.zeros((tokens, shard), jnp.bfloat16)
    kept = []
    for step in range(micro + 1):
        batch = jnp.clip(step - section_rank, 0, micro - 1)
        own_input = x_in[min(step, micro - 1), 0]
        layer_in = jnp.where(first_section, own_input, received)
        routes = lax.dynamic_index_in_dim(expert_ids[0], batch, 0, keepdims=False)[0]
        weights_in = lax.dynamic_index_in_dim(gates[0], batch, 0, keepdims=False)[0]
        fetched = fetch(w_query, w_key, w_value, w_out, w_gate, w_up, w_down)
        result, keep = forward_layer(
            layer_in, fetched, gain_first, gain_second, routes, weights_in, row_rank, col_rank
        )
        kept.append(keep)
        if step < micro:
            received = from_behind(result.astype(jnp.bfloat16), "section", 1)
    outputs = jnp.stack(
        [
            jnp.where(first_section, kept[index_m]["result"], kept[index_m + 1]["result"])
            for index_m in range(micro)
        ]
    )
    grad_received = jnp.zeros((tokens, shard), jnp.bfloat16)
    loss_part = jnp.zeros((), jnp.float32)
    totals = None
    input_list = []
    for step in range(micro + 1):
        picked = jax.tree.map(
            lambda early, later: jnp.where(first_section, early, later),
            kept[max(step - 1, 0)],
            kept[min(step + 1, micro)],
        )
        final_batch = min(step, micro - 1)
        final = kept[min(step + 1, micro)]["result"]
        goal = targets[final_batch, 0].astype(jnp.float32)
        length = lax.dynamic_index_in_dim(lengths[final_batch], row_rank, 0, keepdims=False)
        valid = (jnp.arange(tokens, dtype=jnp.int32) - prompt_rows < length).astype(jnp.float32)[
            :, None
        ]
        active = 1.0 if step < micro else 0.0
        diff = final - goal
        loss_part = loss_part + jnp.where(
            first_section, 0.0, active * jnp.sum(valid * diff * diff) / count
        )
        grad_loss = 2.0 * active / count * valid * diff
        grad_here = jnp.where(first_section, grad_received.astype(jnp.float32), grad_loss)
        fetched = fetch(w_query, w_key, w_value, w_out, w_gate, w_up, w_down)
        grad_input, layer_grads = backward_layer(
            grad_here, picked, fetched, gain_first, gain_second, col_rank
        )
        totals = (
            layer_grads
            if totals is None
            else jax.tree.map(lambda left, right: left + right, totals, layer_grads)
        )
        grad_b = grad_input.astype(jnp.bfloat16)
        input_list.append(grad_b)
        if step < micro:
            grad_received = from_behind(grad_b, "section", -1)
    input_grads = jnp.stack(
        [
            jnp.where(first_section, input_list[index_m + 1], input_list[index_m])
            for index_m in range(micro)
        ]
    )
    query_cols = w_query.shape[2]
    key_cols = w_key.shape[2]
    qkv_total = totals["qkv"]
    gate_up_total = totals["gate_up"]
    grad_query, grad_key, grad_value, grad_out, grad_gate, grad_up, grad_down = (
        lax.psum_scatter(qkv_total[:, :query_cols], "row", scatter_dimension=0, tiled=True),
        lax.psum_scatter(
            qkv_total[:, query_cols : query_cols + key_cols], "row", scatter_dimension=0, tiled=True
        ),
        lax.psum_scatter(
            qkv_total[:, query_cols + key_cols :], "row", scatter_dimension=0, tiled=True
        ),
        lax.psum_scatter(totals["out"], "row", scatter_dimension=1, tiled=True),
        lax.psum_scatter(gate_up_total[..., :HIDDEN_SIZE], "row", scatter_dimension=1, tiled=True),
        lax.psum_scatter(gate_up_total[..., HIDDEN_SIZE:], "row", scatter_dimension=1, tiled=True),
        lax.psum_scatter(totals["down"], "row", scatter_dimension=2, tiled=True),
    )
    gain_grad_first, gain_grad_second = lax.psum(
        (totals["gain_first"], totals["gain_second"]), "row"
    )
    loss = lax.psum(loss_part, ("section", "row", "col"))
    return (
        outputs.astype(jnp.bfloat16)[None, :, None],
        loss,
        input_grads[None, :, None],
        grad_query[None],
        grad_key[None],
        grad_value[None],
        grad_out[None],
        grad_gate[None],
        grad_up[None],
        grad_down[None],
        gain_grad_first[None],
        gain_grad_second[None],
    )


def solution(mesh):
    in_specs = (
        P(None, "row", None, "col"),
        P(None, "row", None, "col"),
        P("section", "row", "col"),
        P("section", "row", "col"),
        P("section", "row", "col"),
        P("section", "col", "row"),
        P("section", "col", "row", None),
        P("section", "col", "row", None),
        P("section", "col", None, "row"),
        P("section", None),
        P("section", None),
        P("section", None, "row", None, None),
        P("section", None, "row", None, None),
        P(),
    )
    out_specs = (
        P("section", None, "row", None, "col"),
        P(),
        P("section", None, "row", None, "col"),
        P("section", "row", "col"),
        P("section", "row", "col"),
        P("section", "row", "col"),
        P("section", "col", "row"),
        P("section", "col", "row", None),
        P("section", "col", "row", None),
        P("section", "col", None, "row"),
        P("section", "col"),
        P("section", "col"),
    )
    return jax.shard_map(
        on_device, mesh=mesh, in_specs=in_specs, out_specs=out_specs, check_vma=False
    )
```

profile of v0, /device:TPU:0, one launch (start us, length us, event | category | flops | bytes accessed | tf_op | source)
XLA Modules:
  0.0 3014.6 jit_solution(6019308065669862335)
XLA Ops:
  129.9 28.5 reduce-scatter.26.cloned.1.call-done
  169.9 23.0 scatter_custom_fusion.8
  193.4 23.0 scatter_custom_fusion.7
  216.9 23.0 scatter_custom_fusion.6
  240.3 20.8 gather_fusion.8
  261.4 20.8 gather_fusion.7
  283.7 20.8 gather_fusion.6
  331.6 149.3 %all-gather.48.cloned.1.call-done = bf16[1,8,1024,512]{3,2,1,0:T(8,128)(2,1)} async-done(((bf16[1,8,256,512]{3,2,1,0:T(8,128)(2,1)}), bf16[1,8,1024,512]{3,2,1,0:T(8,128)(2,1)}) %all-gather.48.cloned.1.call-update) | async-done | bytes 8388624 | tf_op jit(solution)/shard_map/all_gather | solution.py:78
  502.3 129.0 %all-gather.52.cloned.1.call-done = bf16[1,8,512,1024]{3,2,1,0:T(8,128)(2,1)} async-done(((bf16[1,8,512,256]{3,2,1,0:T(8,128)(2,1)}), bf16[1,8,512,1024]{3,2,1,0:T(8,128)(2,1)}) %all-gather.52.cloned.1.call-update) | async-done | bytes 8388624 | tf_op jit(solution)/shard_map/all_gather | solution.py:80
  643.7 29.6 scatter_custom_fusion
  676.7 24.9 reduce-scatter.28.cloned.1.call-done
  715.4 21.0 all-gather.26.cloned.1.call-done
  792.1 28.2 reduce-scatter.30.cloned.1.call-done
  890.7 29.6 scatter_custom_fusion.1
  928.1 23.9 reduce-scatter.32.cloned.1.call-done
  1027.6 29.5 scatter_custom_fusion.3
  1057.2 38.0 %reduce-scatter.38.cloned.1.call-done = f32[768,256]{1,0:T(8,128)} async-done(((f32[768,1024]{1,0:T(8,128)}), f32[768,256]{1,0:T(8,128)}) %reduce-scatter.38.cloned.1.call-update) | async-done | bytes 786448 | tf_op jit(solution)/shard_map/reduce_scatter | solution.py:53
  1176.8 22.0 fusion.10
  1198.8 22.6 fusion.12
  1300.8 21.1 reduce-scatter.40.cloned.1.call-done
  1390.9 29.6 scatter_custom_fusion.2
  1526.4 29.6 scatter_custom_fusion.4
  1556.1 38.1 %reduce-scatter.46.cloned.1.call-done = f32[768,256]{1,0:T(8,128)} async-done(((f32[768,1024]{1,0:T(8,128)}), f32[768,256]{1,0:T(8,128)}) %reduce-scatter.46.cloned.1.call-update) | async-done | bytes 786448 | tf_op jit(solution)/shard_map/reduce_scatter | solution.py:53
  1702.5 36.4 %reduce-scatter.52.cloned.1.call-done = f32[768,256]{1,0:T(8,128)} async-done(((f32[768,1024]{1,0:T(8,128)}), f32[768,256]{1,0:T(8,128)}) %reduce-scatter.52.cloned.1.call-update) | async-done | bytes 786448 | tf_op jit(solution)/shard_map/reduce_scatter | solution.py:53
  1835.8 29.7 scatter_custom_fusion.5
  1866.2 37.4 %reduce-scatter.54.cloned.1.call-done = f32[768,256]{1,0:T(8,128)} async-done(((f32[768,1024]{1,0:T(8,128)}), f32[768,256]{1,0:T(8,128)}) %reduce-scatter.54.cloned.1.call-update) | async-done | bytes 786448 | tf_op jit(solution)/shard_map/reduce_scatter | solution.py:53
  2091.4 38.1 %add_add_fusion = f32[8,1024,1024]{2,1,0:T(8,128)} fusion(f32[8,1024,1024]{2,1,0:T(8,128)} %fusion.54, f32[8,1024,1024]{2,1,0:T(8,128)} %fusion.52, bf16[8,384,1024]{1,2,0:T(8,128)(2,1)} %copy.174, bf16[8,384,1024]{1,2,0:T(8,128)(2,1)} %copy.176, pred[]{:T(512)S(6)} %eq.44, bf16[8,384,512]{2,1,0:T(8,128)(2,1)} %get-tuple-element.137, ...), kind=kOutput, calls=%fused_computation.18 | convolution fusion | flops 6474956800 | bytes 119537664 | tf_op jit(solution)/shard_map/ecd,ech->edh/dot_general | solution.py:248
  2130.7 21.9 fusion.345
  2209.9 41.5 %psum.63 = f32[]{:T(128)} all-reduce(f32[]{:T(128)S(6)} %add.543), channel_id=1, replica_groups=mesh['section'=2,'row'=4,'col'=4] {'section','row','col'}, use_global_device_ids=true, to_apply=%region_42.44 | all-reduce | flops 1 | bytes 8 | tf_op jit(solution)/shard_map/psum | solution.py:438
  2277.1 162.5 %reduce-scatter.70.cloned.1.call-done = f32[8,256,512]{2,1,0:T(8,128)} async-done(((f32[8,1024,512]{2,1,0:T(8,128)}), f32[8,256,512]{2,1,0:T(8,128)}) %reduce-scatter.70.cloned.1.call-update) | async-done | bytes 4194320 | tf_op jit(solution)/shard_map/reduce_scatter | solution.py:431
  2439.6 284.0 %reduce-scatter.72.cloned.1.call-done = f32[8,256,512]{2,1,0:T(8,128)} async-done(((f32[8,1024,512]{2,1,0:T(8,128)}), f32[8,256,512]{2,1,0:T(8,128)}) %reduce-scatter.72.cloned.1.call-update) | async-done | bytes 4194320 | tf_op jit(solution)/shard_map/reduce_scatter | solution.py:432
  2723.6 284.0 %reduce-scatter.74.cloned.1.call-done = f32[8,512,256]{2,1,0:T(8,128)} async-done(((f32[8,512,1024]{2,1,0:T(8,128)}), f32[8,512,256]{2,1,0:T(8,128)}) %reduce-scatter.74.cloned.1.call-update) | async-done | bytes 4194320 | tf_op jit(solution)/shard_map/reduce_scatter | solution.py:433
  (813 shorter events, 1232.2 us)
Async XLA Ops:
  7.2 67.4 %all-gather.46.cloned.1.call-start = ((), (), s32[]{:S(2)}) async-start(), calls=%async_computation.61 | async-start | bytes 1966080 | tf_op jit(solution)/shard_map/all_gather | solution.py:39
  9.0 149.4 %reduce-scatter.26.cloned.1.call-start = ((), (), s32[]{:S(2)}) async-start(), calls=%async_computation.25 | async-start | bytes 1966080 | tf_op jit(solution)/shard_map/reduce_scatter | solution.py:43
  129.5 177.6 %all-gather.24.cloned.1.call-start = ((), (), s32[]{:S(2)}) async-start(), calls=%async_computation.26 | async-start | bytes 1966080 | tf_op jit(solution)/shard_map/all_gather | solution.py:39
  160.3 171.2 %all-gather.50.cloned.1.call-start = ((), (), s32[]{:S(2)}) async-start(), calls=%async_computation.63 | async-start | bytes 10485760 | tf_op jit(solution)/shard_map/all_gather | solution.py:79
  160.9 320.0 %all-gather.48.cloned.1.call-start = ((), (), s32[]{:S(2)}) async-start(), calls=%async_computation.62 | async-start | bytes 10485760 | tf_op jit(solution)/shard_map/all_gather | solution.py:78
  161.5 469.8 %all-gather.52.cloned.1.call-start = ((), (), s32[]{:S(2)}) async-start(), calls=%async_computation.64 | async-start | bytes 10485760 | tf_op jit(solution)/shard_map/all_gather | solution.py:80
  162.1 539.5 %reduce-scatter.28.cloned.1.call-start = ((), (), s32[]{:S(2)}) async-start(), calls=%async_computation.27 | async-start | bytes 1966080 | tf_op jit(solution)/shard_map/reduce_scatter | solution.py:43
  715.3 105.0 %reduce-scatter.30.cloned.1.call-start = ((), (), s32[]{:S(2)}) async-start(), calls=%async_computation.29 | async-start | bytes 1966080 | tf_op jit(solution)/shard_map/reduce_scatter | solution.py:43
  822.3 129.7 %reduce-scatter.32.cloned.1.call-start = ((), (), s32[]{:S(2)}) async-start(), calls=%async_computation.31 | async-start | bytes 1966080 | tf_op jit(solution)/shard_map/reduce_scatter | solution.py:43
  955.5 139.7 %reduce-scatter.38.cloned.1.call-start = ((), (), s32[]{:S(2)}) async-start(), calls=%async_computation.37 | async-start | bytes 3932160 | tf_op jit(solution)/shard_map/reduce_scatter | solution.py:53
  1057.1 73.2 %all-gather.36.cloned.1.call-start = ((), (), s32[]{:S(2)}) async-start(), calls=%async_computation.38 | async-start | bytes 1966080 | tf_op jit(solution)/shard_map/all_gather | solution.py:49
  1119.8 156.3 %reduce-scatter.34.cloned.1.call-start = ((), (), s32[]{:S(2)}) async-start(), calls=%async_computation.33 | async-start | bytes 1966080 | tf_op jit(solution)/shard_map/reduce_scatter | solution.py:43
  1258.1 63.8 %reduce-scatter.40.cloned.1.call-start = ((), (), s32[]{:S(2)}) async-start(), calls=%async_computation.39 | async-start | bytes 655360 | tf_op jit(solution)/shard_map/reduce_scatter | solution.py:288
  1266.8 74.9 %all-gather.32.cloned.1.call-start = ((), (), s32[]{:S(2)}) async-start(), calls=%async_computation.34 | async-start | bytes 1966080 | tf_op jit(solution)/shard_map/all_gather | solution.py:39
  1277.9 146.0 %reduce-scatter.44.cloned.1.call-start = ((), (), s32[]{:S(2)}) async-start(), calls=%async_computation.41 | async-start | bytes 3932160 | tf_op jit(solution)/shard_map/reduce_scatter | solution.py:53
  1326.9 125.3 %reduce-scatter.36.cloned.1.call-start = ((), (), s32[]{:S(2)}) async-start(), calls=%async_computation.35 | async-start | bytes 1966080 | tf_op jit(solution)/shard_map/reduce_scatter | solution.py:43
  1454.6 139.6 %reduce-scatter.46.cloned.1.call-start = ((), (), s32[]{:S(2)}) async-start(), calls=%async_computation.43 | async-start | bytes 3932160 | tf_op jit(solution)/shard_map/reduce_scatter | solution.py:53
  1556.0 70.9 %all-gather.40.cloned.1.call-start = ((), (), s32[]{:S(2)}) async-start(), calls=%async_computation.44 | async-start | bytes 1966080 | tf_op jit(solution)/shard_map/all_gather | solution.py:49
  1605.9 75.5 %reduce-scatter.50.cloned.1.call-start = ((), (), s32[]{:S(2)}) async-start(), calls=%async_computation.46 | async-start | bytes 655360 | tf_op jit(solution)/shard_map/reduce_scatter | solution.py:289
  1674.4 64.5 %reduce-scatter.52.cloned.1.call-start = ((), (), s32[]{:S(2)}) async-start(), calls=%async_computation.47 | async-start | bytes 3932160 | tf_op jit(solution)/shard_map/reduce_scatter | solution.py:53
  1702.5 81.6 %all-gather.42.cloned.1.call-start = ((), (), s32[]{:S(2)}) async-start(), calls=%async_computation.48 | async-start | bytes 1966080 | tf_op jit(solution)/shard_map/all_gather | solution.py:49
  1764.9 138.7 %reduce-scatter.54.cloned.1.call-start = ((), (), s32[]{:S(2)}) async-start(), calls=%async_computation.49 | async-start | bytes 3932160 | tf_op jit(solution)/shard_map/reduce_scatter | solution.py:53
  1865.5 71.1 %all-gather.44.cloned.1.call-start = ((), (), s32[]{:S(2)}) async-start(), calls=%async_computation.50 | async-start | bytes 1966080 | tf_op jit(solution)/shard_map/all_gather | solution.py:49
  1915.5 73.8 %reduce-scatter.58.cloned.1.call-start = ((), (), s32[]{:S(2)}) async-start(), calls=%async_computation.52 | async-start | bytes 655360 | tf_op jit(solution)/shard_map/reduce_scatter | solution.py:289
  1983.5 268.6 %reduce-scatter.60.cloned.1.call-start = ((), (), s32[]{:S(2)}) async-start(), calls=%async_computation.53 | async-start | bytes 3932160 | tf_op jit(solution)/shard_map/reduce_scatter | solution.py:53
  2011.2 265.9 %reduce-scatter.64.cloned.1.call-start = ((), (), s32[]{:S(2)}) async-start(), calls=%async_computation.55 | async-start | bytes 655360 | tf_op jit(solution)/shard_map/reduce_scatter | solution.py:424
  2038.4 238.7 %reduce-scatter.66.cloned.1.call-start = ((), (), s32[]{:S(2)}) async-start(), calls=%async_computation.56 | async-start | bytes 655360 | tf_op jit(solution)/shard_map/reduce_scatter | solution.py:427
  2067.7 209.4 %reduce-scatter.68.cloned.1.call-start = ((), (), s32[]{:S(2)}) async-start(), calls=%async_computation.57 | async-start | bytes 1310720 | tf_op jit(solution)/shard_map/reduce_scatter | solution.py:430
  2091.4 185.7 %reduce-scatter.62.cloned.1.call-start = ((), (), s32[]{:S(2)}) async-start(), calls=%async_computation.54 | async-start | bytes 1310720 | tf_op jit(solution)/shard_map/reduce_scatter | solution.py:423
  2130.6 309.0 %reduce-scatter.70.cloned.1.call-start = ((), (), s32[]{:S(2)}) async-start(), calls=%async_computation.58 | async-start | bytes 20971520 | tf_op jit(solution)/shard_map/reduce_scatter | solution.py:431
  2152.6 571.0 %reduce-scatter.72.cloned.1.call-start = ((), (), s32[]{:S(2)}) async-start(), calls=%async_computation.59 | async-start | bytes 20971520 | tf_op jit(solution)/shard_map/reduce_scatter | solution.py:432
  2153.1 854.4 %reduce-scatter.74.cloned.1.call-start = ((), (), s32[]{:S(2)}) async-start(), calls=%async_computation.60 | async-start | bytes 20971520 | tf_op jit(solution)/shard_map/reduce_scatter | solution.py:433
  (218 other events, 10216.1 us)
Sparse Core Ops, SparseCore 0:
  10.1 22.5 all-gather.45
  129.6 28.7 reduce-scatter.25
  181.8 149.7 all-gather.49
  333.1 147.8 all-gather.47
  482.4 148.8 all-gather.51
  676.7 24.8 reduce-scatter.27
  715.4 20.8 all-gather.25
  792.2 28.1 reduce-scatter.29
  923.7 28.1 reduce-scatter.31
  1057.2 37.9 reduce-scatter.37
  1106.9 20.9 all-gather.35
  1247.8 28.2 reduce-scatter.33
  1278.2 21.6 reduce-scatter.41
  1302.0 19.9 reduce-scatter.39
  1344.0 37.9 reduce-scatter.43
  1423.9 28.1 reduce-scatter.35
  1556.2 37.9 reduce-scatter.45
  1606.0 20.9 all-gather.39
  1652.7 21.6 reduce-scatter.49
  1676.6 19.8 reduce-scatter.47
  1702.6 36.2 reduce-scatter.51
  1865.6 37.9 reduce-scatter.53
  1915.6 21.0 all-gather.43
  1962.3 21.6 reduce-scatter.57
  2011.3 36.1 reduce-scatter.59
  2050.4 21.6 reduce-scatter.63
  2074.9 19.9 reduce-scatter.65
  2097.6 25.4 reduce-scatter.67
  2130.7 25.6 reduce-scatter.61
  2159.4 280.1 reduce-scatter.69
  2442.5 281.0 reduce-scatter.71
  2726.5 281.0 reduce-scatter.73
  (8 shorter events, 155.7 us)
where the time goes:
time: 3030 us; the launch traced here: 3010 us
  waiting for transfers between devices  1540 us (51%)
  matrix products  527 us (17%)
  other arithmetic  364 us (12%)
  local copies, waits for them, and re-layouts  313 us (10%)
  blocking collectives  239 us (8%)
    reduce_scatter x1, waiting for transfers between devices, on_device(): lax.psum_scatter(totals['down'], 'row', scatter_dimension=2, tiled=True)  284 us
    reduce_scatter x1, waiting for transfers between devices, on_device(): lax.psum_scatter(gate_up_total[..., HIDDEN_SIZE:], 'row', scatter_dimensi...  284 us
    reduce_scatter x1, waiting for transfers between devices, on_device(): lax.psum_scatter(gate_up_total[..., :HIDDEN_SIZE], 'row', scatter_dimensi...  162 us
    reduce_scatter x6, waiting for transfers between devices, collect_grad(): return lax.psum_scatter(value, 'col', scatter_dimension=1, tiled=True)  150 us
    all_gather x1, waiting for transfers between devices, fetch(): lax.all_gather(w_gate[0], 'row', axis=1, tiled=True)  149 us
    all_gather x1, waiting for transfers between devices, fetch(): lax.all_gather(w_down[0], 'row', axis=2, tiled=True)  129 us
    reduce_scatter x6, waiting for transfers between devices, collect(): lax.psum_scatter(value.astype(jnp.bfloat16), 'col', scatter_dimension=1,...  120 us
    scatter-add x3, other arithmetic, backward_layer(): jax.ops.segment_sum(grad_chosen.reshape(-1, width), index.reshape(-1), nu...  88.8 us
  transfers between devices with their start and end apart: 44, of which 33 were waited for; matrix products, arithmetic and copies ran while one was open for 20% of the time, Pallas kernels for 0%

commit v1 on v0

--- a/solution.py
+++ b/solution.py
@@ -164,7 +164,14 @@
     )
     member = jnp.any(match, axis=1)
     weight = jnp.sum(jnp.where(match, weights_in[:, :, None], 0.0), axis=1)
-    place = jnp.cumsum(member.astype(jnp.int32), axis=0) - 1
+    order = jnp.arange(tokens, dtype=jnp.int32)
+    earlier = (order[:, None] >= order[None, :]).astype(jnp.bfloat16)
+    place = (
+        jnp.dot(earlier, member.astype(jnp.bfloat16), preferred_element_type=jnp.float32).astype(
+            jnp.int32
+        )
+        - 1
+    )
     slot = jnp.where(member, place, CAP)
     index = (
         jnp.zeros((local_experts, CAP + 1), jnp.int32)
@@ -428,9 +435,9 @@
             qkv_total[:, query_cols + key_cols :], "row", scatter_dimension=0, tiled=True
         ),
         lax.psum_scatter(totals["out"], "row", scatter_dimension=1, tiled=True),
-        lax.psum_scatter(gate_up_total[..., :HIDDEN_SIZE], "row", scatter_dimension=1, tiled=True),
-        lax.psum_scatter(gate_up_total[..., HIDDEN_SIZE:], "row", scatter_dimension=1, tiled=True),
-        lax.psum_scatter(totals["down"], "row", scatter_dimension=2, tiled=True),
+        lax.psum_scatter(gate_up_total[..., :HIDDEN_SIZE].astype(jnp.bfloat16), "row", scatter_dimension=1, tiled=True),
+        lax.psum_scatter(gate_up_total[..., HIDDEN_SIZE:].astype(jnp.bfloat16), "row", scatter_dimension=1, tiled=True),
+        lax.psum_scatter(totals["down"].astype(jnp.bfloat16), "row", scatter_dimension=2, tiled=True),
     )
     gain_grad_first, gain_grad_second = lax.psum(
         (totals["gain_first"], totals["gain_second"]), "row"
@@ -444,9 +451,9 @@
         grad_key[None],
         grad_value[None],
         grad_out[None],
-        grad_gate[None],
-        grad_up[None],
-        grad_down[None],
+        grad_gate.astype(jnp.float32)[None],
+        grad_up.astype(jnp.float32)[None],
+        grad_down.astype(jnp.float32)[None],
         gain_grad_first[None],
         gain_grad_second[None],
     )

time: 3030 us -> 2670 us (0.88)
  waiting for transfers between devices: 1540 us -> 1180 us
    reduce_scatter x3, waiting for transfers between devices: 730 us -> 285 us  [the longest x1 143 us: on_device(): lax.psum_scatter(totals['down'].astype(jnp.bfloat16), 'row', scatter_dime...]
    unnamed x417 -> x423, local copies, waits for them, and re-layouts: 86.1 us -> 86.4 us
  transfers between devices with their start and end apart: 44 -> 44, of which waited for: 33 -> 35; matrix products, arithmetic and copies ran while one was open for 20% -> 22% of each run, Pallas kernels for 0% -> 0%
where the time goes in v1:
time: 2670 us; the launch traced here: 2660 us
  waiting for transfers between devices  1180 us (44%)
  matrix products  518 us (19%)
  other arithmetic  370 us (14%)
  local copies, waits for them, and re-layouts  303 us (11%)
  blocking collectives  242 us (9%)
    reduce_scatter x6, waiting for transfers between devices, collect_grad(): return lax.psum_scatter(value, 'col', scatter_dimension=1, tiled=True)  150 us
    all_gather x1, waiting for transfers between devices, fetch(): lax.all_gather(w_gate[0], 'row', axis=1, tiled=True)  149 us
    reduce_scatter x1, waiting for transfers between devices, on_device(): lax.psum_scatter(totals['down'].astype(jnp.bfloat16), 'row', scatter_dime...  143 us
    reduce_scatter x1, waiting for transfers between devices, on_device(): lax.psum_scatter(gate_up_total[..., HIDDEN_SIZE:].astype(jnp.bfloat16), '...  142 us
    all_gather x1, waiting for transfers between devices, fetch(): lax.all_gather(w_down[0], 'row', axis=2, tiled=True)  129 us
    reduce_scatter x6, waiting for transfers between devices, collect(): lax.psum_scatter(value.astype(jnp.bfloat16), 'col', scatter_dimension=1,...  109 us
    scatter-add x3, other arithmetic, forward_layer(): jax.ops.segment_sum((expert_out * slot_gate[..., None]).reshape(-1, width...  89 us
    scatter-add x3, other arithmetic, backward_layer(): jax.ops.segment_sum(grad_chosen.reshape(-1, width), index.reshape(-1), nu...  88.7 us
  transfers between devices with their start and end apart: 44, of which 35 were waited for; matrix products, arithmetic and copies ran while one was open for 22% of the time, Pallas kernels for 0%

profile of v1, /device:TPU:0, one launch (start us, length us, event | category | flops | bytes accessed | tf_op | source)
XLA Modules:
  0.0 2657.6 jit_solution(11066486425428305940)
XLA Ops:
  164.1 23.0 scatter_custom_fusion.8
  187.5 23.0 scatter_custom_fusion.7
  211.0 23.0 scatter_custom_fusion.6
  234.5 20.8 gather_fusion.8
  277.8 20.8 gather_fusion.6
  331.4 149.4 %all-gather.48.cloned.1.call-done = bf16[1,8,1024,512]{3,2,1,0:T(8,128)(2,1)} async-done(((bf16[1,8,256,512]{3,2,1,0:T(8,128)(2,1)}), bf16[1,8,1024,512]{3,2,1,0:T(8,128)(2,1)}) %all-gather.48.cloned.1.call-update) | async-done | bytes 8388624 | tf_op jit(solution)/shard_map/all_gather | solution.py:78
  502.2 129.0 %all-gather.52.cloned.1.call-done = bf16[1,8,512,1024]{3,2,1,0:T(8,128)(2,1)} async-done(((bf16[1,8,512,256]{3,2,1,0:T(8,128)(2,1)}), bf16[1,8,512,1024]{3,2,1,0:T(8,128)(2,1)}) %all-gather.52.cloned.1.call-update) | async-done | bytes 8388624 | tf_op jit(solution)/shard_map/all_gather | solution.py:80
  643.5 29.9 %scatter_custom_fusion = f32[768,1024]{1,0:T(8,128)} fusion(s32[3072]{0:T(1024)} %reshape.709, f32[3072,1024]{1,0:T(8,128)} %bitcast.479, f32[]{:T(128)} %constant.121.clone.1), kind=kCustom, calls=%fused_computation.199 | custom fusion | flops 3145728 | bytes 3146240 | tf_op jit(solution)/shard_map/scatter-add | solution.py:194
  676.7 24.9 reduce-scatter.28.cloned.1.call-done
  715.4 21.0 all-gather.26.cloned.1.call-done
  792.2 28.3 %reduce-scatter.30.cloned.1.call-done = bf16[768,256]{1,0:T(8,128)(2,1)} async-done(((bf16[768,1024]{1,0:T(8,128)(2,1)}), bf16[768,256]{1,0:T(8,128)(2,1)}) %reduce-scatter.30.cloned.1.call-update) | async-done | bytes 393232 | tf_op jit(solution)/shard_map/reduce_scatter | solution.py:43
  890.9 29.6 %scatter_custom_fusion.1 = f32[768,1024]{1,0:T(8,128)} fusion(s32[3072]{0:T(1024)} %reshape.717, f32[3072,1024]{1,0:T(8,128)} %bitcast.480, f32[]{:T(128)} %constant.121.clone.1), kind=kCustom, calls=%fused_computation.197 | custom fusion | flops 3145728 | bytes 3146240 | tf_op jit(solution)/shard_map/scatter-add | solution.py:194
  928.2 23.9 reduce-scatter.32.cloned.1.call-done
  1027.5 29.5 %scatter_custom_fusion.3 = f32[768,1024]{1,0:T(8,128)} fusion(s32[3072]{0:T(1024)S(1)} %reshape.733, f32[3072,1024]{1,0:T(8,128)} %bitcast.604, f32[]{:T(128)} %constant.121.clone.1), kind=kCustom, calls=%fused_computation.193 | custom fusion | flops 3145728 | bytes 3146240 | tf_op jit(solution)/shard_map/scatter-add | solution.py:259
  1057.1 38.0 %reduce-scatter.38.cloned.1.call-done = f32[768,256]{1,0:T(8,128)} async-done(((f32[768,1024]{1,0:T(8,128)}), f32[768,256]{1,0:T(8,128)}) %reduce-scatter.38.cloned.1.call-update) | async-done | bytes 786448 | tf_op jit(solution)/shard_map/reduce_scatter | solution.py:53
  1176.6 22.0 fusion.10
  1198.6 22.6 fusion.12
  1300.6 21.0 reduce-scatter.40.cloned.1.call-done
  1390.6 29.5 %scatter_custom_fusion.2 = f32[768,1024]{1,0:T(8,128)} fusion(s32[3072]{0:T(1024)S(1)} %reshape.725, f32[3072,1024]{1,0:T(8,128)} %bitcast.478, f32[]{:T(128)} %constant.121.clone.1), kind=kCustom, calls=%fused_computation.195 | custom fusion | flops 3145728 | bytes 3146240 | tf_op jit(solution)/shard_map/scatter-add | solution.py:194
  1525.9 29.6 %scatter_custom_fusion.4 = f32[768,1024]{1,0:T(8,128)} fusion(s32[3072]{0:T(1024)S(1)} %reshape.741, f32[3072,1024]{1,0:T(8,128)} %bitcast.605, f32[]{:T(128)} %constant.121.clone.1), kind=kCustom, calls=%fused_computation.191 | custom fusion | flops 3145728 | bytes 3146240 | tf_op jit(solution)/shard_map/scatter-add | solution.py:259
  1555.6 38.0 %reduce-scatter.46.cloned.1.call-done = f32[768,256]{1,0:T(8,128)} async-done(((f32[768,1024]{1,0:T(8,128)}), f32[768,256]{1,0:T(8,128)}) %reduce-scatter.46.cloned.1.call-update) | async-done | bytes 786448 | tf_op jit(solution)/shard_map/reduce_scatter | solution.py:53
  1702.0 36.3 %reduce-scatter.52.cloned.1.call-done = f32[768,256]{1,0:T(8,128)} async-done(((f32[768,1024]{1,0:T(8,128)}), f32[768,256]{1,0:T(8,128)}) %reduce-scatter.52.cloned.1.call-update) | async-done | bytes 786448 | tf_op jit(solution)/shard_map/reduce_scatter | solution.py:53
  1835.1 29.5 %scatter_custom_fusion.5 = f32[768,1024]{1,0:T(8,128)} fusion(s32[3072]{0:T(1024)S(1)} %reshape.749, f32[3072,1024]{1,0:T(8,128)} %bitcast.603, f32[]{:T(128)} %constant.121.clone.1), kind=kCustom, calls=%fused_computation.189 | custom fusion | flops 3145728 | bytes 3146240 | tf_op jit(solution)/shard_map/scatter-add | solution.py:259
  1865.3 37.4 %reduce-scatter.54.cloned.1.call-done = f32[768,256]{1,0:T(8,128)} async-done(((f32[768,1024]{1,0:T(8,128)}), f32[768,256]{1,0:T(8,128)}) %reduce-scatter.54.cloned.1.call-update) | async-done | bytes 786448 | tf_op jit(solution)/shard_map/reduce_scatter | solution.py:53
  2062.2 32.3 %add_convert_fusion = bf16[8,1024,1024]{2,1,0:T(8,128)(2,1)} fusion(f32[8,1024,1024]{2,1,0:T(8,128)} %fusion.54, f32[8,1024,1024]{2,1,0:T(8,128)} %fusion.52, bf16[8,384,1024]{1,2,0:T(8,128)(2,1)} %copy.114, bf16[8,384,1024]{1,2,0:T(8,128)(2,1)} %copy.116, pred[]{:T(512)S(6)} %eq.44, bf16[8,384,512]{2,1,0:T(8,128)(2,1)} %get-tuple-element.123, ...), kind=kOutput, calls=%fused_computation.18 | convolution fusion | flops 6483345408 | bytes 102760448 | tf_op jit(solution)/shard_map/ecd,ech->edh/dot_general | solution.py:255
  2182.5 43.8 %psum.63 = f32[]{:T(128)} all-reduce(f32[]{:T(128)S(6)} %add.537), channel_id=1, replica_groups=mesh['section'=2,'row'=4,'col'=4] {'section','row','col'}, use_global_device_ids=true, to_apply=%region_36.38 | all-reduce | flops 1 | bytes 8 | tf_op jit(solution)/shard_map/psum | solution.py:445
  2256.6 141.7 %reduce-scatter.72.cloned.1.call-done = bf16[8,256,512]{2,1,0:T(8,128)(2,1)} async-done(((bf16[8,1024,512]{2,1,0:T(8,128)(2,1)}), bf16[8,256,512]{2,1,0:T(8,128)(2,1)}) %reduce-scatter.72.cloned.1.call-update) | async-done | bytes 2097168 | tf_op jit(solution)/shard_map/reduce_scatter | solution.py:439
  2402.4 143.3 %reduce-scatter.74.cloned.1.call-done = bf16[8,512,256]{2,1,0:T(8,128)(2,1)} async-done(((bf16[8,512,1024]{2,1,0:T(8,128)(2,1)}), bf16[8,512,256]{2,1,0:T(8,128)(2,1)}) %reduce-scatter.74.cloned.1.call-update) | async-done | bytes 2097168 | tf_op jit(solution)/shard_map/reduce_scatter | solution.py:440
  2549.6 21.1 reduce-scatter.64.cloned.1.call-done
  2570.8 22.8 reduce-scatter.66.cloned.1.call-done
  2593.6 28.2 %reduce-scatter.68.cloned.1.call-done = f32[256,256]{1,0:T(8,128)} async-done(((f32[256,1024]{1,0:T(8,128)}), f32[256,256]{1,0:T(8,128)}) %reduce-scatter.68.cloned.1.call-update) | async-done | bytes 262160 | tf_op jit(solution)/shard_map/reduce_scatter | solution.py:437
  2621.8 28.8 %reduce-scatter.62.cloned.1.call-done = f32[256,256]{1,0:T(8,128)} async-done(((f32[1024,256]{1,0:T(8,128)}), f32[256,256]{1,0:T(8,128)}) %reduce-scatter.62.cloned.1.call-update) | async-done | bytes 262160 | tf_op jit(solution)/shard_map/reduce_scatter | solution.py:430
  (806 shorter events, 1294.9 us)
Async XLA Ops:
  7.2 67.4 %all-gather.46.cloned.1.call-start = ((), (), s32[]{:S(2)}) async-start(), calls=%async_computation.61 | async-start | bytes 1966080 | tf_op jit(solution)/shard_map/all_gather | solution.py:39
  9.0 149.3 %reduce-scatter.26.cloned.1.call-start = ((), (), s32[]{:S(2)}) async-start(), calls=%async_computation.25 | async-start | bytes 1966080 | tf_op jit(solution)/shard_map/reduce_scatter | solution.py:43
  129.4 172.1 %all-gather.24.cloned.1.call-start = ((), (), s32[]{:S(2)}) async-start(), calls=%async_computation.26 | async-start | bytes 1966080 | tf_op jit(solution)/shard_map/all_gather | solution.py:39
  160.2 171.1 %all-gather.50.cloned.1.call-start = ((), (), s32[]{:S(2)}) async-start(), calls=%async_computation.63 | async-start | bytes 10485760 | tf_op jit(solution)/shard_map/all_gather | solution.py:79
  160.8 319.9 %all-gather.48.cloned.1.call-start = ((), (), s32[]{:S(2)}) async-start(), calls=%async_computation.62 | async-start | bytes 10485760 | tf_op jit(solution)/shard_map/all_gather | solution.py:78
  161.4 469.8 %all-gather.52.cloned.1.call-start = ((), (), s32[]{:S(2)}) async-start(), calls=%async_computation.64 | async-start | bytes 10485760 | tf_op jit(solution)/shard_map/all_gather | solution.py:80
  162.0 539.7 %reduce-scatter.28.cloned.1.call-start = ((), (), s32[]{:S(2)}) async-start(), calls=%async_computation.27 | async-start | bytes 1966080 | tf_op jit(solution)/shard_map/reduce_scatter | solution.py:43
  715.4 105.0 %reduce-scatter.30.cloned.1.call-start = ((), (), s32[]{:S(2)}) async-start(), calls=%async_computation.29 | async-start | bytes 1966080 | tf_op jit(solution)/shard_map/reduce_scatter | solution.py:43
  822.3 129.8 %reduce-scatter.32.cloned.1.call-start = ((), (), s32[]{:S(2)}) async-start(), calls=%async_computation.31 | async-start | bytes 1966080 | tf_op jit(solution)/shard_map/reduce_scatter | solution.py:43
  955.7 139.4 %reduce-scatter.38.cloned.1.call-start = ((), (), s32[]{:S(2)}) async-start(), calls=%async_computation.37 | async-start | bytes 3932160 | tf_op jit(solution)/shard_map/reduce_scatter | solution.py:53
  1057.0 73.4 %all-gather.36.cloned.1.call-start = ((), (), s32[]{:S(2)}) async-start(), calls=%async_computation.38 | async-start | bytes 1966080 | tf_op jit(solution)/shard_map/all_gather | solution.py:49
  1119.6 156.2 %reduce-scatter.34.cloned.1.call-start = ((), (), s32[]{:S(2)}) async-start(), calls=%async_computation.33 | async-start | bytes 1966080 | tf_op jit(solution)/shard_map/reduce_scatter | solution.py:43
  1257.9 63.8 %reduce-scatter.40.cloned.1.call-start = ((), (), s32[]{:S(2)}) async-start(), calls=%async_computation.39 | async-start | bytes 655360 | tf_op jit(solution)/shard_map/reduce_scatter | solution.py:295
  1266.6 74.8 %all-gather.32.cloned.1.call-start = ((), (), s32[]{:S(2)}) async-start(), calls=%async_computation.34 | async-start | bytes 1966080 | tf_op jit(solution)/shard_map/all_gather | solution.py:39
  1277.7 145.9 %reduce-scatter.44.cloned.1.call-start = ((), (), s32[]{:S(2)}) async-start(), calls=%async_computation.41 | async-start | bytes 3932160 | tf_op jit(solution)/shard_map/reduce_scatter | solution.py:53
  1326.7 125.1 %reduce-scatter.36.cloned.1.call-start = ((), (), s32[]{:S(2)}) async-start(), calls=%async_computation.35 | async-start | bytes 1966080 | tf_op jit(solution)/shard_map/reduce_scatter | solution.py:43
  1454.2 139.5 %reduce-scatter.46.cloned.1.call-start = ((), (), s32[]{:S(2)}) async-start(), calls=%async_computation.43 | async-start | bytes 3932160 | tf_op jit(solution)/shard_map/reduce_scatter | solution.py:53
  1555.6 70.9 %all-gather.40.cloned.1.call-start = ((), (), s32[]{:S(2)}) async-start(), calls=%async_computation.44 | async-start | bytes 1966080 | tf_op jit(solution)/shard_map/all_gather | solution.py:49
  1605.4 75.5 %reduce-scatter.50.cloned.1.call-start = ((), (), s32[]{:S(2)}) async-start(), calls=%async_computation.46 | async-start | bytes 655360 | tf_op jit(solution)/shard_map/reduce_scatter | solution.py:296
  1674.0 64.3 %reduce-scatter.52.cloned.1.call-start = ((), (), s32[]{:S(2)}) async-start(), calls=%async_computation.47 | async-start | bytes 3932160 | tf_op jit(solution)/shard_map/reduce_scatter | solution.py:53
  1701.9 81.5 %all-gather.42.cloned.1.call-start = ((), (), s32[]{:S(2)}) async-start(), calls=%async_computation.48 | async-start | bytes 1966080 | tf_op jit(solution)/shard_map/all_gather | solution.py:49
  1764.3 138.4 %reduce-scatter.54.cloned.1.call-start = ((), (), s32[]{:S(2)}) async-start(), calls=%async_computation.49 | async-start | bytes 3932160 | tf_op jit(solution)/shard_map/reduce_scatter | solution.py:53
  1864.6 102.4 %all-gather.44.cloned.1.call-start = ((), (), s32[]{:S(2)}) async-start(), calls=%async_computation.50 | async-start | bytes 1966080 | tf_op jit(solution)/shard_map/all_gather | solution.py:49
  1914.6 104.8 %reduce-scatter.58.cloned.1.call-start = ((), (), s32[]{:S(2)}) async-start(), calls=%async_computation.52 | async-start | bytes 655360 | tf_op jit(solution)/shard_map/reduce_scatter | solution.py:296
  2013.8 212.5 %reduce-scatter.60.cloned.1.call-start = ((), (), s32[]{:S(2)}) async-start(), calls=%async_computation.53 | async-start | bytes 3932160 | tf_op jit(solution)/shard_map/reduce_scatter | solution.py:53
  2043.5 208.9 %reduce-scatter.70.cloned.1.call-start = ((), (), s32[]{:S(2)}) async-start(), calls=%async_computation.58 | async-start | bytes 10485760 | tf_op jit(solution)/shard_map/reduce_scatter | solution.py:438
  2105.9 292.3 %reduce-scatter.72.cloned.1.call-start = ((), (), s32[]{:S(2)}) async-start(), calls=%async_computation.59 | async-start | bytes 10485760 | tf_op jit(solution)/shard_map/reduce_scatter | solution.py:439
  2106.7 439.0 %reduce-scatter.74.cloned.1.call-start = ((), (), s32[]{:S(2)}) async-start(), calls=%async_computation.60 | async-start | bytes 10485760 | tf_op jit(solution)/shard_map/reduce_scatter | solution.py:440
  2153.7 417.1 %reduce-scatter.64.cloned.1.call-start = ((), (), s32[]{:S(2)}) async-start(), calls=%async_computation.55 | async-start | bytes 655360 | tf_op jit(solution)/shard_map/reduce_scatter | solution.py:431
  2163.6 430.0 %reduce-scatter.66.cloned.1.call-start = ((), (), s32[]{:S(2)}) async-start(), calls=%async_computation.56 | async-start | bytes 655360 | tf_op jit(solution)/shard_map/reduce_scatter | solution.py:434
  2164.4 457.4 %reduce-scatter.68.cloned.1.call-start = ((), (), s32[]{:S(2)}) async-start(), calls=%async_computation.57 | async-start | bytes 1310720 | tf_op jit(solution)/shard_map/reduce_scatter | solution.py:437
  2174.6 475.9 %reduce-scatter.62.cloned.1.call-start = ((), (), s32[]{:S(2)}) async-start(), calls=%async_computation.54 | async-start | bytes 1310720 | tf_op jit(solution)/shard_map/reduce_scatter | solution.py:430
  (221 other events, 10133.7 us)
Sparse Core Ops, SparseCore 0:
  10.1 22.5 all-gather.45
  129.6 28.7 reduce-scatter.25
  181.7 149.6 all-gather.49
  332.9 147.8 all-gather.47
  482.3 148.8 all-gather.51
  676.8 24.8 reduce-scatter.27
  715.5 20.8 all-gather.25
  792.3 28.1 reduce-scatter.29
  822.4 19.8 all-gather.27
  923.9 28.1 reduce-scatter.31
  1057.1 37.9 reduce-scatter.37
  1106.8 20.9 all-gather.35
  1247.6 28.1 reduce-scatter.33
  1277.9 21.6 reduce-scatter.41
  1343.7 37.9 reduce-scatter.43
  1423.6 28.1 reduce-scatter.35
  1555.7 37.8 reduce-scatter.45
  1605.5 20.9 all-gather.39
  1652.3 21.6 reduce-scatter.49
  1702.1 36.1 reduce-scatter.51
  1864.7 37.9 reduce-scatter.53
  1914.8 21.0 all-gather.43
  1992.7 22.8 reduce-scatter.57
  2018.6 19.9 reduce-scatter.55
  2043.6 36.0 reduce-scatter.59
  2106.0 144.6 reduce-scatter.69
  2253.0 145.1 reduce-scatter.71
  2400.4 145.1 reduce-scatter.73
  2548.3 22.3 reduce-scatter.63
  2573.6 19.9 reduce-scatter.65
  2596.3 25.4 reduce-scatter.67
  2624.7 25.7 reduce-scatter.61
  (8 shorter events, 155.5 us)

commit v2 on v0

v2 whole, which is shorter than its diff:
```python
import functools

import jax
import jax.numpy as jnp
from jax import lax
from jax.experimental import pallas as pl
from jax.experimental.pallas import tpu as pltpu
from jax.sharding import PartitionSpec as P

HEAD = 64
HIDDEN_SIZE = 512
CONT_LEN = 512
CAP = 384
GROUP = 4

EPS = 1e-06
THETA = 10000.0
NEG = -1e30
BF16 = jnp.bfloat16
F32 = jnp.float32
VMEM_LIMIT = 60 * 1024 * 1024


def shift(value, axis, pairs):
    return lax.ppermute(value, axis, pairs)


def flip(value, bit):
    count = lax.axis_size("col")
    return shift(value, "col", [(i, i ^ bit) for i in range(count)])


def col_bits():
    count = lax.axis_size("col")
    bits = [1]
    while bits[-1] * 2 < count:
        bits.append(bits[-1] * 2)
    return bits


def gather_col(value):
    blocks = {0: value}
    for bit in reversed(col_bits()):
        for k in list(blocks):
            blocks[k ^ bit] = flip(blocks[k], bit)
    return [blocks[k] for k in range(lax.axis_size("col"))]


def scatter_col(blocks):
    blocks = dict(enumerate(blocks))
    total = None
    for bit in col_bits():
        keep = [k for k in blocks if not k & bit]
        total = {k: blocks[k].astype(F32) + flip(blocks[k ^ bit], bit).astype(F32) for k in keep}
        blocks = {k: total[k].astype(BF16) for k in keep}
    return total[0]


def ring(value):
    count = lax.axis_size("row")
    return shift(value, "row", [(i, (i + 1) % count) for i in range(count)])


def gather_row(value):
    pieces = [value]
    for _ in range(lax.axis_size("row") - 1):
        pieces.append(ring(pieces[-1]))
    return pieces


def scatter_row(parts):
    count = len(parts)
    if count == 1:
        return parts[0].astype(F32)
    running = parts[1]
    for k in range(2, count):
        running = (ring(running).astype(F32) + parts[k].astype(F32)).astype(BF16)
    return ring(running).astype(F32) + parts[0].astype(F32)


def dot_nn(left, right):
    return lax.dot_general(left, right, (((1,), (0,)), ((), ())), preferred_element_type=F32)


def dot_nt(left, right):
    return lax.dot_general(left, right, (((1,), (1,)), ((), ())), preferred_element_type=F32)


def dot_tn(left, right):
    return lax.dot_general(left, right, (((0,), (0,)), ((), ())), preferred_element_type=F32)


def swap_halves(value):
    lanes = value.shape[1]
    lane = lax.broadcasted_iota(jnp.int32, value.shape, 1)
    half = HEAD // 2
    ahead = pltpu.roll(value, lanes - half, 1)
    behind = pltpu.roll(value, half, 1)
    return jnp.where(lane % HEAD < half, ahead, behind)


def project_kernel(x_ref, gain_ref, w_ref, cos_ref, sin_ref, n_ref, out_ref):
    step = pl.program_id(0)
    turned = pl.num_programs(0) // 2

    @pl.when(step == 0)
    def _():
        x = x_ref[...].astype(F32)
        rho = lax.rsqrt(jnp.mean(x * x, axis=1, keepdims=True) + EPS)
        n_ref[...] = (x * rho * gain_ref[...]).astype(BF16)

    raw = dot_nn(n_ref[...], w_ref[...])
    cos, sin = cos_ref[...], sin_ref[...]
    left, right = raw[:, :128], raw[:, 128:]
    left = left * cos + swap_halves(left) * sin
    out_ref[:, :128] = left.astype(BF16)

    @pl.when(step < turned)
    def _():
        out_ref[:, 128:] = (right * cos + swap_halves(right) * sin).astype(BF16)

    @pl.when(step >= turned)
    def _():
        out_ref[:, 128:] = right.astype(BF16)


def project(x, gain, w, cos, sin):
    rows, width = x.shape
    columns = w.shape[1]
    whole = lambda i: (0, 0)
    return pl.pallas_call(
        project_kernel,
        grid=(columns // 256,),
        in_specs=[
            pl.BlockSpec((rows, width), whole),
            pl.BlockSpec((1, width), whole),
            pl.BlockSpec((width, 256), lambda i: (0, i)),
            pl.BlockSpec((rows, 128), whole),
            pl.BlockSpec((rows, 128), whole),
        ],
        out_specs=[
            pl.BlockSpec((rows, width), whole),
            pl.BlockSpec((rows, 256), lambda i: (0, i)),
        ],
        out_shape=[
            jax.ShapeDtypeStruct((rows, width), BF16),
            jax.ShapeDtypeStruct((rows, columns), BF16),
        ],
        compiler_params=pltpu.CompilerParams(vmem_limit_bytes=VMEM_LIMIT),
        cost_estimate=pl.CostEstimate(
            flops=2 * rows * width * columns,
            bytes_accessed=2 * (width * columns + rows * columns + 2 * rows * width),
            transcendentals=0,
        ),
    )(x, gain, w, cos, sin)


def stack_heads(value):
    low = (lax.broadcasted_iota(jnp.int32, (value.shape[0], 128), 1) < HEAD).astype(F32)
    first, second = value[:, :128].astype(F32), value[:, 128:].astype(F32)
    return jnp.concatenate(
        [first * low, second * low, first * (1.0 - low), second * (1.0 - low)], axis=0
    )


def unstack_heads(value):
    rows = value.shape[0] // 4
    low = lax.broadcasted_iota(jnp.int32, (rows, 128), 1) < HEAD
    first = jnp.where(low, value[:rows], value[2 * rows : 3 * rows])
    second = jnp.where(low, value[rows : 2 * rows], value[3 * rows :])
    return first, second


def attend_kernel(q_ref, k_ref, v_ref, bias_ref, o_ref, lse_ref):
    stacked = (stack_heads(q_ref[0]) * HEAD**-0.5).astype(BF16)
    scores = dot_nt(k_ref[0], stacked) + bias_ref[...]
    top = jnp.max(scores, axis=0, keepdims=True)
    weights = jnp.exp(scores - top)
    total = jnp.sum(weights, axis=0, keepdims=True)
    mixed = dot_tn(v_ref[0], weights.astype(BF16)) / total
    first, second = unstack_heads(mixed.T)
    o_ref[0, :, :128] = first
    o_ref[0, :, 128:] = second
    lse_ref[0, 0] = top + jnp.log(total)


def attend(qkv, kv, bias):
    micro, rows, _ = qkv.shape
    keys, width = kv.shape[1], kv.shape[2]
    groups = width // 256
    return pl.pallas_call(
        attend_kernel,
        grid=(micro, groups),
        in_specs=[
            pl.BlockSpec((1, rows, 256), lambda m, g: (m, 0, g)),
            pl.BlockSpec((1, keys, 128), lambda m, g: (m, 0, 2 * g)),
            pl.BlockSpec((1, keys, 128), lambda m, g: (m, 0, 2 * g + 1)),
            pl.BlockSpec((keys, 4 * rows), lambda m, g: (0, 0)),
        ],
        out_specs=[
            pl.BlockSpec((1, rows, 256), lambda m, g: (m, 0, g)),
            pl.BlockSpec((1, 1, 1, 4 * rows), lambda m, g: (m, g, 0, 0)),
        ],
        out_shape=[
            jax.ShapeDtypeStruct((micro, rows, groups * 256), F32),
            jax.ShapeDtypeStruct((micro, groups, 1, 4 * rows), F32),
        ],
        compiler_params=pltpu.CompilerParams(vmem_limit_bytes=VMEM_LIMIT),
        cost_estimate=pl.CostEstimate(
            flops=micro * groups * 4 * rows * keys * 128 * 4,
            bytes_accessed=2 * micro * keys * width + 4 * keys * 4 * rows,
            transcendentals=micro * groups * 4 * rows * keys,
        ),
    )(qkv, kv, kv, bias)


def attend_back_kernel(
    q_ref, k_ref, v_ref, bias_ref, do_ref, o_ref, lse_ref, cos_ref, sin_ref, kcos_ref, ksin_ref,
    dq_ref, dkv_ref,
):
    scale = HEAD**-0.5
    queries = (stack_heads(q_ref[0]) * scale).astype(BF16)
    grads_wide = stack_heads(do_ref[0])
    product = grads_wide * stack_heads(o_ref[0])
    delta = jnp.sum(product.T, axis=0, keepdims=True)
    grads = grads_wide.astype(BF16)
    keys, values = k_ref[0], v_ref[0]
    probs = jnp.exp(dot_nt(keys, queries) + bias_ref[...] - lse_ref[0, 0])
    dvalues = dot_nn(probs.astype(BF16), grads)
    dscores = (probs * (dot_nt(values, grads) - delta)).astype(BF16)
    dkeys = dot_nn(dscores, queries)
    dqueries = dot_tn(keys, dscores) * scale
    first, second = unstack_heads(dqueries.T)
    cos, sin = cos_ref[...], sin_ref[...]
    dq_ref[0, :, :128] = (first * cos - swap_halves(first) * sin).astype(BF16)
    dq_ref[0, :, 128:] = (second * cos - swap_halves(second) * sin).astype(BF16)
    dkv_ref[0, :, :128] = (dkeys * kcos_ref[...] - swap_halves(dkeys) * ksin_ref[...]).astype(BF16)
    dkv_ref[0, :, 128:] = dvalues.astype(BF16)


def attend_back(qkv, kv, bias, grad, o, lse, cos, sin, kcos, ksin):
    micro, rows, _ = qkv.shape
    keys, width = kv.shape[1], kv.shape[2]
    groups = width // 256
    mine = pl.BlockSpec((1, rows, 256), lambda m, g: (m, 0, g))
    return pl.pallas_call(
        attend_back_kernel,
        grid=(micro, groups),
        in_specs=[
            mine,
            pl.BlockSpec((1, keys, 128), lambda m, g: (m, 0, 2 * g)),
            pl.BlockSpec((1, keys, 128), lambda m, g: (m, 0, 2 * g + 1)),
            pl.BlockSpec((keys, 4 * rows), lambda m, g: (0, 0)),
            mine,
            mine,
            pl.BlockSpec((1, 1, 1, 4 * rows), lambda m, g: (m, g, 0, 0)),
            pl.BlockSpec((rows, 128), lambda m, g: (0, 0)),
            pl.BlockSpec((rows, 128), lambda m, g: (0, 0)),
            pl.BlockSpec((keys, 128), lambda m, g: (0, 0)),
            pl.BlockSpec((keys, 128), lambda m, g: (0, 0)),
        ],
        out_specs=[mine, pl.BlockSpec((1, keys, 256), lambda m, g: (m, 0, g))],
        out_shape=[
            jax.ShapeDtypeStruct((micro, rows, groups * 256), BF16),
            jax.ShapeDtypeStruct((micro, keys, width), BF16),
        ],
        compiler_params=pltpu.CompilerParams(vmem_limit_bytes=VMEM_LIMIT),
        cost_estimate=pl.CostEstimate(
            flops=micro * groups * 4 * rows * keys * 128 * 10,
            bytes_accessed=4 * micro * keys * width + 4 * keys * 4 * rows,
            transcendentals=micro * groups * 4 * rows * keys,
        ),
    )(qkv, kv, kv, bias, grad, o, lse, cos, sin, kcos, ksin)


def chosen_rows(place_ref, weight_ref, m, cap, tokens):
    slots = lax.broadcasted_iota(jnp.int32, (cap, tokens), 0)
    hit = slots == place_ref[0, m : m + 1, :]
    pick = jnp.where(hit, 1.0, 0.0)
    weight = jnp.sum(pick * weight_ref[0, m : m + 1, :], axis=1, keepdims=True)
    return pick.astype(BF16), weight


def load_tokens(meta_ref, pieces, scratch, cut):
    count = scratch.shape[2] // cut
    for at, piece in enumerate(pieces):
        rows = piece.shape[1]
        for k in range(count):
            start = pl.multiple_of(meta_ref[k], cut)
            scratch[:, at * rows : (at + 1) * rows, k * cut : (k + 1) * cut] = piece[
                :, :, pl.ds(start, cut)
            ]


def store_tokens(meta_ref, out_ref, total, cut):
    count = total.shape[2] // cut
    blocks, _, rows, _ = out_ref.shape
    for at in range(blocks):
        for k in range(count):
            start = pl.multiple_of(meta_ref[k], cut)
            out_ref[at, :, :, pl.ds(start, cut)] = total[
                :, at * rows : (at + 1) * rows, k * cut : (k + 1) * cut
            ].astype(BF16)


def by_load(meta_ref, nrow, body, empty=None):
    e = pl.program_id(0)
    most = jnp.maximum(meta_ref[nrow + 2 * e], meta_ref[nrow + 2 * e + 1])
    below = 0
    for cap in (CAP // 3, 2 * CAP // 3, CAP):
        pl.when((most > below) & (most <= cap))(functools.partial(body, cap))
        below = cap
    if empty is not None:
        pl.when(most == 0)(empty)


def experts_kernel(ncol, nrow, meta_ref, place_ref, weight_ref, *refs):
    pieces, refs = refs[:ncol], refs[ncol:]
    gates, refs = refs[:nrow], refs[nrow:]
    ups, refs = refs[:nrow], refs[nrow:]
    downs, refs = refs[:nrow], refs[nrow:]
    y_ref, chosen_ref, hidden_ref, tokens_ref, total_ref, rows_ref, out_ref = refs
    micro, tokens, width = tokens_ref.shape
    cut = width // nrow
    hidden = gates[0].shape[2]
    e = pl.program_id(0)

    @pl.when(e == 0)
    def _():
        load_tokens(meta_ref, pieces, tokens_ref, cut)
        total_ref[...] = jnp.zeros_like(total_ref)

    def body(cap):
        picks, weights = [], []
        for m in range(micro):
            pick, weight = chosen_rows(place_ref, weight_ref, m, cap, tokens)
            chosen = dot_nn(pick, tokens_ref[m]).astype(BF16)
            rows_ref[m * cap : (m + 1) * cap, :] = chosen
            chosen_ref[0, m, :cap, :] = chosen
            picks.append(pick)
            weights.append(weight)
        used = micro * cap
        gate = sum(
            dot_nn(rows_ref[:used, k * cut : (k + 1) * cut], gates[k][0]) for k in range(nrow)
        )
        up = sum(dot_nn(rows_ref[:used, k * cut : (k + 1) * cut], ups[k][0]) for k in range(nrow))
        for m in range(micro):
            hidden_ref[0, m, :cap, :hidden] = gate[m * cap : (m + 1) * cap].astype(BF16)
            hidden_ref[0, m, :cap, hidden:] = up[m * cap : (m + 1) * cap].astype(BF16)
        active = (gate * jax.nn.sigmoid(gate) * up).astype(BF16)
        scale = jnp.concatenate(weights, axis=0)
        for k in range(nrow):
            out_ref[:used, k * cut : (k + 1) * cut] = (
                dot_nn(active, downs[k][0]) * scale
            ).astype(BF16)
        for m in range(micro):
            total_ref[m] += dot_tn(picks[m], out_ref[m * cap : (m + 1) * cap, :])

    by_load(meta_ref, nrow, body)

    @pl.when(e == pl.num_programs(0) - 1)
    def _():
        store_tokens(meta_ref, y_ref, total_ref, cut)


def expert_specs(pieces, weights, slots):
    micro, rows, width = pieces[0].shape
    at_expert = lambda e: (e, 0, 0)
    specs = [
        pl.BlockSpec(memory_space=pltpu.SMEM),
        pl.BlockSpec((1, *slots.shape[1:]), at_expert),
        pl.BlockSpec((1, *slots.shape[1:]), at_expert),
    ]
    specs += [pl.BlockSpec((micro, rows, width), lambda e: (0, 0, 0)) for _ in pieces]
    specs += [pl.BlockSpec((1, *w.shape[1:]), at_expert) for w in weights]
    return specs


def experts(meta, place, weight, pieces, gates, ups, downs):
    micro, rows, width = pieces[0].shape
    local = place.shape[0]
    ncol, nrow, hidden = len(pieces), len(gates), gates[0].shape[2]
    tokens = ncol * rows
    weights = [*gates, *ups, *downs]
    fixed = lambda e: (0, 0, 0, 0)
    at_expert = lambda e: (e, 0, 0, 0)
    return pl.pallas_call(
        functools.partial(experts_kernel, ncol, nrow),
        grid=(local,),
        in_specs=expert_specs(pieces, weights, place),
        out_specs=[
            pl.BlockSpec((ncol, micro, rows, width), fixed),
            pl.BlockSpec((1, micro, CAP, width), at_expert),
            pl.BlockSpec((1, micro, CAP, 2 * hidden), at_expert),
        ],
        out_shape=[
            jax.ShapeDtypeStruct((ncol, micro, rows, width), BF16),
            jax.ShapeDtypeStruct((local, micro, CAP, width), BF16),
            jax.ShapeDtypeStruct((local, micro, CAP, 2 * hidden), BF16),
        ],
        scratch_shapes=[
            pltpu.VMEM((micro, tokens, width), BF16),
            pltpu.VMEM((micro, tokens, width), F32),
            pltpu.VMEM((micro * CAP, width), BF16),
            pltpu.VMEM((micro * CAP, width), BF16),
        ],
        compiler_params=pltpu.CompilerParams(vmem_limit_bytes=VMEM_LIMIT),
        cost_estimate=pl.CostEstimate(
            flops=local * micro * 256 * width * (6 * hidden + 4 * tokens),
            bytes_accessed=local * width * (6 * hidden + 4 * micro * CAP),
            transcendentals=local * micro * CAP * hidden,
        ),
    )(meta, place, weight, *pieces, *weights)


def experts_back_kernel(ncol, nrow, with_grads, meta_ref, place_ref, weight_ref, *refs):
    pieces, refs = refs[:ncol], refs[ncol:]
    gates, refs = refs[:nrow], refs[nrow:]
    ups, refs = refs[:nrow], refs[nrow:]
    downs, refs = refs[:nrow], refs[nrow:]
    chosen_ref, hidden_ref, dx_ref, refs = refs[0], refs[1], refs[2], refs[3:]
    if with_grads:
        dgates, refs = refs[:nrow], refs[nrow:]
        dups, refs = refs[:nrow], refs[nrow:]
        ddowns, refs = refs[:nrow], refs[nrow:]
    tokens_ref, total_ref, rows_ref, out_ref, dhid_ref = refs
    micro, tokens, width = tokens_ref.shape
    cut = width // nrow
    hidden = gates[0].shape[2]
    e = pl.program_id(0)

    @pl.when(e == 0)
    def _():
        load_tokens(meta_ref, pieces, tokens_ref, cut)
        total_ref[...] = jnp.zeros_like(total_ref)

    def body(cap):
        picks = []
        for m in range(micro):
            pick, weight = chosen_rows(place_ref, weight_ref, m, cap, tokens)
            picks.append(pick)
            rows_ref[m * cap : (m + 1) * cap, :] = (
                dot_nn(pick, tokens_ref[m]) * weight
            ).astype(BF16)
        used = micro * cap
        dactive = sum(
            dot_nt(rows_ref[:used, k * cut : (k + 1) * cut], downs[k][0]) for k in range(nrow)
        )
        gate = jnp.concatenate([hidden_ref[0, m, :cap, :hidden] for m in range(micro)], axis=0)
        up = jnp.concatenate([hidden_ref[0, m, :cap, hidden:] for m in range(micro)], axis=0)
        gate, up = gate.astype(F32), up.astype(F32)
        sigmoid = jax.nn.sigmoid(gate)
        silu = gate * sigmoid
        dhid_ref[:used, :hidden] = (dactive * up * sigmoid * (1.0 + gate * (1.0 - sigmoid))).astype(
            BF16
        )
        dhid_ref[:used, hidden:] = (dactive * silu).astype(BF16)
        dgate, dup = dhid_ref[:used, :hidden], dhid_ref[:used, hidden:]
        for k in range(nrow):
            out_ref[:used, k * cut : (k + 1) * cut] = (
                dot_nt(dgate, gates[k][0]) + dot_nt(dup, ups[k][0])
            ).astype(BF16)
        for m in range(micro):
            total_ref[m] += dot_tn(picks[m], out_ref[m * cap : (m + 1) * cap, :])
        if with_grads:
            active = (silu * up).astype(BF16)
            for m in range(micro):
                out_ref[m * cap : (m + 1) * cap, :] = chosen_ref[0, m, :cap, :]
            for k in range(nrow):
                lanes = slice(k * cut, (k + 1) * cut)
                dgates[k][0] = dot_tn(out_ref[:used, lanes], dgate).astype(BF16)
                dups[k][0] = dot_tn(out_ref[:used, lanes], dup).astype(BF16)
                ddowns[k][0] = dot_tn(active, rows_ref[:used, lanes]).astype(BF16)

    def empty():
        if with_grads:
            for ref in (*dgates, *dups, *ddowns):
                ref[...] = jnp.zeros_like(ref)

    by_load(meta_ref, nrow, body, empty)

    @pl.when(e == pl.num_programs(0) - 1)
    def _():
        store_tokens(meta_ref, dx_ref, total_ref, cut)


def experts_back(meta, place, weight, pieces, gates, ups, downs, chosen, hid, with_grads):
    micro, rows, width = pieces[0].shape
    local = place.shape[0]
    ncol, nrow, hidden = len(pieces), len(gates), gates[0].shape[2]
    tokens = ncol * rows
    weights = [*gates, *ups, *downs]
    at_expert = lambda e: (e, 0, 0, 0)
    out_specs = [pl.BlockSpec((ncol, micro, rows, width), lambda e: (0, 0, 0, 0))]
    out_shape = [jax.ShapeDtypeStruct((ncol, micro, rows, width), BF16)]
    if with_grads:
        out_specs += [pl.BlockSpec((1, *w.shape[1:]), lambda e: (e, 0, 0)) for w in weights]
        out_shape += [jax.ShapeDtypeStruct(w.shape, BF16) for w in weights]
    results = pl.pallas_call(
        functools.partial(experts_back_kernel, ncol, nrow, with_grads),
        grid=(local,),
        in_specs=[
            *expert_specs(pieces, weights, place),
            pl.BlockSpec((1, micro, CAP, width), at_expert),
            pl.BlockSpec((1, micro, CAP, 2 * hidden), at_expert),
        ],
        out_specs=out_specs,
        out_shape=out_shape,
        scratch_shapes=[
            pltpu.VMEM((micro, tokens, width), BF16),
            pltpu.VMEM((micro, tokens, width), F32),
            pltpu.VMEM((micro * CAP, width), BF16),
            pltpu.VMEM((micro * CAP, width), BF16),
            pltpu.VMEM((micro * CAP, 2 * hidden), BF16),
        ],
        compiler_params=pltpu.CompilerParams(vmem_limit_bytes=VMEM_LIMIT),
        cost_estimate=pl.CostEstimate(
            flops=local * micro * 256 * width * (12 * hidden + 4 * tokens),
            bytes_accessed=local * width * (12 * hidden + 4 * micro * CAP),
            transcendentals=local * micro * CAP * hidden,
        ),
    )(meta, place, weight, *pieces, *weights, chosen, hid)
    if not with_grads:
        return results[0], None
    return results[0], (
        results[1 : 1 + nrow],
        results[1 + nrow : 1 + 2 * nrow],
        results[1 + 2 * nrow :],
    )


def forward_layer(layer_in, env, weights):
    micro, rows, width = layer_in.shape
    flat = micro * rows
    prompt = env["prompt"]
    normed, qkv = project(
        layer_in.reshape(flat, width), env["gain_first"], weights["qkv"], env["cos2"], env["sin2"]
    )
    qkv = qkv.reshape(micro, rows, 2 * width)
    own = qkv[:, :, width:]
    blocks = gather_col(own)
    for piece in gather_row(own[:, :prompt])[1:]:
        blocks += gather_col(piece)
    kv = jnp.concatenate(blocks, axis=1)
    mixed, lse = attend(qkv, kv, env["bias"])
    mixed_b = mixed.astype(BF16).reshape(flat, width)
    second = layer_in.reshape(flat, width).astype(F32) + dot_nn(mixed_b, weights["out"])
    second_b = second.astype(BF16)
    wide = second_b.astype(F32)
    rho = lax.rsqrt(jnp.mean(wide * wide, axis=1, keepdims=True) + EPS)
    normed_second = (wide * rho * env["gain_second"]).astype(BF16)
    pieces = gather_col(normed_second.reshape(micro, rows, width))
    partial, chosen, hid = experts(
        env["meta"], env["place"], env["weight"], pieces, *weights["experts"]
    )
    summed = scatter_col([partial[k] for k in range(partial.shape[0])])
    result = second.reshape(micro, rows, width) + summed
    keep = {
        "layer_in": layer_in,
        "normed": normed,
        "qkv": qkv,
        "kv": kv,
        "mixed": mixed,
        "lse": lse,
        "second_b": second_b,
        "chosen": chosen,
        "hid": hid,
    }
    return result, keep


def norm_back(grad, value, gain):
    width = value.shape[1]
    wide = value.astype(F32)
    rho = lax.rsqrt(jnp.mean(wide * wide, axis=1, keepdims=True) + EPS)
    scaled = grad * gain
    inner = jnp.sum(scaled * wide, axis=1, keepdims=True)
    out = rho * scaled - wide * (rho * rho * rho) * (inner / width)
    return out, jnp.sum(grad * wide * rho, axis=0)


def backward_layer(grad_result, keep, env, weights, with_grads):
    micro, rows, width = grad_result.shape
    flat = micro * rows
    prompt = env["prompt"]
    ncol, nrow = lax.axis_size("col"), lax.axis_size("row")
    pieces = gather_col(grad_result.astype(BF16))
    partial, expert_grads = experts_back(
        env["meta"], env["place"], env["weight"], pieces, *weights["experts"],
        keep["chosen"], keep["hid"], with_grads,
    )
    dn2 = scatter_col([partial[k] for k in range(ncol)]).reshape(flat, width)
    dnorm, gain_second = norm_back(dn2, keep["second_b"], env["gain_second"])
    dsecond = grad_result.reshape(flat, width) + dnorm
    dbranch = dsecond.astype(BF16)
    dmixed = dot_nt(dbranch, weights["out"]).astype(BF16)
    dq, dkv = attend_back(
        keep["qkv"], keep["kv"], env["bias"], dmixed.reshape(micro, rows, width), keep["mixed"],
        keep["lse"], env["cos"], env["sin"], env["kcos"], env["ksin"],
    )
    own = scatter_col([dkv[:, k * rows : (k + 1) * rows] for k in range(ncol)])
    parts = [own[:, :prompt]]
    at = ncol * rows
    for _ in range(1, nrow):
        cut = [dkv[:, at + k * prompt : at + (k + 1) * prompt] for k in range(ncol)]
        parts.append(scatter_col(cut).astype(BF16))
        at += ncol * prompt
    own = jnp.concatenate([scatter_row(parts), own[:, prompt:]], axis=1).astype(BF16)
    dqkv = jnp.concatenate([dq, own], axis=2).reshape(flat, 2 * width)
    dn1 = dot_nt(dqkv, weights["qkv"])
    dnorm, gain_first = norm_back(dn1, keep["layer_in"].reshape(flat, width), env["gain_first"])
    grad_in = (dsecond + dnorm).reshape(micro, rows, width)
    if not with_grads:
        return grad_in, None
    return grad_in, {
        "qkv": dot_tn(keep["normed"], dqkv),
        "out": dot_tn(keep["mixed"].astype(BF16).reshape(flat, width), dbranch),
        "experts": expert_grads,
        "gain_first": gain_first,
        "gain_second": gain_second,
    }


def own_rows(value, prompt_rows):
    micro, _, shard = value.shape
    ncol = lax.axis_size("col")
    return jnp.concatenate(
        [
            value[:, :prompt_rows].reshape(micro, ncol, -1, shard),
            value[:, prompt_rows:].reshape(micro, ncol, -1, shard),
        ],
        axis=2,
    )


def to_rows(value, prompt_rows):
    split = own_rows(value, prompt_rows)
    return lax.all_to_all(split, "col", 1, 3, tiled=True)[:, 0]


def to_columns(value, prompt):
    micro, _, width = value.shape
    ncol = lax.axis_size("col")
    split = lax.all_to_all(value[:, None], "col", 3, 1, tiled=True)
    shard = width // ncol
    return jnp.concatenate(
        [
            split[:, :, :prompt].reshape(micro, -1, shard),
            split[:, :, prompt:].reshape(micro, -1, shard),
        ],
        axis=1,
    )


def turn_tables(positions):
    half = HEAD // 2
    freqs = THETA ** (-(jnp.arange(half).astype(F32) * 2.0) / HEAD)
    angles = positions.astype(F32)[:, None] * freqs[None, :]
    cos, sin = jnp.cos(angles), jnp.sin(angles)
    return (
        jnp.concatenate([cos, cos, cos, cos], axis=1),
        jnp.concatenate([-sin, sin, -sin, sin], axis=1),
    )


def small_weights(w_query, w_key, w_value, w_out):
    nrow, ncol = lax.axis_size("row"), lax.axis_size("col")
    cut, columns = w_query.shape
    packed = jnp.concatenate([w_query, w_key, w_value], axis=1)
    whole = lax.all_gather(packed, ("row", "col"), axis=0)
    whole = whole.reshape(nrow, ncol, cut, -1)
    pick = lambda a, b: whole[..., a:b].transpose(0, 2, 1, 3).reshape(nrow * cut, -1)
    kcols = w_key.shape[1]
    query = pick(0, columns)
    key, value = pick(columns, columns + kcols), pick(columns + kcols, columns + 2 * kcols)
    width = nrow * cut
    query = query.reshape(width, -1, 2, 2, HEAD).transpose(0, 1, 3, 2, 4).reshape(width, -1)
    both = jnp.stack([key.reshape(width, -1, 128), value.reshape(width, -1, 128)], axis=2)
    out = lax.all_gather(w_out, ("row", "col"), axis=0)
    out = out.reshape(nrow, ncol, *w_out.shape).transpose(1, 2, 0, 3).reshape(-1, width)
    out = out.reshape(-1, 2, 2, HEAD, width).transpose(0, 2, 1, 3, 4).reshape(-1, width)
    return jnp.concatenate([query, both.reshape(width, -1)], axis=1), out


def small_gradients(grad_qkv, grad_out, cut, columns, kcols):
    nrow, ncol = lax.axis_size("row"), lax.axis_size("col")
    width = grad_out.shape[1]
    heads = nrow * cut
    query = grad_qkv[:, :width].astype(BF16)
    query = query.reshape(heads, -1, 2, 2, HEAD).transpose(0, 1, 3, 2, 4).reshape(heads, -1)
    both = grad_qkv[:, width:].astype(BF16).reshape(heads, -1, 2, 128)
    key, value = both[:, :, 0].reshape(heads, -1), both[:, :, 1].reshape(heads, -1)
    split = lambda g: g.reshape(nrow, cut, ncol, -1).transpose(0, 2, 1, 3)
    packed = jnp.concatenate([split(query), split(key), split(value)], axis=3)
    packed = packed.reshape(nrow * ncol * cut, -1)
    packed = lax.psum_scatter(packed, ("row", "col"), scatter_dimension=0, tiled=True).astype(F32)
    out = grad_out.astype(BF16)
    out = out.reshape(-1, 2, 2, HEAD, width).transpose(0, 2, 1, 3, 4).reshape(ncol, -1, nrow, width // nrow)
    out = out.transpose(2, 0, 1, 3).reshape(-1, width // nrow)
    out = lax.psum_scatter(out, ("row", "col"), scatter_dimension=0, tiled=True).astype(F32)
    return (
        packed[:, :columns],
        packed[:, columns : columns + kcols],
        packed[:, columns + kcols :],
        out,
    )


def routing(expert_ids, gates, prompt_rows, local):
    ncol, col = lax.axis_size("col"), lax.axis_index("col")

    def mine(value):
        blocks = own_rows(value, prompt_rows)
        order = [lax.dynamic_index_in_dim(blocks, col ^ k, 1, False) for k in range(ncol)]
        return jnp.concatenate(order, axis=1).transpose(0, 2, 1)

    ids, scale = mine(expert_ids), mine(gates)
    names = col * local + jnp.arange(local, dtype=jnp.int32)
    match = ids[None] == names[:, None, None, None]
    member = jnp.any(match, axis=2)
    weight = jnp.sum(jnp.where(match, scale[None], 0.0), axis=2)
    tokens = member.shape[2]
    order = jnp.arange(tokens, dtype=jnp.int32)
    earlier = (order[:, None] <= order[None, :]).astype(BF16)
    seen = dot_nn(member.astype(BF16).reshape(-1, tokens), earlier).astype(jnp.int32)
    seen = seen.reshape(member.shape)
    return jnp.where(member, seen - 1, -1), weight, seen[:, :, -1]


def on_device(
    x_in,
    targets,
    w_query,
    w_key,
    w_value,
    w_out,
    w_gate,
    w_up,
    w_down,
    gain_attn,
    gain_ffn,
    expert_ids,
    gates,
    lengths,
):
    section, row, col = (lax.axis_index(name) for name in ("section", "row", "col"))
    nrow, ncol = lax.axis_size("row"), lax.axis_size("col")
    micro, _, tokens, shard = x_in.shape
    width = shard * ncol
    prompt_rows = tokens - CONT_LEN
    prompt_len = prompt_rows * nrow
    prompt, cont = prompt_rows // ncol, CONT_LEN // ncol
    rows = prompt + cont
    local, cut = w_gate.shape[1], w_gate.shape[2]
    first_section = section == 0

    gathered = tuple(gather_row(w[0]) for w in (w_gate, w_up, w_down))
    qkv_weight, out_weight = small_weights(w_query[0], w_key[0], w_value[0], w_out[0])
    weights = {"experts": gathered, "qkv": qkv_weight, "out": out_weight}

    def positions_of(row_index, col_index):
        return row_index * prompt_rows + col_index * prompt + jnp.arange(prompt, dtype=jnp.int32)

    def cont_positions(col_index):
        return prompt_len + col_index * cont + jnp.arange(cont, dtype=jnp.int32)

    positions = jnp.concatenate([positions_of(row, col), cont_positions(col)])
    key_positions = []
    for k in range(ncol):
        key_positions += [positions_of(row, col ^ k), cont_positions(col ^ k)]
    for j in range(1, nrow):
        key_positions += [positions_of((row - j) % nrow, col ^ k) for k in range(ncol)]
    key_positions = jnp.concatenate(key_positions)
    bias = jnp.where(key_positions[:, None] <= jnp.tile(positions, GROUP)[None, :], 0.0, NEG)
    cos, sin = turn_tables(positions)
    kcos, ksin = turn_tables(key_positions)
    place, weight, counts = routing(expert_ids[0, :, 0], gates[0, :, 0], prompt_rows, local)
    starts = ((row - jnp.arange(nrow, dtype=jnp.int32)) % nrow) * cut
    env = {
        "prompt": prompt,
        "gain_first": gain_attn.astype(F32),
        "gain_second": gain_ffn.astype(F32),
        "cos": cos,
        "sin": sin,
        "cos2": jnp.concatenate([cos] * micro, axis=0),
        "sin2": jnp.concatenate([sin] * micro, axis=0),
        "kcos": kcos,
        "ksin": ksin,
        "bias": bias,
        "place": place,
        "weight": weight,
        "meta": jnp.concatenate([starts, counts.reshape(-1)]),
    }

    first_in = to_rows(x_in[:, 0], prompt_rows)
    goal = to_rows(targets[:, 0], prompt_rows).astype(F32)

    mid, _ = forward_layer(first_in, env, weights)
    received = shift(mid.astype(BF16), "section", [(0, 1)])
    layer_in = jnp.where(first_section, first_in, received)
    final, keep = forward_layer(layer_in, env, weights)

    count = (micro * prompt_len + jnp.sum(lengths)).astype(F32)
    length = lax.dynamic_index_in_dim(lengths, row, 1, keepdims=False)
    valid = (positions[None, :] - prompt_len < length[:, None]).astype(F32)[:, :, None]
    diff = (final - goal) * valid
    loss = jnp.where(first_section, 0.0, jnp.sum(diff * diff) / count)
    dfinal = (2.0 / count) * diff

    dmid, _ = backward_layer(dfinal, keep, env, weights, False)
    received = shift(dmid.astype(BF16), "section", [(1, 0)])
    grad_result = jnp.where(first_section, received.astype(F32), dfinal)
    grad_in, grads = backward_layer(grad_result, keep, env, weights, True)

    grad_gate, grad_up, grad_down = (scatter_row(list(g)) for g in grads["experts"])
    grad_query, grad_key, grad_value, grad_out = small_gradients(
        grads["qkv"], grads["out"], w_query.shape[1], w_query.shape[2], w_key.shape[2]
    )
    gains = lax.psum(jnp.stack([grads["gain_first"], grads["gain_second"]]), ("row", "col"))
    gains = lax.dynamic_slice_in_dim(gains, col * shard, shard, 1)
    loss = lax.psum(loss, ("section", "row", "col"))
    outputs = to_columns(final.astype(BF16), prompt)
    input_grads = to_columns(grad_in.astype(BF16), prompt)
    return (
        outputs[None, :, None],
        loss,
        input_grads[None, :, None],
        grad_query[None],
        grad_key[None],
        grad_value[None],
        grad_out[None],
        grad_gate[None],
        grad_up[None],
        grad_down[None],
        gains[:1],
        gains[1:],
    )


def solution(mesh):
    in_specs = (
        P(None, "row", None, "col"),
        P(None, "row", None, "col"),
        P("section", "row", "col"),
        P("section", "row", "col"),
        P("section", "row", "col"),
        P("section", "col", "row"),
        P("section", "col", "row", None),
        P("section", "col", "row", None),
        P("section", "col", None, "row"),
        P("section", None),
        P("section", None),
        P("section", None, "row", None, None),
        P("section", None, "row", None, None),
        P(),
    )
    out_specs = (
        P("section", None, "row", None, "col"),
        P(),
        P("section", None, "row", None, "col"),
        P("section", "row", "col"),
        P("section", "row", "col"),
        P("section", "row", "col"),
        P("section", "col", "row"),
        P("section", "col", "row", None),
        P("section", "col", "row", None),
        P("section", "col", None, "row"),
        P("section", "col"),
        P("section", "col"),
    )
    return jax.shard_map(
        on_device, mesh=mesh, in_specs=in_specs, out_specs=out_specs, check_vma=False
    )
```

time: 3030 us -> 1770 us (0.58)
  waiting for transfers between devices: 1540 us -> 890 us
  matrix products: 527 us -> 20.3 us
  Pallas kernels: 0 us -> 309 us
  other arithmetic: 364 us -> 116 us
  local copies, waits for them, and re-layouts: 313 us -> 155 us
  starting transfers between devices: 13.8 us -> 82.4 us
  blocking collectives: 239 us -> 173 us
    reduce_scatter x25 -> x2, waiting for transfers between devices: 1070 us -> 0.01 us  [the longest x1 0.01 us: small_gradients(): lax.psum_scatter(out, ('row', 'col'), scatter_dimension=0, tiled=True)]
    ppermute x4 -> x104, waiting for transfers between devices: 38 us -> 825 us  [shift(): return lax.ppermute(value, axis, pairs)]
    dot_general x57 -> x9, matrix products: 527 us -> 20.3 us  [the longest x4 10.1 us: dot_nt(): lax.dot_general(left, right, (((1,), (1,)), ((), ())), preferred_element_...]
    all_gather x15 -> x2, waiting for transfers between devices: 430 us -> 54.1 us  [the longest x1 54.1 us: small_weights(): whole = lax.all_gather(packed, ('row', 'col'), axis=0)]
    pallas_call x0 -> x10, Pallas kernels: none -> 309 us  [the longest x2 105 us: experts_back(): pl.pallas_call(functools.partial(experts_back_kernel, ncol, nrow, with_gr...]
    gather x18 -> x0, local copies, waits for them, and re-layouts: 185 us -> none  [the longest x6 69.2 us: forward_layer(): chosen = normed_second[index]]
    scatter-add x6 -> x0, other arithmetic: 178 us -> none  [the longest x3 88.8 us: backward_layer(): jax.ops.segment_sum(grad_chosen.reshape(-1, width), index.reshape(-1), nu...]
    all_gather x10 -> x0, blocking collectives: 149 us -> none  [the longest x3 43.5 us: forward_layer(): lax.all_gather(values_own[:prompt_rows], 'row', axis=0, tiled=True)]
  transfers between devices with their start and end apart: 44 -> 112, of which waited for: 33 -> 49; matrix products, arithmetic and copies ran while one was open for 20% -> 13% of each run, Pallas kernels for 0% -> 2%
where the time goes in v2:
time: 1770 us; the launch traced here: 1760 us
  waiting for transfers between devices  890 us (50%)
  Pallas kernels  309 us (17%)
  blocking collectives  173 us (10%)
  local copies, waits for them, and re-layouts  155 us (9%)
  other arithmetic  116 us (7%)
  starting transfers between devices  82.4 us (5%)
  matrix products  20.3 us (1%)
    ppermute x104, waiting for transfers between devices, shift(): return lax.ppermute(value, axis, pairs)  825 us
    psum x1, blocking collectives, on_device(): loss = lax.psum(loss, ('section', 'row', 'col'))  141 us
    pallas_call x2, Pallas kernels, experts_back(): pl.pallas_call(functools.partial(experts_back_kernel, ncol, nrow, with_gr...  105 us
    pallas_call x2, Pallas kernels, experts(): pl.pallas_call(functools.partial(experts_kernel, ncol, nrow), grid=(local...  84.3 us
    ppermute x104, starting transfers between devices, shift(): return lax.ppermute(value, axis, pairs)  65.7 us
    pallas_call x2, Pallas kernels, attend_back(): pl.pallas_call(attend_back_kernel, grid=(micro, groups), in_specs=[mine,...  63.1 us
    all_gather x1, waiting for transfers between devices, small_weights(): whole = lax.all_gather(packed, ('row', 'col'), axis=0)  54.1 us
    unnamed x159, local copies, waits for them, and re-layouts  41.4 us
  transfers between devices with their start and end apart: 112, of which 49 were waited for; matrix products, arithmetic and copies ran while one was open for 13% of the time, Pallas kernels for 2%

profile of v2, /device:TPU:0, one launch (start us, length us, event | category | flops | bytes accessed | tf_op | source)
XLA Modules:
  0.0 1763.4 jit_solution(17020169866470958429)
XLA Ops:
  32.4 54.1 %all-gather.6.cloned.1.call-done = bf16[4096,512]{1,0:T(8,128)(2,1)} async-done(((bf16[256,512]{1,0:T(8,128)(2,1)}), bf16[4096,512]{1,0:T(8,128)(2,1)}) %all-gather.6.cloned.1.call-update) | async-done | bytes 4194320 | tf_op jit(solution)/shard_map/all_gather | solution.py:670
  110.7 9.0 shard_map.229
  124.5 76.0 %collective-permute-done.3 = bf16[2,64,1024]{2,1,0:T(8,128)(2,1)S(1)} collective-permute-done((bf16[2,64,1024]{2,1,0:T(8,128)(2,1)S(1)}, bf16[2,64,1024]{2,1,0:T(8,128)(2,1)S(1)}, u32[]{:S(2)}, u32[]{:S(2)}) %collective-permute-start.3) | collective-permute-done | bytes 262176 | tf_op jit(solution)/shard_map/ppermute | solution.py:25
  224.0 123.7 %collective-permute-done.7 = bf16[2,64,1024]{2,1,0:T(8,128)(2,1)} collective-permute-done((bf16[2,64,1024]{2,1,0:T(8,128)(2,1)S(1)}, bf16[2,64,1024]{2,1,0:T(8,128)(2,1)}, u32[]{:S(2)}, u32[]{:S(2)}) %collective-permute-start.7) | collective-permute-done | bytes 262176 | tf_op jit(solution)/shard_map/ppermute | solution.py:25
  374.3 19.1 %shard_map.230 = (f32[2,192,1024]{2,1,0:T(8,128)}, f32[2,4,1,768]{3,2,1,0:T(1,128)}) custom-call(bf16[2,192,2048]{2,1,0:T(8,128)(2,1)} %bitcast.253, bf16[2,1536,1024]{2,1,0:T(8,128)(2,1)} %constant_dynamic-update-slice_fusion.k_ref.v_ref, bf16[2,1536,1024]{2,1,0:T(8,128)(2,1)} %constant_dynamic-update-slice_fusion.k_ref.v_ref, ...), custom_call_target="tpu_custom_call" | custom-call | flops 4831838208 | bytes 11010048 | tf_op jit(solution)/shard_map/pallas_call | solution.py:191
  402.2 16.8 collective-permute-done.16.refs_2_
  420.7 43.1 %collective-permute-done.23.refs_11_ = bf16[8,256,512]{2,1,0:T(8,128)(2,1)} collective-permute-done((bf16[8,256,512]{2,1,0:T(8,128)(2,1)}, bf16[8,256,512]{2,1,0:T(8,128)(2,1)}, u32[]{:S(2)}, u32[]{:S(2)}) %collective-permute-start.23) | collective-permute-done | bytes 2097184 | tf_op jit(solution)/shard_map/ppermute | solution.py:25
  463.8 44.6 %collective-permute-done.26.refs_15_ = bf16[8,512,256]{2,1,0:T(8,128)(2,1)} collective-permute-done((bf16[8,512,256]{2,1,0:T(8,128)(2,1)}, bf16[8,512,256]{2,1,0:T(8,128)(2,1)}, u32[]{:S(2)}, u32[]{:S(2)}) %collective-permute-start.26) | collective-permute-done | bytes 2097184 | tf_op jit(solution)/shard_map/ppermute | solution.py:25
  508.3 42.3 %shard_map.231 = (bf16[4,2,192,1024]{3,2,1,0:T(8,128)(2,1)}, bf16[8,2,384,1024]{3,2,1,0:T(8,128)(2,1)}, bf16[8,2,384,1024]{3,2,1,0:T(8,128)(2,1)}) custom-call(s32[20]{0:T(128)} %pad_add_fusion.1.meta_ref, s32[8,2,768]{2,1,0:T(2,128)} %add_select_fusion.place_ref, f32[8,2,768]{2,1,0:T(2,128)} %fusion.41.weight_ref, bf16[2,192,1024]{2,1,0:T(8,128)(2,1)} %bitcast.39.refs_0_, ...), custom_call_target="tpu_custom_call" | custom-call | flops 25769803776 | bytes 50331648 | tf_op jit(solution)/shard_map/pallas_call | solution.py:387
  558.1 19.1 %collective-permute-done.29 = bf16[2,192,1024]{2,1,0:T(8,128)(2,1)S(1)} collective-permute-done((bf16[2,192,1024]{2,1,0:T(8,128)(2,1)S(1)}, bf16[2,192,1024]{2,1,0:T(8,128)(2,1)S(1)}, u32[]{:S(2)}, u32[]{:S(2)}) %collective-permute-start.29) | collective-permute-done | bytes 786464 | tf_op jit(solution)/shard_map/ppermute | solution.py:25
  582.6 16.2 collective-permute-done.30
  612.7 10.5 collective-permute-done.34
  661.0 19.1 %shard_map.233 = (f32[2,192,1024]{2,1,0:T(8,128)}, f32[2,4,1,768]{3,2,1,0:T(1,128)}) custom-call(bf16[2,192,2048]{2,1,0:T(8,128)(2,1)} %bitcast.248, bf16[2,1536,1024]{2,1,0:T(8,128)(2,1)} %constant_dynamic-update-slice_fusion.16.k_ref.v_ref, bf16[2,1536,1024]{2,1,0:T(8,128)(2,1)} %constant_dynamic-update-slice_fusion.16.k_ref.v_ref, ...), custom_call_target="tpu_custom_call" | custom-call | flops 4831838208 | bytes 11010048 | tf_op jit(solution)/shard_map/pallas_call | solution.py:191
  687.8 18.2 %collective-permute-done.47.refs_2_ = bf16[2,192,1024]{2,1,0:T(8,128)(2,1)S(1)} collective-permute-done((bf16[2,192,1024]{2,1,0:T(8,128)(2,1)S(1)}, bf16[2,192,1024]{2,1,0:T(8,128)(2,1)S(1)}, u32[]{:S(2)}, u32[]{:S(2)}) %collective-permute-start.47) | collective-permute-done | bytes 786464 | tf_op jit(solution)/shard_map/ppermute | solution.py:25
  708.5 42.0 %shard_map.234 = (bf16[4,2,192,1024]{3,2,1,0:T(8,128)(2,1)}, bf16[8,2,384,1024]{3,2,1,0:T(8,128)(2,1)}, bf16[8,2,384,1024]{3,2,1,0:T(8,128)(2,1)}) custom-call(s32[20]{0:T(128)} %pad_add_fusion.1.meta_ref, s32[8,2,768]{2,1,0:T(2,128)} %add_select_fusion.place_ref, f32[8,2,768]{2,1,0:T(2,128)} %fusion.41.weight_ref, bf16[2,192,1024]{2,1,0:T(8,128)(2,1)} %bitcast.290, ...), custom_call_target="tpu_custom_call" | custom-call | flops 25769803776 | bytes 50331648 | tf_op jit(solution)/shard_map/pallas_call | solution.py:387
  780.2 10.0 collective-permute-done.51
  795.6 18.2 %collective-permute-done.53.refs_2_ = bf16[2,192,1024]{2,1,0:T(8,128)(2,1)S(1)} collective-permute-done((bf16[2,192,1024]{2,1,0:T(8,128)(2,1)S(1)}, bf16[2,192,1024]{2,1,0:T(8,128)(2,1)S(1)}, u32[]{:S(2)}, u32[]{:S(2)}) %collective-permute-start.53) | collective-permute-done | bytes 786464 | tf_op jit(solution)/shard_map/ppermute | solution.py:25
  817.0 44.8 %shard_map.235 = bf16[4,2,192,1024]{3,2,1,0:T(8,128)(2,1)} custom-call(s32[20]{0:T(128)} %pad_add_fusion.1.meta_ref, s32[8,2,768]{2,1,0:T(2,128)} %add_select_fusion.place_ref, f32[8,2,768]{2,1,0:T(2,128)} %fusion.41.weight_ref, bf16[2,192,1024]{2,1,0:T(8,128)(2,1)} %copy-done.43, bf16[2,192,1024]{2,1,0:T(8,128)(2,1)} %copy-done.61, ...), custom_call_target="tpu_custom_call" | custom-call | flops 38654705664 | bytes 75497472 | tf_op jit(solution)/shard_map/pallas_call | solution.py:499
  876.4 12.9 collective-permute-done.57
  893.5 31.5 %shard_map.236 = (bf16[2,192,1024]{2,1,0:T(8,128)(2,1)}, bf16[2,1536,1024]{2,1,0:T(8,128)(2,1)}) custom-call(bf16[2,192,2048]{2,1,0:T(8,128)(2,1)} %bitcast.249, bf16[2,1536,1024]{2,1,0:T(8,128)(2,1)} %constant_dynamic-update-slice_fusion.16.k_ref.v_ref, bf16[2,1536,1024]{2,1,0:T(8,128)(2,1)} %constant_dynamic-update-slice_fusion.16.k_ref.v_ref, ...), custom_call_target="tpu_custom_call" | custom-call | flops 12079595520 | bytes 17301504 | tf_op jit(solution)/shard_map/pallas_call | solution.py:246
  979.3 19.1 %collective-permute-done.73 = bf16[2,192,1024]{2,1,0:T(8,128)(2,1)S(1)} collective-permute-done((bf16[2,192,1024]{2,1,0:T(8,128)(2,1)S(1)}, bf16[2,192,1024]{2,1,0:T(8,128)(2,1)S(1)}, u32[]{:S(2)}, u32[]{:S(2)}) %collective-permute-start.73) | collective-permute-done | bytes 786464 | tf_op jit(solution)/shard_map/ppermute | solution.py:25
  1000.9 16.7 collective-permute-done.75.refs_2_
  1020.0 60.5 %shard_map.237 = (bf16[4,2,192,1024]{3,2,1,0:T(8,128)(2,1)}, bf16[8,256,512]{2,1,0:T(8,128)(2,1)}, bf16[8,256,512]{2,1,0:T(8,128)(2,1)}, bf16[8,256,512]{2,1,0:T...) custom-call(s32[20]{0:T(128)} %pad_add_fusion.1.meta_ref, ...), custom_call_target="tpu_custom_call" | custom-call | flops 38654705664 | bytes 75497472 | tf_op jit(solution)/shard_map/pallas_call | solution.py:499
  1090.2 19.1 %collective-permute-done.79 = bf16[2,192,1024]{2,1,0:T(8,128)(2,1)S(1)} collective-permute-done((bf16[2,192,1024]{2,1,0:T(8,128)(2,1)S(1)}, bf16[2,192,1024]{2,1,0:T(8,128)(2,1)S(1)}, u32[]{:S(2)}, u32[]{:S(2)}) %collective-permute-start.79) | collective-permute-done | bytes 786464 | tf_op jit(solution)/shard_map/ppermute | solution.py:25
  1114.6 31.6 %shard_map.238 = (bf16[2,192,1024]{2,1,0:T(8,128)(2,1)}, bf16[2,1536,1024]{2,1,0:T(8,128)(2,1)}) custom-call(bf16[2,192,2048]{2,1,0:T(8,128)(2,1)} %bitcast.250, bf16[2,1536,1024]{2,1,0:T(8,128)(2,1)} %constant_dynamic-update-slice_fusion.16.k_ref.v_ref, bf16[2,1536,1024]{2,1,0:T(8,128)(2,1)} %constant_dynamic-update-slice_fusion.16.k_ref.v_ref, ...), custom_call_target="tpu_custom_call" | custom-call | flops 12079595520 | bytes 17301504 | tf_op jit(solution)/shard_map/pallas_call | solution.py:246
  1194.6 143.9 %collective-permute-done.91 = bf16[2,64,1024]{2,1,0:T(8,128)(2,1)S(1)} collective-permute-done((bf16[2,64,1024]{2,1,0:T(8,128)(2,1)S(1)}, bf16[2,64,1024]{2,1,0:T(8,128)(2,1)S(1)}, u32[]{:S(2)}, u32[]{:S(2)}) %collective-permute-start.91) | collective-permute-done | bytes 262176 | tf_op jit(solution)/shard_map/ppermute | solution.py:25
  1366.7 9.7 pad_maximum_fusion.1
  1414.2 42.5 %collective-permute-done.96 = bf16[8,256,512]{2,1,0:T(8,128)(2,1)} collective-permute-done((bf16[8,256,512]{2,1,0:T(8,128)(2,1)}, bf16[8,256,512]{2,1,0:T(8,128)(2,1)}, u32[]{:S(2)}, u32[]{:S(2)}) %collective-permute-start.96) | collective-permute-done | bytes 2097184 | tf_op jit(solution)/shard_map/ppermute | solution.py:25
  1460.4 41.3 %collective-permute-done.99 = bf16[8,256,512]{2,1,0:T(8,128)(2,1)} collective-permute-done((bf16[8,256,512]{2,1,0:T(8,128)(2,1)}, bf16[8,256,512]{2,1,0:T(8,128)(2,1)}, u32[]{:S(2)}, u32[]{:S(2)}) %collective-permute-start.99) | collective-permute-done | bytes 2097184 | tf_op jit(solution)/shard_map/ppermute | solution.py:25
  1505.4 41.3 %collective-permute-done.102 = bf16[8,512,256]{2,1,0:T(8,128)(2,1)} collective-permute-done((bf16[8,512,256]{2,1,0:T(8,128)(2,1)}, bf16[8,512,256]{2,1,0:T(8,128)(2,1)}, u32[]{:S(2)}, u32[]{:S(2)}) %collective-permute-start.102) | collective-permute-done | bytes 2097184 | tf_op jit(solution)/shard_map/ppermute | solution.py:25
  1556.9 140.5 %psum.14 = f32[]{:T(128)} all-reduce(f32[]{:T(128)S(6)} %select_n.108), channel_id=1, replica_groups=mesh['section'=2,'row'=4,'col'=4] {'section','row','col'}, use_global_device_ids=true, to_apply=%region_6.7 | all-reduce | flops 1 | bytes 8 | tf_op jit(solution)/shard_map/psum | solution.py:821
  1702.6 32.8 %psum.15 = f32[2,1024]{1,0:T(2,128)S(1)} all-reduce(f32[2,1024]{1,0:T(2,128)S(1)} %pad_maximum_fusion.10), channel_id=1, replica_groups=mesh['section'=2,'row'=4,'col'=4] {'row','col'}, use_global_device_ids=true, to_apply=%region_16.17 | all-reduce | flops 2048 | bytes 16384 | tf_op jit(solution)/shard_map/psum | solution.py:819
  (559 shorter events, 476.2 us)
Async XLA Ops:
  7.2 79.4 %all-gather.6.cloned.1.call-start = ((), (), s32[]{:S(2)}) async-start(), calls=%async_computation.9 | async-start | bytes 4456448 | tf_op jit(solution)/shard_map/all_gather | solution.py:670
  16.3 197.6 %all-gather.4.cloned.1.call-start = ((), (), s32[]{:S(2)}) async-start(), calls=%async_computation.6 | async-start | bytes 2228224 | tf_op jit(solution)/shard_map/all_gather | solution.py:679
  16.3 184.3 %collective-permute-start.18 = (bf16[8,256,512]{2,1,0:T(8,128)(2,1)}, bf16[8,256,512]{2,1,0:T(8,128)(2,1)}, u32[]{:S(2)}, u32[]{:S(2)}) collective-permute-start(bf16[8,256,512]{2,1,0:T(8,128)(2,1)} %bitcast.40.refs_4_), channel_id=1, source_target_pairs={{0,4},{4,8},{8,12},{12,0},{1,5},{5,9},{9,13},{13,1},{2,6},{6,10},{... | collective-permute-start | bytes 6291464 | tf_op jit(solution)/shard_map/ppermute | solution.py:25
  18.7 183.5 %collective-permute-start.21 = (bf16[8,256,512]{2,1,0:T(8,128)(2,1)}, bf16[8,256,512]{2,1,0:T(8,128)(2,1)}, u32[]{:S(2)}, u32[]{:S(2)}) collective-permute-start(bf16[8,256,512]{2,1,0:T(8,128)(2,1)} %bitcast.41.refs_8_), channel_id=1, source_target_pairs={{0,4},{4,8},{8,12},{12,0},{1,5},{5,9},{9,13},{13,1},{2,6},{6,10},{... | collective-permute-start | bytes 6291464 | tf_op jit(solution)/shard_map/ppermute | solution.py:25
  20.2 182.0 %collective-permute-start.24 = (bf16[8,512,256]{2,1,0:T(8,128)(2,1)}, bf16[8,512,256]{2,1,0:T(8,128)(2,1)}, u32[]{:S(2)}, u32[]{:S(2)}) collective-permute-start(bf16[8,512,256]{2,1,0:T(8,128)(2,1)} %bitcast.42.refs_12_), channel_id=1, source_target_pairs={{0,4},{4,8},{8,12},{12,0},{1,5},{5,9},{9,13},{13,1},{2,6},{6,10},{... | collective-permute-start | bytes 6291464 | tf_op jit(solution)/shard_map/ppermute | solution.py:25
  123.0 86.6 %collective-permute-start.1 = (bf16[2,192,1024]{2,1,0:T(8,128)(2,1)S(1)}, bf16[2,192,1024]{2,1,0:T(8,128)(2,1)}, u32[]{:S(2)}, u32[]{:S(2)}) collective-permute-start(bf16[2,192,1024]{2,1,0:T(8,128)(2,1)S(1)} %get-tuple-element.119), channel_id=1, source_target_pairs={{0,2},{1,3},{2,0},{3,1},{4,6},{5,7},{6,4},{7,5},{8,10},{9,11},{10,... | collective-permute-start | bytes 2359304 | tf_op jit(solution)/shard_map/ppermute | solution.py:25
  124.4 76.1 %collective-permute-start.3 = (bf16[2,64,1024]{2,1,0:T(8,128)(2,1)S(1)}, bf16[2,64,1024]{2,1,0:T(8,128)(2,1)S(1)}, u32[]{:S(2)}, u32[]{:S(2)}) collective-permute-start(bf16[2,64,1024]{2,1,0:T(8,128)(2,1)S(1)} %slice.336), channel_id=1, source_target_pairs={{0,4},{4,8},{8,12},{12,0},{1,5},{5,9},{9,13},{13,1},{2,6},{6,10},{... | collective-permute-start | bytes 786440 | tf_op jit(solution)/shard_map/ppermute | solution.py:25
  202.2 165.3 %collective-permute-start.19 = (bf16[8,256,512]{2,1,0:T(8,128)(2,1)}, bf16[8,256,512]{2,1,0:T(8,128)(2,1)}, u32[]{:S(2)}, u32[]{:S(2)}) collective-permute-start(bf16[8,256,512]{2,1,0:T(8,128)(2,1)} %collective-permute-done.18.refs_5_), channel_id=1, source_target_pairs={{0,4},{4,8},{8,12},{12,0},{1,5},{5,9},{9,13},{13,1},{2,6},{6,10},{... | collective-permute-start | bytes 6291464 | tf_op jit(solution)/shard_map/ppermute | solution.py:25
  202.6 165.7 %collective-permute-start.22 = (bf16[8,256,512]{2,1,0:T(8,128)(2,1)}, bf16[8,256,512]{2,1,0:T(8,128)(2,1)}, u32[]{:S(2)}, u32[]{:S(2)}) collective-permute-start(bf16[8,256,512]{2,1,0:T(8,128)(2,1)} %collective-permute-done.21.refs_9_), channel_id=1, source_target_pairs={{0,4},{4,8},{8,12},{12,0},{1,5},{5,9},{9,13},{13,1},{2,6},{6,10},{... | collective-permute-start | bytes 6291464 | tf_op jit(solution)/shard_map/ppermute | solution.py:25
  209.2 159.0 %collective-permute-start.25 = (bf16[8,512,256]{2,1,0:T(8,128)(2,1)}, bf16[8,512,256]{2,1,0:T(8,128)(2,1)}, u32[]{:S(2)}, u32[]{:S(2)}) collective-permute-start(bf16[8,512,256]{2,1,0:T(8,128)(2,1)} %collective-permute-done.24.refs_13_), channel_id=1, source_target_pairs={{0,4},{4,8},{8,12},{12,0},{1,5},{5,9},{9,13},{13,1},{2,6},{6,10},{... | collective-permute-start | bytes 6291464 | tf_op jit(solution)/shard_map/ppermute | solution.py:25
  209.6 138.1 %collective-permute-start.2 = (bf16[2,192,1024]{2,1,0:T(8,128)(2,1)}, bf16[2,192,1024]{2,1,0:T(8,128)(2,1)}, u32[]{:S(2)}, u32[]{:S(2)}) collective-permute-start(bf16[2,192,1024]{2,1,0:T(8,128)(2,1)} %collective-permute-done.1), channel_id=1, source_target_pairs={{0,1},{1,0},{2,3},{3,2},{4,5},{5,4},{6,7},{7,6},{8,9},{9,8},{10,11... | collective-permute-start | bytes 2359304 | tf_op jit(solution)/shard_map/ppermute | solution.py:25
  212.2 135.4 %collective-permute-start.7 = (bf16[2,64,1024]{2,1,0:T(8,128)(2,1)S(1)}, bf16[2,64,1024]{2,1,0:T(8,128)(2,1)}, u32[]{:S(2)}, u32[]{:S(2)}) collective-permute-start(bf16[2,64,1024]{2,1,0:T(8,128)(2,1)S(1)} %collective-permute-done.3), channel_id=1, source_target_pairs={{0,4},{4,8},{8,12},{12,0},{1,5},{5,9},{9,13},{13,1},{2,6},{6,10},{... | collective-permute-start | bytes 786440 | tf_op jit(solution)/shard_map/ppermute | solution.py:25
  368.3 52.4 %collective-permute-start.20 = (bf16[8,256,512]{2,1,0:T(8,128)(2,1)}, bf16[8,256,512]{2,1,0:T(8,128)(2,1)}, u32[]{:S(2)}, u32[]{:S(2)}) collective-permute-start(bf16[8,256,512]{2,1,0:T(8,128)(2,1)} %collective-permute-done.19.refs_6_), channel_id=1, source_target_pairs={{0,4},{4,8},{8,12},{12,0},{1,5},{5,9},{9,13},{13,1},{2,6},{6,10},{... | collective-permute-start | bytes 6291464 | tf_op jit(solution)/shard_map/ppermute | solution.py:25
  368.3 95.5 %collective-permute-start.23 = (bf16[8,256,512]{2,1,0:T(8,128)(2,1)}, bf16[8,256,512]{2,1,0:T(8,128)(2,1)}, u32[]{:S(2)}, u32[]{:S(2)}) collective-permute-start(bf16[8,256,512]{2,1,0:T(8,128)(2,1)} %collective-permute-done.22.refs_10_), channel_id=1, source_target_pairs={{0,4},{4,8},{8,12},{12,0},{1,5},{5,9},{9,13},{13,1},{2,6},{6,10},{... | collective-permute-start | bytes 6291464 | tf_op jit(solution)/shard_map/ppermute | solution.py:25
  368.4 140.0 %collective-permute-start.26 = (bf16[8,512,256]{2,1,0:T(8,128)(2,1)}, bf16[8,512,256]{2,1,0:T(8,128)(2,1)}, u32[]{:S(2)}, u32[]{:S(2)}) collective-permute-start(bf16[8,512,256]{2,1,0:T(8,128)(2,1)} %collective-permute-done.25.refs_14_), channel_id=1, source_target_pairs={{0,4},{4,8},{8,12},{12,0},{1,5},{5,9},{9,13},{13,1},{2,6},{6,10},{... | collective-permute-start | bytes 6291464 | tf_op jit(solution)/shard_map/ppermute | solution.py:25
  402.0 106.3 %collective-permute-start.15 = (bf16[2,192,1024]{2,1,0:T(8,128)(2,1)}, bf16[2,192,1024]{2,1,0:T(8,128)(2,1)}, u32[]{:S(2)}, u32[]{:S(2)}) collective-permute-start(bf16[2,192,1024]{2,1,0:T(8,128)(2,1)} %bitcast.39.refs_0_), channel_id=1, source_target_pairs={{0,1},{1,0},{2,3},{3,2},{4,5},{5,4},{6,7},{7,6},{8,9},{9,8},{10,11... | collective-permute-start | bytes 2359304 | tf_op jit(solution)/shard_map/ppermute | solution.py:25
  419.0 89.3 %collective-permute-start.17 = (bf16[2,192,1024]{2,1,0:T(8,128)(2,1)}, bf16[2,192,1024]{2,1,0:T(8,128)(2,1)}, u32[]{:S(2)}, u32[]{:S(2)}) collective-permute-start(bf16[2,192,1024]{2,1,0:T(8,128)(2,1)} %collective-permute-done.16.refs_2_), channel_id=1, source_target_pairs={{0,1},{1,0},{2,3},{3,2},{4,5},{5,4},{6,7},{7,6},{8,9},{9,8},{10,11... | collective-permute-start | bytes 2359304 | tf_op jit(solution)/shard_map/ppermute | solution.py:25
  761.7 977.2 %reduce-scatter.5.cloned.1.call-start = ((), (), s32[]{:S(2)}) async-start(), calls=%async_computation.8 | async-start | bytes 2228224 | tf_op jit(solution)/shard_map/reduce_scatter | solution.py:700
  1153.6 35.0 %collective-permute-start.92 = (bf16[2,192,1024]{2,1,0:T(8,128)(2,1)}, bf16[2,192,1024]{2,1,0:T(8,128)(2,1)}, u32[]{:S(2)}, u32[]{:S(2)}) collective-permute-start(bf16[2,192,1024]{2,1,0:T(8,128)(2,1)} %get-tuple-element.88), channel_id=1, source_target_pairs={{0,1},{1,0},{2,3},{3,2},{4,5},{5,4},{6,7},{7,6},{8,9},{9,8},{10,11... | collective-permute-start | bytes 2359304 | tf_op jit(solution)/shard_map/ppermute | solution.py:25
  1182.5 571.5 %reduce-scatter.3.cloned.1.call-start = ((), (), s32[]{:S(2)}) async-start(), calls=%async_computation.7 | async-start | bytes 4456448 | tf_op jit(solution)/shard_map/reduce_scatter | solution.py:696
  1182.5 201.3 %collective-permute-start.95 = (bf16[8,256,512]{2,1,0:T(8,128)(2,1)}, bf16[8,256,512]{2,1,0:T(8,128)(2,1)}, u32[]{:S(2)}, u32[]{:S(2)}) collective-permute-start(bf16[8,256,512]{2,1,0:T(8,128)(2,1)} %get-tuple-element.54), channel_id=1, source_target_pairs={{0,4},{4,8},{8,12},{12,0},{1,5},{5,9},{9,13},{13,1},{2,6},{6,10},{... | collective-permute-start | bytes 6291464 | tf_op jit(solution)/shard_map/ppermute | solution.py:25
  1182.7 206.4 %collective-permute-start.98 = (bf16[8,256,512]{2,1,0:T(8,128)(2,1)}, bf16[8,256,512]{2,1,0:T(8,128)(2,1)}, u32[]{:S(2)}, u32[]{:S(2)}) collective-permute-start(bf16[8,256,512]{2,1,0:T(8,128)(2,1)} %get-tuple-element.58), channel_id=1, source_target_pairs={{0,4},{4,8},{8,12},{12,0},{1,5},{5,9},{9,13},{13,1},{2,6},{6,10},{... | collective-permute-start | bytes 6291464 | tf_op jit(solution)/shard_map/ppermute | solution.py:25
  1185.1 208.1 %collective-permute-start.101 = (bf16[8,512,256]{2,1,0:T(8,128)(2,1)}, bf16[8,512,256]{2,1,0:T(8,128)(2,1)}, u32[]{:S(2)}, u32[]{:S(2)}) collective-permute-start(bf16[8,512,256]{2,1,0:T(8,128)(2,1)} %get-tuple-element.62), channel_id=1, source_target_pairs={{0,4},{4,8},{8,12},{12,0},{1,5},{5,9},{9,13},{13,1},{2,6},{6,10},{... | collective-permute-start | bytes 6291464 | tf_op jit(solution)/shard_map/ppermute | solution.py:25
  1188.7 149.9 %collective-permute-start.91 = (bf16[2,64,1024]{2,1,0:T(8,128)(2,1)S(1)}, bf16[2,64,1024]{2,1,0:T(8,128)(2,1)S(1)}, u32[]{:S(2)}, u32[]{:S(2)}) collective-permute-start(bf16[2,64,1024]{2,1,0:T(8,128)(2,1)S(1)} %add_convert_fusion.11), channel_id=1, source_target_pairs={{0,4},{4,8},{8,12},{12,0},{1,5},{5,9},{9,13},{13,1},{2,6},{6,10},{... | collective-permute-start | bytes 786440 | tf_op jit(solution)/shard_map/ppermute | solution.py:25
  1389.1 67.7 %collective-permute-start.96 = (bf16[8,256,512]{2,1,0:T(8,128)(2,1)}, bf16[8,256,512]{2,1,0:T(8,128)(2,1)}, u32[]{:S(2)}, u32[]{:S(2)}) collective-permute-start(bf16[8,256,512]{2,1,0:T(8,128)(2,1)} %add_convert_fusion.5), channel_id=1, source_target_pairs={{0,4},{4,8},{8,12},{12,0},{1,5},{5,9},{9,13},{13,1},{2,6},{6,10},{... | collective-permute-start | bytes 6291464 | tf_op jit(solution)/shard_map/ppermute | solution.py:25
  1392.9 108.8 %collective-permute-start.99 = (bf16[8,256,512]{2,1,0:T(8,128)(2,1)}, bf16[8,256,512]{2,1,0:T(8,128)(2,1)}, u32[]{:S(2)}, u32[]{:S(2)}) collective-permute-start(bf16[8,256,512]{2,1,0:T(8,128)(2,1)} %add_convert_fusion.3), channel_id=1, source_target_pairs={{0,4},{4,8},{8,12},{12,0},{1,5},{5,9},{9,13},{13,1},{2,6},{6,10},{... | collective-permute-start | bytes 6291464 | tf_op jit(solution)/shard_map/ppermute | solution.py:25
  1397.0 149.6 %collective-permute-start.102 = (bf16[8,512,256]{2,1,0:T(8,128)(2,1)}, bf16[8,512,256]{2,1,0:T(8,128)(2,1)}, u32[]{:S(2)}, u32[]{:S(2)}) collective-permute-start(bf16[8,512,256]{2,1,0:T(8,128)(2,1)} %add_convert_fusion.1), channel_id=1, source_target_pairs={{0,4},{4,8},{8,12},{12,0},{1,5},{5,9},{9,13},{13,1},{2,6},{6,10},{... | collective-permute-start | bytes 6291464 | tf_op jit(solution)/shard_map/ppermute | solution.py:25
  1405.3 147.4 %all-to-all-start.1 = ((bf16[2,1,192,1024]{2,0,1,3:T(2,128)(2,1)}), bf16[2,1,192,1024]{2,0,1,3:T(2,128)(2,1)}, u32[]{:S(2)}, u32[]{:S(2)}) async-start(bf16[2,1,192,1024]{2,0,1,3:T(2,128)(2,1)} %copy.188), calls=%async_computation.1 | async-start | bytes 2097152 | tf_op jit(solution)/shard_map/all_to_all | solution.py:644
  1460.4 280.1 %collective-permute-start.97 = (bf16[8,256,512]{2,1,0:T(8,128)(2,1)}, bf16[8,256,512]{2,1,0:T(8,128)(2,1)}, u32[]{:S(2)}, u32[]{:S(2)}) collective-permute-start(bf16[8,256,512]{2,1,0:T(8,128)(2,1)} %add_convert_fusion.4), channel_id=1, source_target_pairs={{0,4},{4,8},{8,12},{12,0},{1,5},{5,9},{9,13},{13,1},{2,6},{6,10},{... | collective-permute-start | bytes 6291464 | tf_op jit(solution)/shard_map/ppermute | solution.py:25
  1505.3 240.2 %collective-permute-start.100 = (bf16[8,256,512]{2,1,0:T(8,128)(2,1)}, bf16[8,256,512]{2,1,0:T(8,128)(2,1)}, u32[]{:S(2)}, u32[]{:S(2)}) collective-permute-start(bf16[8,256,512]{2,1,0:T(8,128)(2,1)} %add_convert_fusion.2), channel_id=1, source_target_pairs={{0,4},{4,8},{8,12},{12,0},{1,5},{5,9},{9,13},{13,1},{2,6},{6,10},{... | collective-permute-start | bytes 6291464 | tf_op jit(solution)/shard_map/ppermute | solution.py:25
  1550.2 199.6 %collective-permute-start.103 = (bf16[8,512,256]{2,1,0:T(8,128)(2,1)}, bf16[8,512,256]{2,1,0:T(8,128)(2,1)}, u32[]{:S(2)}, u32[]{:S(2)}) collective-permute-start(bf16[8,512,256]{2,1,0:T(8,128)(2,1)} %add_convert_fusion), channel_id=1, source_target_pairs={{0,4},{4,8},{8,12},{12,0},{1,5},{5,9},{9,13},{13,1},{2,6},{6,10},{... | collective-permute-start | bytes 6291464 | tf_op jit(solution)/shard_map/ppermute | solution.py:25
  1552.7 183.3 %all-to-all-start.3 = ((bf16[2,1,192,1024]{2,0,1,3:T(2,128)(2,1)}), bf16[2,1,192,1024]{2,0,1,3:T(2,128)(2,1)S(1)}, u32[]{:S(2)}, u32[]{:S(2)}) async-start(bf16[2,1,192,1024]{2,0,1,3:T(2,128)(2,1)} %copy.194), calls=%async_computation.3 | async-start | bytes 2097152 | tf_op jit(solution)/shard_map/all_to_all | solution.py:644
  (144 other events, 1810.6 us)
Sparse Core Ops, SparseCore 0:
  10.7 75.7 all-gather.5
  88.7 48.5 all-gather.3
  1182.6 156.8 reduce-scatter.4
  1384.0 312.1 reduce-scatter.2

commit v3 on v2

v3 whole, which is shorter than its diff:
```python
import functools

import jax
import jax.numpy as jnp
from jax import lax
from jax.experimental import pallas as pl
from jax.experimental.pallas import tpu as pltpu
from jax.sharding import PartitionSpec as P

HEAD = 64
HIDDEN_SIZE = 512
CONT_LEN = 512
CAP = 384
GROUP = 4

EPS = 1e-06
THETA = 10000.0
NEG = -1e30
BF16 = jnp.bfloat16
F32 = jnp.float32
VMEM_LIMIT = 60 * 1024 * 1024


def shift(value, axis, pairs):
    return lax.ppermute(value, axis, pairs)


def flip(value, bit):
    count = lax.axis_size("col")
    return shift(value, "col", [(i, i ^ bit) for i in range(count)])


def col_bits():
    count = lax.axis_size("col")
    bits = [1]
    while bits[-1] * 2 < count:
        bits.append(bits[-1] * 2)
    return bits


def gather_col(value):
    blocks = {0: value}
    for bit in reversed(col_bits()):
        for k in list(blocks):
            blocks[k ^ bit] = flip(blocks[k], bit)
    return [blocks[k] for k in range(lax.axis_size("col"))]


def scatter_col(blocks):
    blocks = dict(enumerate(blocks))
    total = None
    for bit in col_bits():
        keep = [k for k in blocks if not k & bit]
        total = {k: blocks[k].astype(F32) + flip(blocks[k ^ bit], bit).astype(F32) for k in keep}
        blocks = {k: total[k].astype(BF16) for k in keep}
    return total[0]


def exchange(value):
    return shift(value, "section", [(0, 1), (1, 0)])


def ring(value):
    count = lax.axis_size("row")
    return shift(value, "row", [(i, (i + 1) % count) for i in range(count)])


def gather_row(value):
    count = lax.axis_size("row")
    pieces = [value]
    for k in range(1, count):
        pieces.append(shift(value, "row", [(i, (i + k) % count) for i in range(count)]))
    return pieces


def scatter_row(parts):
    count = len(parts)
    total = parts[0].astype(F32)
    for k in range(1, count):
        pairs = [(i, (i - k) % count) for i in range(count)]
        total = total + shift(parts[k], "row", pairs).astype(F32)
    return total


def total_everywhere(value):
    for bit in col_bits():
        value = value + flip(value, bit)
    count, bit = lax.axis_size("row"), 1
    while bit < count:
        value = value + shift(value, "row", [(i, i ^ bit) for i in range(count)])
        bit *= 2
    return value + exchange(value)


def after(value, *others):
    return lax.optimization_barrier((value, *others))[0]


def dot_nn(left, right):
    return lax.dot_general(left, right, (((1,), (0,)), ((), ())), preferred_element_type=F32)


def dot_nt(left, right):
    return lax.dot_general(left, right, (((1,), (1,)), ((), ())), preferred_element_type=F32)


def dot_tn(left, right):
    return lax.dot_general(left, right, (((0,), (0,)), ((), ())), preferred_element_type=F32)


def swap_halves(value):
    lanes = value.shape[1]
    lane = lax.broadcasted_iota(jnp.int32, value.shape, 1)
    half = HEAD // 2
    ahead = pltpu.roll(value, lanes - half, 1)
    behind = pltpu.roll(value, half, 1)
    return jnp.where(lane % HEAD < half, ahead, behind)


def ordered(value, starts_ref, first, count, cut):
    picks = []
    for k in range(count):
        start = pl.multiple_of(starts_ref[first + k], cut)
        picks.append(value[:, pl.ds(start, cut)])
    return jnp.concatenate(picks, axis=1)


def flat(ref):
    return ref[...].reshape(ref.shape[0] * ref.shape[1], ref.shape[2])


def normalised(value):
    return lax.rsqrt(jnp.mean(value * value, axis=1, keepdims=True) + EPS)


def project_kernel(nblocks, starts_ref, x_ref, gain_ref, cos_ref, sin_ref, *refs):
    blocks, (n_ref, out_ref) = refs[:nblocks], refs[nblocks:]
    nrow, cut = blocks[0].shape[0], blocks[0].shape[1]
    width = x_ref.shape[1]
    x = x_ref[...].astype(F32)
    n_ref[...] = (x * normalised(x) * gain_ref[...]).astype(BF16)
    normed = ordered(n_ref, starts_ref, 0, nrow, cut)
    cos, sin = cos_ref[...], sin_ref[...]
    turn = lambda v: (v * cos + swap_halves(v) * sin).astype(BF16)
    for k, block in enumerate(blocks):
        raw = dot_nn(normed, flat(block))
        start = pl.multiple_of(starts_ref[nrow + k], 256)
        out_ref[:, pl.ds(start, 256)] = jnp.concatenate(
            [turn(raw[:, :128]), turn(raw[:, 128:256])], axis=1
        )
        start = pl.multiple_of(starts_ref[nrow + k] + width, 256)
        out_ref[:, pl.ds(start, 256)] = jnp.concatenate(
            [turn(raw[:, 256:384]), raw[:, 384:].astype(BF16)], axis=1
        )


def close_kernel(nblocks, starts_ref, x_ref, mixed_ref, gain_ref, *refs):
    blocks, (second_ref, n_ref, wide_ref) = refs[:nblocks], refs[nblocks:]
    nrow, cut = blocks[0].shape[0], blocks[0].shape[2]
    wide_ref[...] = mixed_ref[...].astype(BF16)
    mixed = ordered(wide_ref, starts_ref, nrow, nblocks, 256)
    for j in range(nrow):
        weight = jnp.concatenate([block[j] for block in blocks], axis=0)
        lanes = pl.ds(pl.multiple_of(starts_ref[j], cut), cut)
        second_ref[:, lanes] = x_ref[:, lanes].astype(F32) + dot_nn(mixed, weight)
    second = second_ref[...].astype(BF16).astype(F32)
    n_ref[...] = (second * normalised(second) * gain_ref[...]).astype(BF16)


def norm_back(grad, value, gain):
    rho = normalised(value)
    scaled = grad * gain
    inner = jnp.sum(scaled * value, axis=1, keepdims=True)
    out = rho * scaled - value * (rho * rho * rho) * (inner / value.shape[1])
    return out, jnp.sum(grad * value * rho, axis=0, keepdims=True)


def open_back_kernel(nblocks, starts_ref, grad_ref, dn_ref, second_ref, gain_ref, *refs):
    blocks, (dsecond_ref, dbranch_ref, dmixed_ref, dgain_ref) = refs[:nblocks], refs[nblocks:]
    nrow, cut = blocks[0].shape[0], blocks[0].shape[2]
    second = second_ref[...].astype(BF16).astype(F32)
    dnorm, dgain_ref[...] = norm_back(dn_ref[...], second, gain_ref[...])
    dsecond = grad_ref[...].astype(F32) + dnorm
    dsecond_ref[...] = dsecond
    dbranch_ref[...] = dsecond.astype(BF16)
    for k, block in enumerate(blocks):
        total = None
        for j in range(nrow):
            lanes = pl.ds(pl.multiple_of(starts_ref[j], cut), cut)
            term = dot_nt(dbranch_ref[:, lanes], block[j])
            total = term if total is None else total + term
        start = pl.multiple_of(starts_ref[nrow + k], 256)
        dmixed_ref[:, pl.ds(start, 256)] = total.astype(BF16)


def project_back_kernel(nblocks, starts_ref, dq_ref, dkv_ref, x_ref, gain_ref, dsecond_ref, *refs):
    blocks, (dx_ref, dgain_ref, wide_ref) = refs[:nblocks], refs[nblocks:]
    nrow, cut = blocks[0].shape[0], blocks[0].shape[1]
    total = None
    for k, block in enumerate(blocks):
        lanes = pl.ds(pl.multiple_of(starts_ref[nrow + k], 256), 256)
        grad = jnp.concatenate([dq_ref[:, lanes], dkv_ref[:, lanes]], axis=1)
        term = dot_nt(grad, flat(block))
        total = term if total is None else total + term
    for j in range(nrow):
        lanes = pl.ds(pl.multiple_of(starts_ref[j], cut), cut)
        wide_ref[:, lanes] = total[:, j * cut : (j + 1) * cut]
    dnorm, dgain_ref[...] = norm_back(wide_ref[...], x_ref[...].astype(F32), gain_ref[...])
    dx_ref[...] = (dsecond_ref[...] + dnorm).astype(BF16)


def weight_back_kernel(nblocks, starts_ref, n_ref, dq_ref, dkv_ref, mixed_ref, dbranch_ref, *refs):
    qkvs, outs = refs[:nblocks], refs[nblocks : 2 * nblocks]
    nrow, cut = qkvs[0].shape[0], qkvs[0].shape[1]
    normed = ordered(n_ref, starts_ref, 0, nrow, cut)
    for k in range(nblocks):
        lanes = pl.ds(pl.multiple_of(starts_ref[nrow + k], 256), 256)
        grad = jnp.concatenate([dq_ref[:, lanes], dkv_ref[:, lanes]], axis=1)
        qkvs[k][...] = dot_tn(normed, grad).astype(BF16).reshape(qkvs[k].shape)
        mixed = mixed_ref[:, lanes].astype(BF16)
        for j in range(nrow):
            there = pl.ds(pl.multiple_of(starts_ref[j], cut), cut)
            outs[k][j] = dot_tn(mixed, dbranch_ref[:, there]).astype(BF16)


def whole_call(kernel, out_shape, starts, operands, blocks, lanes, scratch=(), flops=0):
    start, count = lanes
    specs = [pl.BlockSpec(memory_space=pltpu.SMEM)]
    specs += [pl.BlockSpec(memory_space=pltpu.VMEM) for _ in operands]
    specs += [
        pl.BlockSpec((*b.shape[:2], count), lambda i: (0, 0, start // count)) for b in blocks
    ]
    specs[1 : 1 + len(operands)] = [
        pl.BlockSpec(o.shape, lambda i, n=o.ndim: (0,) * n) for o in operands
    ]
    return pl.pallas_call(
        functools.partial(kernel, len(blocks)),
        grid=(1,),
        in_specs=specs,
        out_specs=[pl.BlockSpec(o.shape, lambda i, n=len(o.shape): (0,) * n) for o in out_shape],
        out_shape=out_shape,
        scratch_shapes=scratch,
        compiler_params=pltpu.CompilerParams(vmem_limit_bytes=VMEM_LIMIT),
        cost_estimate=pl.CostEstimate(
            flops=flops,
            bytes_accessed=8 * 1024 * 1024,
            transcendentals=0,
        ),
    )(starts, *operands, *blocks)


def project(x, gain, cos, sin, part):
    rows, width = x.shape
    shapes = [
        jax.ShapeDtypeStruct((rows, width), BF16),
        jax.ShapeDtypeStruct((rows, 2 * width), BF16),
    ]
    return whole_call(
        project_kernel, shapes, part["starts"], (x, gain, cos, sin), part["qkv"], (0, 512),
        flops=4 * rows * width * width,
    )


def close_attention(x, mixed, gain, part):
    rows, width = x.shape
    shapes = [jax.ShapeDtypeStruct((rows, width), F32), jax.ShapeDtypeStruct((rows, width), BF16)]
    return whole_call(
        close_kernel, shapes, part["starts"], (x, mixed, gain), part["out"], part["out_lanes"],
        [pltpu.VMEM((rows, width), BF16)], 2 * rows * width * width,
    )


def open_back(grad, dn, second, gain, part):
    rows, width = grad.shape
    shapes = [
        jax.ShapeDtypeStruct((rows, width), F32),
        jax.ShapeDtypeStruct((rows, width), BF16),
        jax.ShapeDtypeStruct((rows, width), BF16),
        jax.ShapeDtypeStruct((1, width), F32),
    ]
    return whole_call(
        open_back_kernel, shapes, part["starts"], (grad, dn, second, gain), part["out"],
        part["out_lanes"], flops=2 * rows * width * width,
    )


def project_back(dq, dkv, x, gain, dsecond, part):
    rows, width = x.shape
    shapes = [jax.ShapeDtypeStruct((rows, width), BF16), jax.ShapeDtypeStruct((1, width), F32)]
    return whole_call(
        project_back_kernel, shapes, part["starts"], (dq, dkv, x, gain, dsecond), part["qkv"],
        (0, 512), [pltpu.VMEM((rows, width), F32)], 4 * rows * width * width,
    )


def weight_back(normed, dq, dkv, mixed, dbranch, part):
    rows, width = normed.shape
    nblocks = len(part["qkv"])
    nrow, cut = part["qkv"][0].shape[:2]
    shapes = [jax.ShapeDtypeStruct((nrow, cut, 512), BF16)] * nblocks
    shapes += [jax.ShapeDtypeStruct((nrow, 256, width // nrow), BF16)] * nblocks
    operands = (normed, dq, dkv, mixed, dbranch)
    grads = pl.pallas_call(
        functools.partial(weight_back_kernel, nblocks),
        in_specs=[pl.BlockSpec(memory_space=pltpu.SMEM)]
        + [pl.BlockSpec(memory_space=pltpu.VMEM)] * len(operands),
        out_specs=[pl.BlockSpec(memory_space=pltpu.VMEM)] * len(shapes),
        out_shape=shapes,
        compiler_params=pltpu.CompilerParams(vmem_limit_bytes=VMEM_LIMIT),
        cost_estimate=pl.CostEstimate(
            flops=6 * rows * width * width, bytes_accessed=8 * 1024 * 1024, transcendentals=0
        ),
    )(part["starts"], *operands)
    return grads[:nblocks], grads[nblocks:]


def stack_heads(value):
    low = (lax.broadcasted_iota(jnp.int32, (value.shape[0], 128), 1) < HEAD).astype(F32)
    first, second = value[:, :128].astype(F32), value[:, 128:].astype(F32)
    return jnp.concatenate(
        [first * low, second * low, first * (1.0 - low), second * (1.0 - low)], axis=0
    )


def unstack_heads(value):
    rows = value.shape[0] // 4
    low = lax.broadcasted_iota(jnp.int32, (rows, 128), 1) < HEAD
    first = jnp.where(low, value[:rows], value[2 * rows : 3 * rows])
    second = jnp.where(low, value[rows : 2 * rows], value[3 * rows :])
    return first, second


def attend_kernel(q_ref, k_ref, v_ref, bias_ref, o_ref, lse_ref):
    stacked = (stack_heads(q_ref[0]) * HEAD**-0.5).astype(BF16)
    scores = dot_nt(k_ref[0], stacked) + bias_ref[...]
    top = jnp.max(scores, axis=0, keepdims=True)
    weights = jnp.exp(scores - top)
    total = jnp.sum(weights, axis=0, keepdims=True)
    mixed = dot_tn(v_ref[0], weights.astype(BF16)) / total
    first, second = unstack_heads(mixed.T)
    o_ref[0, :, :128] = first
    o_ref[0, :, 128:] = second
    lse_ref[0, 0] = top + jnp.log(total)


def attend(qkv, kv, bias):
    micro, rows, _ = qkv.shape
    keys, width = kv.shape[1], kv.shape[2]
    groups = width // 256
    return pl.pallas_call(
        attend_kernel,
        grid=(micro, groups),
        in_specs=[
            pl.BlockSpec((1, rows, 256), lambda m, g: (m, 0, g)),
            pl.BlockSpec((1, keys, 128), lambda m, g: (m, 0, 2 * g)),
            pl.BlockSpec((1, keys, 128), lambda m, g: (m, 0, 2 * g + 1)),
            pl.BlockSpec((keys, 4 * rows), lambda m, g: (0, 0)),
        ],
        out_specs=[
            pl.BlockSpec((1, rows, 256), lambda m, g: (m, 0, g)),
            pl.BlockSpec((1, 1, 1, 4 * rows), lambda m, g: (m, g, 0, 0)),
        ],
        out_shape=[
            jax.ShapeDtypeStruct((micro, rows, groups * 256), F32),
            jax.ShapeDtypeStruct((micro, groups, 1, 4 * rows), F32),
        ],
        compiler_params=pltpu.CompilerParams(vmem_limit_bytes=VMEM_LIMIT),
        cost_estimate=pl.CostEstimate(
            flops=micro * groups * 4 * rows * keys * 128 * 4,
            bytes_accessed=2 * micro * keys * width + 4 * keys * 4 * rows,
            transcendentals=micro * groups * 4 * rows * keys,
        ),
    )(qkv, kv, kv, bias)


def attend_back_kernel(
    q_ref, k_ref, v_ref, bias_ref, do_ref, o_ref, lse_ref, cos_ref, sin_ref, kcos_ref, ksin_ref,
    dq_ref, dkv_ref,
):
    scale = HEAD**-0.5
    queries = (stack_heads(q_ref[0]) * scale).astype(BF16)
    grads_wide = stack_heads(do_ref[0])
    product = grads_wide * stack_heads(o_ref[0])
    delta = jnp.sum(product.T, axis=0, keepdims=True)
    grads = grads_wide.astype(BF16)
    keys, values = k_ref[0], v_ref[0]
    probs = jnp.exp(dot_nt(keys, queries) + bias_ref[...] - lse_ref[0, 0])
    dvalues = dot_nn(probs.astype(BF16), grads)
    dscores = (probs * (dot_nt(values, grads) - delta)).astype(BF16)
    dkeys = dot_nn(dscores, queries)
    dqueries = dot_tn(keys, dscores) * scale
    first, second = unstack_heads(dqueries.T)
    cos, sin = cos_ref[...], sin_ref[...]
    dq_ref[0, :, :128] = (first * cos - swap_halves(first) * sin).astype(BF16)
    dq_ref[0, :, 128:] = (second * cos - swap_halves(second) * sin).astype(BF16)
    dkv_ref[0, :, :128] = (dkeys * kcos_ref[...] - swap_halves(dkeys) * ksin_ref[...]).astype(BF16)
    dkv_ref[0, :, 128:] = dvalues.astype(BF16)


def attend_back(qkv, kv, bias, grad, o, lse, cos, sin, kcos, ksin):
    micro, rows, _ = qkv.shape
    keys, width = kv.shape[1], kv.shape[2]
    groups = width // 256
    mine = pl.BlockSpec((1, rows, 256), lambda m, g: (m, 0, g))
    return pl.pallas_call(
        attend_back_kernel,
        grid=(micro, groups),
        in_specs=[
            mine,
            pl.BlockSpec((1, keys, 128), lambda m, g: (m, 0, 2 * g)),
            pl.BlockSpec((1, keys, 128), lambda m, g: (m, 0, 2 * g + 1)),
            pl.BlockSpec((keys, 4 * rows), lambda m, g: (0, 0)),
            mine,
            mine,
            pl.BlockSpec((1, 1, 1, 4 * rows), lambda m, g: (m, g, 0, 0)),
            pl.BlockSpec((rows, 128), lambda m, g: (0, 0)),
            pl.BlockSpec((rows, 128), lambda m, g: (0, 0)),
            pl.BlockSpec((keys, 128), lambda m, g: (0, 0)),
            pl.BlockSpec((keys, 128), lambda m, g: (0, 0)),
        ],
        out_specs=[mine, pl.BlockSpec((1, keys, 256), lambda m, g: (m, 0, g))],
        out_shape=[
            jax.ShapeDtypeStruct((micro, rows, groups * 256), BF16),
            jax.ShapeDtypeStruct((micro, keys, width), BF16),
        ],
        compiler_params=pltpu.CompilerParams(vmem_limit_bytes=VMEM_LIMIT),
        cost_estimate=pl.CostEstimate(
            flops=micro * groups * 4 * rows * keys * 128 * 10,
            bytes_accessed=4 * micro * keys * width + 4 * keys * 4 * rows,
            transcendentals=micro * groups * 4 * rows * keys,
        ),
    )(qkv, kv, kv, bias, grad, o, lse, cos, sin, kcos, ksin)


def chosen_rows(place_ref, weight_ref, m, cap, tokens):
    slots = lax.broadcasted_iota(jnp.int32, (cap, tokens), 0)
    hit = slots == place_ref[0, m : m + 1, :]
    pick = jnp.where(hit, 1.0, 0.0)
    weight = jnp.sum(pick * weight_ref[0, m : m + 1, :], axis=1, keepdims=True)
    return pick.astype(BF16), weight


def load_tokens(pieces, scratch):
    for at, piece in enumerate(pieces):
        rows = piece.shape[1]
        scratch[:, at * rows : (at + 1) * rows, :] = piece[...]


def store_tokens(out_ref, total):
    blocks, _, rows, _ = out_ref.shape
    for at in range(blocks):
        out_ref[at] = total[:, at * rows : (at + 1) * rows, :].astype(BF16)


def by_load(counts_ref, body, empty=None):
    e = pl.program_id(0)
    most = jnp.maximum(counts_ref[2 * e], counts_ref[2 * e + 1])
    below = 0
    for cap in (CAP // 3, 2 * CAP // 3, CAP):
        pl.when((most > below) & (most <= cap))(functools.partial(body, cap))
        below = cap
    if empty is not None:
        pl.when(most == 0)(empty)


def experts_kernel(ncol, counts_ref, place_ref, weight_ref, *refs):
    pieces, refs = refs[:ncol], refs[ncol:]
    gate_ref, up_ref, down_ref, y_ref, chosen_ref, hidden_ref, tokens_ref, total_ref, rows_ref, out_ref = refs
    micro, tokens, _ = tokens_ref.shape
    hidden = gate_ref.shape[2]
    e = pl.program_id(0)

    @pl.when(e == 0)
    def _():
        load_tokens(pieces, tokens_ref)
        total_ref[...] = jnp.zeros_like(total_ref)

    def body(cap):
        picks, weights = [], []
        for m in range(micro):
            pick, weight = chosen_rows(place_ref, weight_ref, m, cap, tokens)
            chosen = dot_nn(pick, tokens_ref[m]).astype(BF16)
            rows_ref[m * cap : (m + 1) * cap, :] = chosen
            chosen_ref[0, m, :cap, :] = chosen
            picks.append(pick)
            weights.append(weight)
        used = micro * cap
        gate = dot_nn(rows_ref[:used, :], gate_ref[0])
        up = dot_nn(rows_ref[:used, :], up_ref[0])
        for m in range(micro):
            hidden_ref[0, m, :cap, :hidden] = gate[m * cap : (m + 1) * cap].astype(BF16)
            hidden_ref[0, m, :cap, hidden:] = up[m * cap : (m + 1) * cap].astype(BF16)
        active = (gate * jax.nn.sigmoid(gate) * up).astype(BF16)
        scale = jnp.concatenate(weights, axis=0)
        out_ref[:used, :] = (dot_nn(active, down_ref[0]) * scale).astype(BF16)
        for m in range(micro):
            total_ref[m] += dot_tn(picks[m], out_ref[m * cap : (m + 1) * cap, :])

    by_load(counts_ref, body)

    @pl.when(e == pl.num_programs(0) - 1)
    def _():
        store_tokens(y_ref, total_ref)


def expert_specs(pieces, weights, slots):
    micro, rows, width = pieces[0].shape
    at_expert = lambda e: (e, 0, 0)
    specs = [
        pl.BlockSpec(memory_space=pltpu.SMEM),
        pl.BlockSpec((1, *slots.shape[1:]), at_expert),
        pl.BlockSpec((1, *slots.shape[1:]), at_expert),
    ]
    specs += [pl.BlockSpec((micro, rows, width), lambda e: (0, 0, 0)) for _ in pieces]
    specs += [pl.BlockSpec((1, *w.shape[1:]), at_expert) for w in weights]
    return specs


def experts(counts, place, weight, pieces, weights):
    micro, rows, width = pieces[0].shape
    local, hidden = weights[0].shape[0], weights[0].shape[2]
    ncol = len(pieces)
    tokens = ncol * rows
    at_expert = lambda e: (e, 0, 0, 0)
    return pl.pallas_call(
        functools.partial(experts_kernel, ncol),
        grid=(local,),
        in_specs=expert_specs(pieces, weights, place),
        out_specs=[
            pl.BlockSpec((ncol, micro, rows, width), lambda e: (0, 0, 0, 0)),
            pl.BlockSpec((1, micro, CAP, width), at_expert),
            pl.BlockSpec((1, micro, CAP, 2 * hidden), at_expert),
        ],
        out_shape=[
            jax.ShapeDtypeStruct((ncol, micro, rows, width), BF16),
            jax.ShapeDtypeStruct((local, micro, CAP, width), BF16),
            jax.ShapeDtypeStruct((local, micro, CAP, 2 * hidden), BF16),
        ],
        scratch_shapes=[
            pltpu.VMEM((micro, tokens, width), BF16),
            pltpu.VMEM((micro, tokens, width), F32),
            pltpu.VMEM((micro * CAP, width), BF16),
            pltpu.VMEM((micro * CAP, width), BF16),
        ],
        compiler_params=pltpu.CompilerParams(vmem_limit_bytes=VMEM_LIMIT),
        cost_estimate=pl.CostEstimate(
            flops=local * micro * 256 * width * (6 * hidden + 4 * tokens),
            bytes_accessed=local * width * (6 * hidden + 4 * micro * CAP),
            transcendentals=local * micro * CAP * hidden,
        ),
    )(counts, place, weight, *pieces, *weights)


def experts_back_kernel(ncol, counts_ref, place_ref, weight_ref, *refs):
    pieces, refs = refs[:ncol], refs[ncol:]
    gate_ref, up_ref, down_ref, chosen_ref, hidden_ref, dx_ref, dgate_ref, dup_ref, ddown_ref, *refs = refs
    tokens_ref, total_ref, rows_ref, out_ref, dhid_ref = refs
    micro, tokens, _ = tokens_ref.shape
    hidden = gate_ref.shape[2]
    e = pl.program_id(0)

    @pl.when(e == 0)
    def _():
        load_tokens(pieces, tokens_ref)
        total_ref[...] = jnp.zeros_like(total_ref)

    def body(cap):
        picks = []
        for m in range(micro):
            pick, weight = chosen_rows(place_ref, weight_ref, m, cap, tokens)
            picks.append(pick)
            rows_ref[m * cap : (m + 1) * cap, :] = (
                dot_nn(pick, tokens_ref[m]) * weight
            ).astype(BF16)
        used = micro * cap
        dactive = dot_nt(rows_ref[:used, :], down_ref[0])
        gate = jnp.concatenate([hidden_ref[0, m, :cap, :hidden] for m in range(micro)], axis=0)
        up = jnp.concatenate([hidden_ref[0, m, :cap, hidden:] for m in range(micro)], axis=0)
        gate, up = gate.astype(F32), up.astype(F32)
        sigmoid = jax.nn.sigmoid(gate)
        silu = gate * sigmoid
        dhid_ref[:used, :hidden] = (dactive * up * sigmoid * (1.0 + gate * (1.0 - sigmoid))).astype(
            BF16
        )
        dhid_ref[:used, hidden:] = (dactive * silu).astype(BF16)
        dgate, dup = dhid_ref[:used, :hidden], dhid_ref[:used, hidden:]
        out_ref[:used, :] = (dot_nt(dgate, gate_ref[0]) + dot_nt(dup, up_ref[0])).astype(BF16)
        for m in range(micro):
            total_ref[m] += dot_tn(picks[m], out_ref[m * cap : (m + 1) * cap, :])
        active = (silu * up).astype(BF16)
        for m in range(micro):
            out_ref[m * cap : (m + 1) * cap, :] = chosen_ref[0, m, :cap, :]
        dgate_ref[0] = dot_tn(out_ref[:used, :], dgate).astype(BF16)
        dup_ref[0] = dot_tn(out_ref[:used, :], dup).astype(BF16)
        ddown_ref[0] = dot_tn(active, rows_ref[:used, :]).astype(BF16)

    def empty():
        for ref in (dgate_ref, dup_ref, ddown_ref):
            ref[...] = jnp.zeros_like(ref)

    by_load(counts_ref, body, empty)

    @pl.when(e == pl.num_programs(0) - 1)
    def _():
        store_tokens(dx_ref, total_ref)


def experts_back(counts, place, weight, pieces, weights, chosen, hid):
    micro, rows, width = pieces[0].shape
    local, hidden = weights[0].shape[0], weights[0].shape[2]
    ncol = len(pieces)
    tokens = ncol * rows
    at_expert = lambda e: (e, 0, 0, 0)
    return pl.pallas_call(
        functools.partial(experts_back_kernel, ncol),
        grid=(local,),
        in_specs=[
            *expert_specs(pieces, weights, place),
            pl.BlockSpec((1, micro, CAP, width), at_expert),
            pl.BlockSpec((1, micro, CAP, 2 * hidden), at_expert),
        ],
        out_specs=[
            pl.BlockSpec((ncol, micro, rows, width), lambda e: (0, 0, 0, 0)),
            *[pl.BlockSpec((1, *w.shape[1:]), lambda e: (e, 0, 0)) for w in weights],
        ],
        out_shape=[
            jax.ShapeDtypeStruct((ncol, micro, rows, width), BF16),
            *[jax.ShapeDtypeStruct(w.shape, BF16) for w in weights],
        ],
        scratch_shapes=[
            pltpu.VMEM((micro, tokens, width), BF16),
            pltpu.VMEM((micro, tokens, width), F32),
            pltpu.VMEM((micro * CAP, width), BF16),
            pltpu.VMEM((micro * CAP, width), BF16),
            pltpu.VMEM((micro * CAP, 2 * hidden), BF16),
        ],
        compiler_params=pltpu.CompilerParams(vmem_limit_bytes=VMEM_LIMIT),
        cost_estimate=pl.CostEstimate(
            flops=local * micro * 256 * width * (12 * hidden + 4 * tokens),
            bytes_accessed=local * width * (12 * hidden + 4 * micro * CAP),
            transcendentals=local * micro * CAP * hidden,
        ),
    )(counts, place, weight, *pieces, *weights, chosen, hid)


def spread_rows(value):
    both = jnp.stack([value, exchange(value)])
    return gather_col(both)


def collect_rows(partial):
    blocks = [partial[k] for k in range(partial.shape[0])]
    theirs = exchange(scatter_col([b[1] for b in blocks]).astype(BF16))
    return scatter_col([b[0] for b in blocks]) + theirs.astype(F32)


def forward_layer(layer_in, env, part):
    rows, width = layer_in.shape
    prompt = env["prompt"]
    normed, qkv = project(layer_in, part["gain_first"], env["cos"], env["sin"], part)
    own = qkv[:, width:]
    near = gather_col(own)
    far = gather_col(jnp.concatenate(gather_row(own[:prompt])[1:], axis=0))
    kv = jnp.concatenate([b for pair in zip(near, far) for b in pair], axis=0)
    mixed, lse = attend(qkv[None], kv[None], env["bias"])
    second, normed_second = close_attention(layer_in, mixed[0], part["gain_second"], part)
    pieces = spread_rows(normed_second)
    partial, chosen, hid = experts(*part["slots"], pieces, part["experts"])
    result = second + collect_rows(partial)
    keep = {
        "layer_in": layer_in,
        "normed": normed,
        "qkv": qkv,
        "kv": kv,
        "mixed": mixed,
        "lse": lse,
        "second": second,
        "pieces": pieces[-1],
        "chosen": chosen,
        "hid": hid,
    }
    return result, keep


def backward_layer(grad_result, keep, env, part):
    rows, _ = grad_result.shape
    prompt = env["prompt"]
    ncol, nrow = lax.axis_size("col"), lax.axis_size("row")
    pieces = spread_rows(grad_result.astype(BF16))
    partial, *expert_grads = experts_back(
        *part["slots"], pieces, part["experts"], keep["chosen"], keep["hid"]
    )
    dn2 = collect_rows(partial)
    dsecond, dbranch, dmixed, gain_second = open_back(
        grad_result, dn2, keep["second"], part["gain_second"], part
    )
    dq, dkv = attend_back(
        keep["qkv"][None], keep["kv"][None], env["bias"], dmixed[None], keep["mixed"],
        keep["lse"], env["cos"], env["sin"], env["kcos"], env["ksin"],
    )
    span = dkv.shape[1] // ncol
    own = scatter_col([dkv[0, k * span : (k + 1) * span] for k in range(ncol)])
    parts = [own[:prompt]]
    for j in range(1, nrow):
        at = rows + (j - 1) * prompt
        parts.append(own[at : at + prompt].astype(BF16))
    own = jnp.concatenate([scatter_row(parts), own[prompt:rows]], axis=0).astype(BF16)
    grad_in, gain_first = project_back(
        dq[0], own, keep["layer_in"], part["gain_first"], dsecond, part
    )
    small = weight_back(keep["normed"], dq[0], own, keep["mixed"][0], dbranch, part)
    return grad_in, {
        "small": small,
        "experts": expert_grads,
        "gain_first": gain_first[0],
        "gain_second": gain_second[0],
    }


def own_rows(value, prompt_rows):
    micro, _, shard = value.shape
    ncol = lax.axis_size("col")
    return jnp.concatenate(
        [
            value[:, :prompt_rows].reshape(micro, ncol, -1, shard),
            value[:, prompt_rows:].reshape(micro, ncol, -1, shard),
        ],
        axis=2,
    )


def to_rows(value, prompt_rows):
    split = own_rows(value, prompt_rows)
    return lax.all_to_all(split, "col", 1, 3, tiled=True)[:, 0]


def to_columns(value, prompt):
    micro, _, width = value.shape
    ncol = lax.axis_size("col")
    split = lax.all_to_all(value[:, None], "col", 3, 1, tiled=True)
    shard = width // ncol
    return jnp.concatenate(
        [
            split[:, :, :prompt].reshape(micro, -1, shard),
            split[:, :, prompt:].reshape(micro, -1, shard),
        ],
        axis=1,
    )


def turn_tables(positions):
    half = HEAD // 2
    freqs = THETA ** (-(jnp.arange(half).astype(F32) * 2.0) / HEAD)
    angles = positions.astype(F32)[:, None] * freqs[None, :]
    cos, sin = jnp.cos(angles), jnp.sin(angles)
    return (
        jnp.concatenate([cos, cos, cos, cos], axis=1),
        jnp.concatenate([-sin, sin, -sin, sin], axis=1),
    )


def small_weights(packed, w_rows, early):
    nrow, ncol = lax.axis_size("row"), lax.axis_size("col")
    row, col = lax.axis_index("row"), lax.axis_index("col")
    cut = packed.shape[0]
    starts = ((row - jnp.arange(nrow, dtype=jnp.int32)) % nrow) * cut
    if early:
        pieces = [packed]
        for _ in range(nrow - 1):
            pieces.append(ring(pieces[-1]))
    else:
        pieces = gather_row(packed)
    blocks = gather_col(jnp.stack(pieces))
    if w_rows == 256:
        order = (col ^ jnp.arange(ncol, dtype=jnp.int32)) * 256
        lanes = (512, 256)
        return {"starts": jnp.concatenate([starts, order]), "qkv": blocks, "out": blocks, "out_lanes": lanes}
    blocks = jnp.stack(blocks)
    whole = [lax.dynamic_index_in_dim(blocks, col ^ c, 0, False) for c in range(ncol)]
    qkv, out = [], []
    for a, b in zip(whole[::2], whole[1::2]):
        heads = [a[..., :64], b[..., :64], a[..., 64:128], b[..., 64:128]]
        others = [a[..., 128:192], b[..., 128:192], a[..., 192:256], b[..., 192:256]]
        qkv.append(jnp.concatenate(heads + others, axis=2))
        a, b = a[..., 256:], b[..., 256:]
        out.append(jnp.concatenate([a[:, :64], b[:, :64], a[:, 64:], b[:, 64:]], axis=1))
    order = jnp.arange(len(qkv), dtype=jnp.int32) * 256
    return {"starts": jnp.concatenate([starts, order]), "qkv": qkv, "out": out, "out_lanes": (0, cut)}


def pack_weights(w_query, w_key, w_value, w_out):
    if w_out.shape[0] == 256:
        heads = lambda v: [v[..., :64], v[..., 128:192], v[..., 64:128], v[..., 192:]]
        rows = [w_out[:64], w_out[128:192], w_out[64:128], w_out[192:]]
        w_out = jnp.concatenate(rows, axis=0)
        w_query = jnp.concatenate(heads(w_query), axis=1)
    return jnp.concatenate([w_query, w_key, w_value, w_out], axis=1)


def small_gradients(qkv, out, w_rows):
    nrow, ncol = lax.axis_size("row"), lax.axis_size("col")
    col = lax.axis_index("col")
    if w_rows == 256:
        blocks = [jnp.concatenate([a, b], axis=2) for a, b in zip(qkv, out)]
    else:
        whole = []
        for a, b in zip(qkv, out):
            for c in (0, 1):
                at = lambda i: a[..., 64 * i : 64 * i + 64]
                heads = [at(c), at(2 + c), at(4 + c), at(6 + c)]
                rows = jnp.concatenate(
                    [b[:, 64 * c : 64 * c + 64], b[:, 128 + 64 * c : 192 + 64 * c]], axis=1
                )
                whole.append(jnp.concatenate([*heads, rows], axis=2))
        whole = jnp.stack(whole)
        blocks = [lax.dynamic_index_in_dim(whole, col ^ k, 0, False) for k in range(ncol)]
    mine = scatter_col(blocks).astype(BF16)
    return scatter_row([mine[j] for j in range(nrow)]).astype(BF16)


def routing(ids, scale, prompt_rows, first, local):
    ncol, col = lax.axis_size("col"), lax.axis_index("col")

    def mine(value):
        blocks = own_rows(value, prompt_rows)
        order = [lax.dynamic_index_in_dim(blocks, col ^ k, 1, False) for k in range(ncol)]
        return jnp.concatenate(order, axis=1).transpose(0, 2, 1)

    ids, scale = mine(ids), mine(scale)
    names = first + jnp.arange(local, dtype=jnp.int32)
    match = ids[None] == names[:, None, None, None]
    member = jnp.any(match, axis=2)
    weight = jnp.sum(jnp.where(match, scale[None], 0.0), axis=2)
    tokens = member.shape[2]
    order = jnp.arange(tokens, dtype=jnp.int32)
    earlier = (order[:, None] <= order[None, :]).astype(BF16)
    seen = dot_nn(member.astype(BF16).reshape(-1, tokens), earlier).astype(jnp.int32)
    seen = seen.reshape(member.shape)
    return seen[:, :, -1].reshape(-1), jnp.where(member, seen - 1, -1), weight


def on_device(
    x_in,
    targets,
    w_query,
    w_key,
    w_value,
    w_out,
    w_gate,
    w_up,
    w_down,
    gain_attn,
    gain_ffn,
    expert_ids,
    gates,
    lengths,
):
    section, row, col = (lax.axis_index(name) for name in ("section", "row", "col"))
    nrow, ncol = lax.axis_size("row"), lax.axis_size("col")
    micro, _, tokens, shard = x_in.shape
    width = shard * ncol
    prompt_rows = tokens - CONT_LEN
    prompt_len = prompt_rows * nrow
    prompt, cont = prompt_rows // ncol, CONT_LEN // ncol
    local = w_gate.shape[1]
    half = local // 2
    columns, kcols = w_query.shape[2], w_key.shape[2]
    home = [section == 0, section == 1]

    def by_layer(value):
        other = exchange(value)
        return [jnp.where(is_home, value, other) for is_home in home]

    w_rows = w_out.shape[1]
    packed = by_layer(pack_weights(w_query[0], w_key[0], w_value[0], w_out[0]))
    big = [w[0] for w in (w_gate, w_up, w_down)]
    crossed = [exchange(after(w[half:], packed[0])) for w in big]
    shards = [
        [jnp.where(is_home, w[:half], c) for w, c in zip(big, crossed)] for is_home in home
    ]
    ids_layer, gates_layer = by_layer(expert_ids[0, :, 0]), by_layer(gates[0, :, 0])
    gains = by_layer(jnp.concatenate([gain_attn, gain_ffn]).astype(F32))

    def whole(pieces):
        return [
            lax.all_gather(w, "row", axis=axis, tiled=True) for w, axis in zip(pieces, (1, 1, 2))
        ]

    def layer_part(layer, held):
        own_first = lambda v: jnp.where(home[0], v, v[::-1])
        first = col * local + jnp.where(home[layer], 0, half)
        ids, scale = own_first(ids_layer[layer]), own_first(gates_layer[layer])
        return {
            "experts": held,
            "gain_first": gains[layer][:1],
            "gain_second": gains[layer][1:],
            "slots": routing(ids, scale, prompt_rows, first, half),
        }

    parts = [layer_part(0, whole(shards[0]))]
    parts[0].update(small_weights(packed[0], w_rows, True))
    later = lax.optimization_barrier((shards[1], parts[0]["experts"][0]))[0]
    parts.append(layer_part(1, whole(later)))

    def prompt_positions(row_index, col_index):
        return row_index * prompt_rows + col_index * prompt + jnp.arange(prompt, dtype=jnp.int32)

    def cont_positions(col_index):
        return prompt_len + col_index * cont + jnp.arange(cont, dtype=jnp.int32)

    positions = jnp.concatenate([prompt_positions(row, col), cont_positions(col)])
    key_positions = []
    for k in range(ncol):
        key_positions += [prompt_positions(row, col ^ k), cont_positions(col ^ k)]
        key_positions += [prompt_positions((row - j) % nrow, col ^ k) for j in range(1, nrow)]
    key_positions = jnp.concatenate(key_positions)
    bias = jnp.where(key_positions[:, None] <= jnp.tile(positions, GROUP)[None, :], 0.0, NEG)
    cos, sin = turn_tables(positions)
    kcos, ksin = turn_tables(key_positions)
    env = {"prompt": prompt, "cos": cos, "sin": sin, "kcos": kcos, "ksin": ksin, "bias": bias}

    mine = lambda v: lax.dynamic_index_in_dim(v, section, 0, keepdims=True)
    first_in = to_rows(mine(x_in[:, 0]), prompt_rows)[0]
    goal = to_rows(mine(targets[:, 0]), prompt_rows)[0].astype(F32)

    result, keep_first = forward_layer(first_in, env, parts[0])
    mid = result.astype(BF16)
    parts[1].update(small_weights(after(packed[1], keep_first["pieces"]), w_rows, False))
    final, keep_last = forward_layer(mid, env, parts[1])

    count = (micro * prompt_len + jnp.sum(lengths)).astype(F32)
    length = lengths[section, row]
    valid = (positions - prompt_len < length).astype(F32)[:, None]
    diff = (final - goal) * valid
    loss = jnp.sum(diff * diff) / count
    dfinal = (2.0 / count) * diff

    dmid, last_grads = backward_layer(dfinal, keep_last, env, parts[1])
    dx, first_grads = backward_layer(dmid, keep_first, env, parts[0])

    layer_grads = [first_grads, last_grads]

    def over_rows(j, layer, *earlier):
        grad = after(layer_grads[layer]["experts"][j], *earlier)
        return lax.psum_scatter(grad, "row", scatter_dimension=(1, 1, 2)[j], tiled=True)

    returned = []

    def expert_gradient(j):
        last = over_rows(j, 1)
        back = shift(last, "section", [(0, 1)])
        first = over_rows(j, 0, back)
        returned.append(shift(first, "section", [(1, 0)]))
        own = jnp.where(home[0], first, last)
        other = jnp.where(home[0], returned[-1], back)
        return jnp.concatenate([own, other], axis=0).astype(F32)

    grad_gate, grad_up, grad_down = (expert_gradient(j) for j in range(3))
    small = [small_gradients(*grads["small"], w_rows) for grads in layer_grads]

    def at_home(first, last):
        received = exchange(jnp.where(home[0], last, first))
        return jnp.where(home[0], first, last).astype(F32) + received.astype(F32)

    small = at_home(*small)
    grad_query, grad_out = small[:, :columns], small[:, columns + 2 * kcols :]
    if w_rows == 256:
        heads = lambda v: [v[:, :64], v[:, 128:192], v[:, 64:128], v[:, 192:]]
        grad_query = jnp.concatenate(heads(grad_query), axis=1)
        grad_out = jnp.concatenate(
            [grad_out[:64], grad_out[128:192], grad_out[64:128], grad_out[192:]], axis=0
        )
    tally = jnp.concatenate(
        [g[name] for g in layer_grads for name in ("gain_first", "gain_second")]
        + [jnp.broadcast_to(loss, (128,))]
    )
    tally = total_everywhere(after(tally, returned[0]))
    loss = tally[4 * width]
    gains = tally[: 4 * width].reshape(2, 2, width)
    gains = jnp.where(home[0], gains[0], gains[1])
    gains = lax.dynamic_slice_in_dim(gains, col * shard, shard, 1)

    def both_micros(first, last):
        received = exchange(jnp.where(home[0], last, first))
        pair = jnp.where(home[0], jnp.stack([first, received]), jnp.stack([received, last]))
        return to_columns(pair, prompt)

    outputs = both_micros(mid, final.astype(BF16))
    input_grads = both_micros(after(dx, returned[1]), dmid)
    return (
        outputs[None, :, None],
        loss,
        input_grads[None, :, None],
        grad_query[None],
        small[None, :, columns : columns + kcols],
        small[None, :, columns + kcols : columns + 2 * kcols],
        grad_out[None],
        grad_gate[None],
        grad_up[None],
        grad_down[None],
        gains[:1],
        gains[1:],
    )


def solution(mesh):
    in_specs = (
        P(None, "row", None, "col"),
        P(None, "row", None, "col"),
        P("section", "row", "col"),
        P("section", "row", "col"),
        P("section", "row", "col"),
        P("section", "col", "row"),
        P("section", "col", "row", None),
        P("section", "col", "row", None),
        P("section", "col", None, "row"),
        P("section", None),
        P("section", None),
        P("section", None, "row", None, None),
        P("section", None, "row", None, None),
        P(),
    )
    out_specs = (
        P("section", None, "row", None, "col"),
        P(),
        P("section", None, "row", None, "col"),
        P("section", "row", "col"),
        P("section", "row", "col"),
        P("section", "row", "col"),
        P("section", "col", "row"),
        P("section", "col", "row", None),
        P("section", "col", "row", None),
        P("section", "col", None, "row"),
        P("section", "col"),
        P("section", "col"),
    )
    return jax.shard_map(
        on_device, mesh=mesh, in_specs=in_specs, out_specs=out_specs, check_vma=False
    )
```

time: 1770 us -> 1360 us (0.77)
  blocking collectives: 173 us -> 0 us
  waiting for transfers between devices: 890 us -> 752 us
  starting transfers between devices: 82.4 us -> 204 us
  Pallas kernels: 309 us -> 215 us
  local copies, waits for them, and re-layouts: 155 us -> 70.6 us
  matrix products: 20.3 us -> 0.43 us
    ppermute x104 -> x119, waiting for transfers between devices: 825 us -> 627 us  [shift(): return lax.ppermute(value, axis, pairs)]
    psum x2 -> x0, blocking collectives: 173 us -> none  [the longest x1 141 us: on_device(): loss = lax.psum(loss, ('section', 'row', 'col'))]
    ppermute x104 -> x119, starting transfers between devices: 65.7 us -> 187 us  [shift(): return lax.ppermute(value, axis, pairs)]
    reduce_scatter x2 -> x6, waiting for transfers between devices: 0.01 us -> 52.6 us  [over_rows(): lax.psum_scatter(grad, 'row', scatter_dimension=(1, 1, 2)[j], tiled=True)]
    pallas_call x6 -> x14, Pallas kernels: 208 us -> 157 us  [the longest x2 64.1 us: experts_back(): pl.pallas_call(functools.partial(experts_back_kernel, ncol), grid=(local,...]
    pallas_call x2, Pallas kernels: 63.1 us -> 35.8 us  [attend_back(): pl.pallas_call(attend_back_kernel, grid=(micro, groups), in_specs=[mine,...]
    convert_element_type x25 -> x14, other arithmetic: 46.5 us -> 20.6 us  [the longest x3 8.17 us: expert_gradient(): return jnp.concatenate([own, other], axis=0).astype(F32)]
    unnamed x159 -> x164, local copies, waits for them, and re-layouts: 41.4 us -> 20.2 us
  transfers between devices with their start and end apart: 112 -> 135, of which waited for: 49 -> 66; matrix products, arithmetic and copies ran while one was open for 13% -> 11% of each run, Pallas kernels for 2% -> 12%
where the time goes in v3:
time: 1360 us
  waiting for transfers between devices  752 us (55%)
  Pallas kernels  215 us (16%)
  starting transfers between devices  204 us (15%)
  other arithmetic  98.4 us (7%)
  local copies, waits for them, and re-layouts  70.6 us (5%)
  between operations  17.5 us (1%)
    ppermute x119, waiting for transfers between devices, shift(): return lax.ppermute(value, axis, pairs)  627 us
    ppermute x119, starting transfers between devices, shift(): return lax.ppermute(value, axis, pairs)  187 us
    all_gather x6, waiting for transfers between devices, whole(): lax.all_gather(w, 'row', axis=axis, tiled=True)  65.4 us
    pallas_call x2, Pallas kernels, experts_back(): pl.pallas_call(functools.partial(experts_back_kernel, ncol), grid=(local,...  64.1 us
    reduce_scatter x6, waiting for transfers between devices, over_rows(): lax.psum_scatter(grad, 'row', scatter_dimension=(1, 1, 2)[j], tiled=True)  52.6 us
    pallas_call x2, Pallas kernels, experts(): pl.pallas_call(functools.partial(experts_kernel, ncol), grid=(local,), in...  45 us
    pallas_call x8, Pallas kernels, whole_call(): pl.pallas_call(functools.partial(kernel, len(blocks)), grid=(1,), in_spec...  36.3 us
    pallas_call x2, Pallas kernels, attend_back(): pl.pallas_call(attend_back_kernel, grid=(micro, groups), in_specs=[mine,...  35.8 us
  transfers between devices with their start and end apart: 135, of which 66 were waited for; matrix products, arithmetic and copies ran while one was open for 11% of the time, Pallas kernels for 12%

profile of v3, /device:TPU:0, one launch (start us, length us, event | category | flops | bytes accessed | tf_op | source)
XLA Modules:
  0.0 1358.3 jit_solution(2437023024473264727)
XLA Ops:
  25.4 22.6 %collective-permute-done.23 = bf16[4,256,512]{2,1,0:T(8,128)(2,1)S(1)} collective-permute-done((bf16[4,256,512]{2,1,0:T(8,128)(2,1)S(1)}, bf16[4,256,512]{2,1,0:T(8,128)(2,1)S(1)}, u32[]{:S(2)}, u32[]{:S(2)}) %collective-permute-start.23) | collective-permute-done | bytes 1048608 | tf_op jit(solution)/shard_map/ppermute | solution.py:25
  52.3 22.0 %collective-permute-done.24 = bf16[4,256,512]{2,1,0:T(8,128)(2,1)S(1)} collective-permute-done((bf16[4,256,512]{2,1,0:T(8,128)(2,1)S(1)}, bf16[4,256,512]{2,1,0:T(8,128)(2,1)S(1)}, u32[]{:S(2)}, u32[]{:S(2)}) %collective-permute-start.24) | collective-permute-done | bytes 1048608 | tf_op jit(solution)/shard_map/ppermute | solution.py:25
  78.3 21.5 %collective-permute-done.25 = bf16[4,512,256]{2,1,0:T(8,128)(2,1)S(1)} collective-permute-done((bf16[4,512,256]{2,1,0:T(8,128)(2,1)S(1)}, bf16[4,512,256]{2,1,0:T(8,128)(2,1)S(1)}, u32[]{:S(2)}, u32[]{:S(2)}) %collective-permute-start.25) | collective-permute-done | bytes 1048608 | tf_op jit(solution)/shard_map/ppermute | solution.py:25
  101.4 30.2 %all-gather.7.cloned.1.call-done.refs_4_ = bf16[4,1024,512]{2,1,0:T(8,128)(2,1)} async-done(((bf16[4,256,512]{2,1,0:T(8,128)(2,1)}), bf16[4,1024,512]{2,1,0:T(8,128)(2,1)}) %all-gather.7.cloned.1.call-update) | async-done | bytes 4194320 | tf_op jit(solution)/shard_map/all_gather | solution.py:886
  131.7 12.8 collective-permute-done.2
  144.4 21.5 %collective-permute-done.3 = bf16[256,768]{1,0:T(8,128)(2,1)S(1)} collective-permute-done((bf16[256,768]{1,0:T(8,128)(2,1)S(1)}, bf16[256,768]{1,0:T(8,128)(2,1)S(1)}, u32[]{:S(2)}, u32[]{:S(2)}) %collective-permute-start.3) | collective-permute-done | bytes 393248 | tf_op jit(solution)/shard_map/ppermute | solution.py:25
  167.4 22.1 %collective-permute-done.4 = bf16[256,768]{1,0:T(8,128)(2,1)S(1)} collective-permute-done((bf16[256,768]{1,0:T(8,128)(2,1)S(1)}, bf16[256,768]{1,0:T(8,128)(2,1)S(1)}, u32[]{:S(2)}, u32[]{:S(2)}) %collective-permute-start.4) | collective-permute-done | bytes 393248 | tf_op jit(solution)/shard_map/ppermute | solution.py:25
  205.2 21.2 %collective-permute-done.6.refs_2_ = bf16[4,256,768]{2,1,0:T(8,128)(2,1)S(1)} collective-permute-done((bf16[4,256,768]{2,1,0:T(8,128)(2,1)S(1)}, bf16[4,256,768]{2,1,0:T(8,128)(2,1)S(1)}, u32[]{:S(2)}, u32[]{:S(2)}) %collective-permute-start.6) | collective-permute-done | bytes 1572896 | tf_op jit(solution)/shard_map/ppermute | solution.py:25
  321.7 16.7 %collective-permute-done.21.refs_2_ = bf16[2,192,1024]{2,1,0:T(8,128)(2,1)S(1)} collective-permute-done((bf16[2,192,1024]{2,1,0:T(8,128)(2,1)}, bf16[2,192,1024]{2,1,0:T(8,128)(2,1)S(1)}, u32[]{:S(2)}, u32[]{:S(2)}) %collective-permute-start.21) | collective-permute-done | bytes 786464 | tf_op jit(solution)/shard_map/ppermute | solution.py:25
  341.5 12.4 collective-permute-start.35
  357.1 14.7 %collective-permute-done.35 = bf16[256,768]{1,0:T(8,128)(2,1)S(1)} collective-permute-done((bf16[256,768]{1,0:T(8,128)(2,1)S(1)}, bf16[256,768]{1,0:T(8,128)(2,1)S(1)}, u32[]{:S(2)}, u32[]{:S(2)}) %collective-permute-start.35) | collective-permute-done | bytes 393248 | tf_op jit(solution)/shard_map/ppermute | solution.py:25
  371.8 47.9 %collective-permute-done.34 = bf16[256,768]{1,0:T(8,128)(2,1)S(1)} collective-permute-done((bf16[256,768]{1,0:T(8,128)(2,1)S(1)}, bf16[256,768]{1,0:T(8,128)(2,1)S(1)}, u32[]{:S(2)}, u32[]{:S(2)}) %collective-permute-start.34) | collective-permute-done | bytes 393248 | tf_op jit(solution)/shard_map/ppermute | solution.py:25
  421.4 23.5 %shard_map.232 = (bf16[4,2,192,1024]{3,2,1,0:T(8,128)(2,1)}, bf16[4,2,384,1024]{3,2,1,0:T(8,128)(2,1)}, bf16[4,2,384,1024]{3,2,1,0:T(8,128)(2,1)}) custom-call(s32[8]{0:T(128)} %reshape_squeeze.6.counts_ref, s32[4,2,768]{2,1,0:T(2,128)} %add_select_fusion.1.place_ref, f32[4,2,768]{2,1,0:T(2,128)} %fusion.37.weight_ref, ...), custom_call_target="tpu_custom_call" | custom-call | flops 12884901888 | bytes 25165824 | tf_op jit(solution)/shard_map/pallas_call | solution.py:525
  559.3 15.9 %collective-permute-done.50.refs_2_ = bf16[2,192,1024]{2,1,0:T(8,128)(2,1)S(1)} collective-permute-done((bf16[2,192,1024]{2,1,0:T(8,128)(2,1)S(1)}, bf16[2,192,1024]{2,1,0:T(8,128)(2,1)S(1)}, u32[]{:S(2)}, u32[]{:S(2)}) %collective-permute-start.50) | collective-permute-done | bytes 786464 | tf_op jit(solution)/shard_map/ppermute | solution.py:25
  576.8 35.2 %all-gather.17.cloned.1.call-done.refs_6_ = bf16[4,512,1024]{2,1,0:T(8,128)(2,1)} async-done(((bf16[4,512,256]{2,1,0:T(8,128)(2,1)}), bf16[4,512,1024]{2,1,0:T(8,128)(2,1)}) %all-gather.17.cloned.1.call-update) | async-done | bytes 4194320 | tf_op jit(solution)/shard_map/all_gather | solution.py:886
  612.0 21.5 %shard_map.236 = (bf16[4,2,192,1024]{3,2,1,0:T(8,128)(2,1)}, bf16[4,2,384,1024]{3,2,1,0:T(8,128)(2,1)}, bf16[4,2,384,1024]{3,2,1,0:T(8,128)(2,1)}) custom-call(s32[8]{0:T(128)} %reshape_squeeze.7.counts_ref, s32[4,2,768]{2,1,0:T(2,128)} %add_select_fusion.place_ref, f32[4,2,768]{2,1,0:T(2,128)} %fusion.38.weight_ref, bf16[2,192,1024]{2,1,0:T(8,128)(2,1)} %copy-done.38, ...), custom_call_target="tpu_custom_call" | custom-call | flops 12884901888 | bytes 25165824 | tf_op jit(solution)/shard_map/pallas_call | solution.py:525
  684.9 17.1 %collective-permute-done.62.refs_2_ = bf16[2,192,1024]{2,1,0:T(8,128)(2,1)S(1)} collective-permute-done((bf16[2,192,1024]{2,1,0:T(8,128)(2,1)S(1)}, bf16[2,192,1024]{2,1,0:T(8,128)(2,1)S(1)}, u32[]{:S(2)}, u32[]{:S(2)}) %collective-permute-start.62) | collective-permute-done | bytes 786464 | tf_op jit(solution)/shard_map/ppermute | solution.py:25
  705.2 29.9 %shard_map.237 = (bf16[4,2,192,1024]{3,2,1,0:T(8,128)(2,1)}, bf16[4,1024,512]{2,1,0:T(8,128)(2,1)}, bf16[4,1024,512]{2,1,0:T(8,128)(2,1)}, bf16[4,512,1024]{2,1,0:T(8,128)(2,1)}) custom-call(s32[8]{0:T(128)} %reshape_squeeze.7.counts_ref, s32[4,2,768]{2,1,0:T(2,128)} %add_select_fusion.place_ref, f32[4,2,768]{2,1,0:T(2,128)} %fusion.38.weight_ref, ...), custom_call_target="tpu_custom_call" | custom-call | flops 19327352832 | bytes 37748736 | tf_op jit(solution)/shard_map/pallas_call | solution.py:614
  783.6 18.0 %shard_map.239 = (bf16[1,192,1024]{2,1,0:T(8,128)(2,1)}, bf16[1,1536,1024]{2,1,0:T(8,128)(2,1)}) custom-call(bf16[1,192,2048]{2,1,0:T(8,128)(2,1)} %bitcast.347, bf16[1,1536,1024]{2,1,0:T(8,128)(2,1)} %bitcast.328, bf16[1,1536,1024]{2,1,0:T(8,128)(2,1)} %bitcast.329, f32[1536,768]{1,0:T(8,128)} %compare_select_fusion.bias_ref, ...), custom_call_target="tpu_custom_call" | custom-call | flops 6039797760 | bytes 11010048 | tf_op jit(solution)/shard_map/pallas_call | solution.py:405
  807.5 18.0 %collective-permute-done.73 = bf16[384,1024]{1,0:T(8,128)(2,1)S(1)} collective-permute-done((bf16[384,1024]{1,0:T(8,128)(2,1)S(1)}, bf16[384,1024]{1,0:T(8,128)(2,1)S(1)}, u32[]{:S(2)}, u32[]{:S(2)}) %collective-permute-start.73) | collective-permute-done | bytes 786464 | tf_op jit(solution)/shard_map/ppermute | solution.py:25
  835.0 11.8 collective-permute-done.75
  863.8 12.9 collective-permute-done.79.refs_2_
  880.4 34.2 %shard_map.241 = (bf16[4,2,192,1024]{3,2,1,0:T(8,128)(2,1)}, bf16[4,1024,512]{2,1,0:T(8,128)(2,1)}, bf16[4,1024,512]{2,1,0:T(8,128)(2,1)}, bf16[4,512,1024]{2,1,0:T(8,128)(2,1)}) custom-call(s32[8]{0:T(128)} %reshape_squeeze.6.counts_ref, s32[4,2,768]{2,1,0:T(2,128)} %add_select_fusion.1.place_ref, f32[4,2,768]{2,1,0:T(2,128)} %fusion.37.weight_ref, ...), custom_call_target="tpu_custom_call" | custom-call | flops 19327352832 | bytes 37748736 | tf_op jit(solution)/shard_map/pallas_call | solution.py:614
  916.1 20.1 %collective-permute-done.101 = bf16[4,256,512]{2,1,0:T(8,128)(2,1)S(1)} collective-permute-done((bf16[4,256,512]{2,1,0:T(8,128)(2,1)}, bf16[4,256,512]{2,1,0:T(8,128)(2,1)S(1)}, u32[]{:S(2)}, u32[]{:S(2)}) %collective-permute-start.101) | collective-permute-done | bytes 1048608 | tf_op jit(solution)/shard_map/ppermute | solution.py:25
  972.7 17.8 %shard_map.243 = (bf16[1,192,1024]{2,1,0:T(8,128)(2,1)}, bf16[1,1536,1024]{2,1,0:T(8,128)(2,1)}) custom-call(bf16[1,192,2048]{2,1,0:T(8,128)(2,1)} %bitcast.345, bf16[1,1536,1024]{2,1,0:T(8,128)(2,1)} %bitcast.324, bf16[1,1536,1024]{2,1,0:T(8,128)(2,1)} %bitcast.325, f32[1536,768]{1,0:T(8,128)} %compare_select_fusion.bias_ref, ...), custom_call_target="tpu_custom_call" | custom-call | flops 6039797760 | bytes 11010048 | tf_op jit(solution)/shard_map/pallas_call | solution.py:405
  1000.7 19.6 %collective-permute-done.117 = bf16[4,512,256]{2,1,0:T(8,128)(2,1)S(1)} collective-permute-done((bf16[4,512,256]{2,1,0:T(8,128)(2,1)}, bf16[4,512,256]{2,1,0:T(8,128)(2,1)S(1)}, u32[]{:S(2)}, u32[]{:S(2)}) %collective-permute-start.117) | collective-permute-done | bytes 1048608 | tf_op jit(solution)/shard_map/ppermute | solution.py:25
  1088.5 15.3 %collective-permute-done.112 = bf16[4,256,768]{2,1,0:T(8,128)(2,1)} collective-permute-done((bf16[4,256,768]{2,1,0:T(8,128)(2,1)}, bf16[4,256,768]{2,1,0:T(8,128)(2,1)}, u32[]{:S(2)}, u32[]{:S(2)}) %collective-permute-start.112) | collective-permute-done | bytes 1572896 | tf_op jit(solution)/shard_map/ppermute | solution.py:25
  1121.0 16.5 %collective-permute-done.106 = bf16[4,256,768]{2,1,0:T(8,128)(2,1)} collective-permute-done((bf16[4,256,768]{2,1,0:T(8,128)(2,1)}, bf16[4,256,768]{2,1,0:T(8,128)(2,1)}, u32[]{:S(2)}, u32[]{:S(2)}) %collective-permute-start.106) | collective-permute-done | bytes 1572896 | tf_op jit(solution)/shard_map/ppermute | solution.py:25
  1169.6 20.0 %collective-permute-done.109 = bf16[256,768]{1,0:T(8,128)(2,1)} collective-permute-done((bf16[256,768]{1,0:T(8,128)(2,1)}, bf16[256,768]{1,0:T(8,128)(2,1)}, u32[]{:S(2)}, u32[]{:S(2)}) %collective-permute-start.109) | collective-permute-done | bytes 393248 | tf_op jit(solution)/shard_map/ppermute | solution.py:25
  1189.6 25.8 %collective-permute-done.108 = bf16[256,768]{1,0:T(8,128)(2,1)} collective-permute-done((bf16[256,768]{1,0:T(8,128)(2,1)}, bf16[256,768]{1,0:T(8,128)(2,1)}, u32[]{:S(2)}, u32[]{:S(2)}) %collective-permute-start.108) | collective-permute-done | bytes 393248 | tf_op jit(solution)/shard_map/ppermute | solution.py:25
  1234.0 52.6 %reduce-scatter.17.cloned.1.call-done = bf16[4,512,256]{2,1,0:T(8,128)(2,1)} async-done(((bf16[4,512,1024]{2,1,0:T(8,128)(2,1)}), bf16[4,512,256]{2,1,0:T(8,128)(2,1)}) %reduce-scatter.17.cloned.1.call-update) | async-done | bytes 1048592 | tf_op jit(solution)/shard_map/reduce_scatter | solution.py:945
  1297.5 17.5 %collective-permute-done.118 = bf16[4,512,256]{2,1,0:T(8,128)(2,1)S(1)} collective-permute-done((bf16[4,512,256]{2,1,0:T(8,128)(2,1)}, bf16[4,512,256]{2,1,0:T(8,128)(2,1)S(1)}, u32[]{:S(2)}, u32[]{:S(2)}) %collective-permute-start.118) | collective-permute-done | bytes 1048608 | tf_op jit(solution)/shard_map/ppermute | solution.py:25
  (633 shorter events, 632.1 us)
Async XLA Ops:
  7.2 124.4 %all-gather.7.cloned.1.call-start = ((), (), s32[]{:S(2)}) async-start(), calls=%async_computation.10 | async-start | bytes 5242880 | tf_op jit(solution)/shard_map/all_gather | solution.py:886
  49.5 372.0 %all-gather.9.cloned.1.call-start = ((), (), s32[]{:S(2)}) async-start(), calls=%async_computation.11 | async-start | bytes 5242880 | tf_op jit(solution)/shard_map/all_gather | solution.py:886
  77.0 344.4 %all-gather.11.cloned.1.call-start = ((), (), s32[]{:S(2)}) async-start(), calls=%async_computation.12 | async-start | bytes 5242880 | tf_op jit(solution)/shard_map/all_gather | solution.py:886
  101.3 475.5 %all-gather.13.cloned.1.call-start = ((), (), s32[]{:S(2)}) async-start(), calls=%async_computation.13 | async-start | bytes 5242880 | tf_op jit(solution)/shard_map/all_gather | solution.py:886
  194.9 40.6 %all-to-all-start = ((bf16[1,4,192,256]{3,2,0,1:T(8,128)(2,1)}), bf16[1,4,192,256]{3,2,0,1:T(8,128)(2,1)}, u32[]{:S(2)}, u32[]{:S(2)}) async-start(bf16[1,4,192,256]{3,2,0,1:T(8,128)(2,1)} %maximum_bitcast_fusion.2), calls=%async_computation | async-start | bytes 786432 | tf_op jit(solution)/shard_map/all_to_all | solution.py:734
  199.0 377.8 %all-gather.15.cloned.1.call-start = ((), (), s32[]{:S(2)}) async-start(), calls=%async_computation.14 | async-start | bytes 5242880 | tf_op jit(solution)/shard_map/all_gather | solution.py:886
  200.7 105.5 %collective-permute-start.17 = (s32[2,768,8]{1,2,0:T(8,128)}, s32[2,768,8]{1,2,0:T(8,128)}, u32[]{:S(2)}, u32[]{:S(2)}) collective-permute-start(s32[2,768,8]{1,2,0:T(8,128)} %bitcast.386), channel_id=1, source_target_pairs={{0,16},{16,0},{1,17},{17,1},{2,18},{18,2},{3,19},{19,3},{4,20},{20... | collective-permute-start | bytes 147464 | tf_op jit(solution)/shard_map/ppermute | solution.py:25
  228.1 383.9 %all-gather.17.cloned.1.call-start = ((), (), s32[]{:S(2)}) async-start(), calls=%async_computation.15 | async-start | bytes 5242880 | tf_op jit(solution)/shard_map/all_gather | solution.py:886
  277.8 42.5 %collective-permute-start.18 = (f32[2,768,8]{1,2,0:T(8,128)}, f32[2,768,8]{1,2,0:T(8,128)}, u32[]{:S(2)}, u32[]{:S(2)}) collective-permute-start(f32[2,768,8]{1,2,0:T(8,128)} %bitcast.387), channel_id=1, source_target_pairs={{0,16},{16,0},{1,17},{17,1},{2,18},{18,2},{3,19},{19,3},{4,20},{20... | collective-permute-start | bytes 147464 | tf_op jit(solution)/shard_map/ppermute | solution.py:25
  338.7 82.7 %collective-permute-start.20 = (bf16[2,192,1024]{2,1,0:T(8,128)(2,1)}, bf16[2,192,1024]{2,1,0:T(8,128)(2,1)}, u32[]{:S(2)}, u32[]{:S(2)}) collective-permute-start(bf16[2,192,1024]{2,1,0:T(8,128)(2,1)} %pad_maximum_fusion.6.refs_0_), channel_id=1, source_target_pairs={{0,1},{1,0},{2,3},{3,2},{4,5},{5,4},{6,7},{7,6},{8,9},{9,8},{10,11... | collective-permute-start | bytes 2359304 | tf_op jit(solution)/shard_map/ppermute | solution.py:25
  353.9 65.8 %collective-permute-start.34 = (bf16[256,768]{1,0:T(8,128)(2,1)S(1)}, bf16[256,768]{1,0:T(8,128)(2,1)S(1)}, u32[]{:S(2)}, u32[]{:S(2)}) collective-permute-start(bf16[256,768]{1,0:T(8,128)(2,1)S(1)} %get-tuple-element.90), channel_id=1, source_target_pairs={{0,8},{4,12},{8,0},{12,4},{1,9},{5,13},{9,1},{13,5},{2,10},{6,14},... | collective-permute-start | bytes 1179656 | tf_op jit(solution)/shard_map/ppermute | solution.py:25
  353.9 65.8 %collective-permute-start.33 = (bf16[256,768]{1,0:T(8,128)(2,1)S(1)}, bf16[256,768]{1,0:T(8,128)(2,1)S(1)}, u32[]{:S(2)}, u32[]{:S(2)}) collective-permute-start(bf16[256,768]{1,0:T(8,128)(2,1)S(1)} %get-tuple-element.90), channel_id=1, source_target_pairs={{0,4},{4,8},{8,12},{12,0},{1,5},{5,9},{9,13},{13,1},{2,6},{6,10},{... | collective-permute-start | bytes 1179656 | tf_op jit(solution)/shard_map/ppermute | solution.py:25
  575.2 36.8 %collective-permute-start.51 = (bf16[2,192,1024]{2,1,0:T(8,128)(2,1)S(1)}, bf16[2,192,1024]{2,1,0:T(8,128)(2,1)}, u32[]{:S(2)}, u32[]{:S(2)}) collective-permute-start(bf16[2,192,1024]{2,1,0:T(8,128)(2,1)S(1)} %collective-permute-done.50.refs_2_), channel_id=1, source_target_pairs={{0,1},{1,0},{2,3},{3,2},{4,5},{5,4},{6,7},{7,6},{8,9},{9,8},{10,11... | collective-permute-start | bytes 2359304 | tf_op jit(solution)/shard_map/ppermute | solution.py:25
  645.7 231.0 %reduce-scatter.7.cloned.1.call-start = ((), (), s32[]{:S(2)}) async-start(), calls=%async_computation.16 | async-start | bytes 5242880 | tf_op jit(solution)/shard_map/reduce_scatter | solution.py:945
  735.1 179.6 %reduce-scatter.11.cloned.1.call-start = ((), (), s32[]{:S(2)}) async-start(), calls=%async_computation.18 | async-start | bytes 5242880 | tf_op jit(solution)/shard_map/reduce_scatter | solution.py:945
  735.9 257.3 %reduce-scatter.15.cloned.1.call-start = ((), (), s32[]{:S(2)}) async-start(), calls=%async_computation.20 | async-start | bytes 5242880 | tf_op jit(solution)/shard_map/reduce_scatter | solution.py:945
  750.7 479.1 %reduce-scatter.9.cloned.1.call-start = ((), (), s32[]{:S(2)}) async-start(), calls=%async_computation.17 | async-start | bytes 5242880 | tf_op jit(solution)/shard_map/reduce_scatter | solution.py:945
  876.7 37.9 %collective-permute-start.94 = (bf16[4,256,512]{2,1,0:T(8,128)(2,1)}, bf16[4,256,512]{2,1,0:T(8,128)(2,1)S(1)}, u32[]{:S(2)}, u32[]{:S(2)}) collective-permute-start(bf16[4,256,512]{2,1,0:T(8,128)(2,1)} %reduce-scatter.7.cloned.1.call-done), channel_id=1, source_target_pairs={{0,16},{1,17},{2,18},{3,19},{4,20},{5,21},{6,22},{7,23},{8,24},{9,... | collective-permute-start | bytes 3145736 | tf_op jit(solution)/shard_map/ppermute | solution.py:25
  914.6 316.5 %reduce-scatter.13.cloned.1.call-start = ((), (), s32[]{:S(2)}) async-start(), calls=%async_computation.19 | async-start | bytes 5242880 | tf_op jit(solution)/shard_map/reduce_scatter | solution.py:945
  936.2 350.4 %reduce-scatter.17.cloned.1.call-start = ((), (), s32[]{:S(2)}) async-start(), calls=%async_computation.21 | async-start | bytes 5242880 | tf_op jit(solution)/shard_map/reduce_scatter | solution.py:945
  1066.2 37.6 %collective-permute-start.112 = (bf16[4,256,768]{2,1,0:T(8,128)(2,1)}, bf16[4,256,768]{2,1,0:T(8,128)(2,1)}, u32[]{:S(2)}, u32[]{:S(2)}) collective-permute-start(bf16[4,256,768]{2,1,0:T(8,128)(2,1)} %add_convert_fusion.1), channel_id=1, source_target_pairs={{0,2},{1,3},{2,0},{3,1},{4,6},{5,7},{6,4},{7,5},{8,10},{9,11},{10,... | collective-permute-start | bytes 4718600 | tf_op jit(solution)/shard_map/ppermute | solution.py:25
  1066.5 54.5 %collective-permute-start.104 = (bf16[4,256,768]{2,1,0:T(8,128)(2,1)S(1)}, bf16[4,256,768]{2,1,0:T(8,128)(2,1)}, u32[]{:S(2)}, u32[]{:S(2)}) collective-permute-start(bf16[4,256,768]{2,1,0:T(8,128)(2,1)S(1)} %pad_maximum_fusion.2), channel_id=1, source_target_pairs={{0,1},{1,0},{2,3},{3,2},{4,5},{5,4},{6,7},{7,6},{8,9},{9,8},{10,11... | collective-permute-start | bytes 4718600 | tf_op jit(solution)/shard_map/ppermute | solution.py:25
  1068.2 69.3 %collective-permute-start.106 = (bf16[4,256,768]{2,1,0:T(8,128)(2,1)}, bf16[4,256,768]{2,1,0:T(8,128)(2,1)}, u32[]{:S(2)}, u32[]{:S(2)}) collective-permute-start(bf16[4,256,768]{2,1,0:T(8,128)(2,1)} %add_convert_fusion.4), channel_id=1, source_target_pairs={{0,2},{1,3},{2,0},{3,1},{4,6},{5,7},{6,4},{7,5},{8,10},{9,11},{10,... | collective-permute-start | bytes 4718600 | tf_op jit(solution)/shard_map/ppermute | solution.py:25
  1084.2 70.7 %all-to-all-start.1 = ((bf16[2,1,192,1024]{2,0,1,3:T(2,128)(2,1)}), bf16[2,1,192,1024]{2,0,1,3:T(2,128)(2,1)}, u32[]{:S(2)}, u32[]{:S(2)}) async-start(bf16[2,1,192,1024]{2,0,1,3:T(2,128)(2,1)} %copy.130), calls=%async_computation.1 | async-start | bytes 2097152 | tf_op jit(solution)/shard_map/all_to_all | solution.py:740
  1107.8 46.4 %collective-permute-start.115 = (bf16[256,768]{1,0:T(8,128)(2,1)S(1)}, bf16[256,768]{1,0:T(8,128)(2,1)S(1)}, u32[]{:S(2)}, u32[]{:S(2)}) collective-permute-start(bf16[256,768]{1,0:T(8,128)(2,1)S(1)} %get-tuple-element.246), channel_id=1, source_target_pairs={{0,4},{4,8},{8,12},{12,0},{1,5},{5,9},{9,13},{13,1},{2,6},{6,10},{... | collective-permute-start | bytes 1179656 | tf_op jit(solution)/shard_map/ppermute | solution.py:25
  1117.7 50.4 %collective-permute-start.114 = (bf16[256,768]{1,0:T(8,128)(2,1)}, bf16[256,768]{1,0:T(8,128)(2,1)}, u32[]{:S(2)}, u32[]{:S(2)}) collective-permute-start(bf16[256,768]{1,0:T(8,128)(2,1)} %get-tuple-element.247), channel_id=1, source_target_pairs={{0,8},{4,12},{8,0},{12,4},{1,9},{5,13},{9,1},{13,5},{2,10},{6,14},... | collective-permute-start | bytes 1179656 | tf_op jit(solution)/shard_map/ppermute | solution.py:25
  1121.0 48.6 %collective-permute-start.113 = (bf16[256,768]{1,0:T(8,128)(2,1)}, bf16[256,768]{1,0:T(8,128)(2,1)}, u32[]{:S(2)}, u32[]{:S(2)}) collective-permute-start(bf16[256,768]{1,0:T(8,128)(2,1)} %get-tuple-element.245), channel_id=1, source_target_pairs={{0,12},{4,0},{8,4},{12,8},{1,13},{5,1},{9,5},{13,9},{2,14},{6,2},{... | collective-permute-start | bytes 1179656 | tf_op jit(solution)/shard_map/ppermute | solution.py:25
  1141.0 48.7 %collective-permute-start.109 = (bf16[256,768]{1,0:T(8,128)(2,1)}, bf16[256,768]{1,0:T(8,128)(2,1)}, u32[]{:S(2)}, u32[]{:S(2)}) collective-permute-start(bf16[256,768]{1,0:T(8,128)(2,1)} %get-tuple-element.249), channel_id=1, source_target_pairs={{0,4},{4,8},{8,12},{12,0},{1,5},{5,9},{9,13},{13,1},{2,6},{6,10},{... | collective-permute-start | bytes 1179656 | tf_op jit(solution)/shard_map/ppermute | solution.py:25
  1150.9 64.6 %collective-permute-start.108 = (bf16[256,768]{1,0:T(8,128)(2,1)}, bf16[256,768]{1,0:T(8,128)(2,1)}, u32[]{:S(2)}, u32[]{:S(2)}) collective-permute-start(bf16[256,768]{1,0:T(8,128)(2,1)} %get-tuple-element.250), channel_id=1, source_target_pairs={{0,8},{4,12},{8,0},{12,4},{1,9},{5,13},{9,1},{13,5},{2,10},{6,14},... | collective-permute-start | bytes 1179656 | tf_op jit(solution)/shard_map/ppermute | solution.py:25
  1154.2 61.3 %collective-permute-start.107 = (bf16[256,768]{1,0:T(8,128)(2,1)}, bf16[256,768]{1,0:T(8,128)(2,1)}, u32[]{:S(2)}, u32[]{:S(2)}) collective-permute-start(bf16[256,768]{1,0:T(8,128)(2,1)} %get-tuple-element.248), channel_id=1, source_target_pairs={{0,12},{4,0},{8,4},{12,8},{1,13},{5,1},{9,5},{13,9},{2,14},{6,2},{... | collective-permute-start | bytes 1179656 | tf_op jit(solution)/shard_map/ppermute | solution.py:25
  1229.8 60.1 %collective-permute-start.95 = (bf16[4,256,512]{2,1,0:T(8,128)(2,1)}, bf16[4,256,512]{2,1,0:T(8,128)(2,1)}, u32[]{:S(2)}, u32[]{:S(2)}) collective-permute-start(bf16[4,256,512]{2,1,0:T(8,128)(2,1)} %reduce-scatter.9.cloned.1.call-done), channel_id=1, source_target_pairs={{16,0},{17,1},{18,2},{19,3},{20,4},{21,5},{22,6},{23,7},{24,8},{25... | collective-permute-start | bytes 3145736 | tf_op jit(solution)/shard_map/ppermute | solution.py:25
  1231.1 59.2 %collective-permute-start.102 = (bf16[4,256,512]{2,1,0:T(8,128)(2,1)}, bf16[4,256,512]{2,1,0:T(8,128)(2,1)}, u32[]{:S(2)}, u32[]{:S(2)}) collective-permute-start(bf16[4,256,512]{2,1,0:T(8,128)(2,1)} %reduce-scatter.13.cloned.1.call-done), channel_id=1, source_target_pairs={{16,0},{17,1},{18,2},{19,3},{20,4},{21,5},{22,6},{23,7},{24,8},{25... | collective-permute-start | bytes 3145736 | tf_op jit(solution)/shard_map/ppermute | solution.py:25
  (175 other events, 2948.1 us)
Sparse Core Ops, SparseCore 0:
  49.6 81.9 all-gather.6
  133.1 96.1 all-gather.8
  230.9 91.6 all-gather.10
  324.6 114.5 all-gather.12
  441.2 90.3 all-gather.14
  533.0 79.0 all-gather.16
  735.2 84.9 reduce-scatter.6
  823.2 82.9 reduce-scatter.10
  909.1 78.0 reduce-scatter.14
  989.9 85.6 reduce-scatter.8
  1078.0 120.7 reduce-scatter.12
  1201.0 85.5 reduce-scatter.16

commit v4 on v3

--- a/solution.py
+++ b/solution.py
@@ -46,13 +46,15 @@
     return [blocks[k] for k in range(lax.axis_size("col"))]
 
 
-def scatter_col(blocks):
+def scatter_col(blocks, begun=None):
     blocks = dict(enumerate(blocks))
     total = None
     for bit in col_bits():
         keep = [k for k in blocks if not k & bit]
         total = {k: blocks[k].astype(F32) + flip(blocks[k ^ bit], bit).astype(F32) for k in keep}
         blocks = {k: total[k].astype(BF16) for k in keep}
+        if begun is not None and bit == 1:
+            begun.append(blocks[0])
     return total[0]
 
 
@@ -94,6 +96,14 @@
 
 def after(value, *others):
     return lax.optimization_barrier((value, *others))[0]
+
+
+def needing(value, other):
+    return value + (other.reshape(-1)[0] * 0.0).astype(value.dtype)
+
+
+def behind(kernel, count):
+    return lambda *refs: kernel(*refs[count:])
 
 
 def dot_nn(left, right):
@@ -223,7 +233,7 @@
             outs[k][j] = dot_tn(mixed, dbranch_ref[:, there]).astype(BF16)
 
 
-def whole_call(kernel, out_shape, starts, operands, blocks, lanes, scratch=(), flops=0):
+def whole_call(kernel, out_shape, starts, operands, blocks, lanes, scratch=(), flops=0, ready=()):
     start, count = lanes
     specs = [pl.BlockSpec(memory_space=pltpu.SMEM)]
     specs += [pl.BlockSpec(memory_space=pltpu.VMEM) for _ in operands]
@@ -233,8 +243,9 @@
     specs[1 : 1 + len(operands)] = [
         pl.BlockSpec(o.shape, lambda i, n=o.ndim: (0,) * n) for o in operands
     ]
+    specs = [pl.BlockSpec(memory_space=pl.ANY) for _ in ready] + specs
     return pl.pallas_call(
-        functools.partial(kernel, len(blocks)),
+        behind(functools.partial(kernel, len(blocks)), len(ready)),
         grid=(1,),
         in_specs=specs,
         out_specs=[pl.BlockSpec(o.shape, lambda i, n=len(o.shape): (0,) * n) for o in out_shape],
@@ -246,7 +257,7 @@
             bytes_accessed=8 * 1024 * 1024,
             transcendentals=0,
         ),
-    )(starts, *operands, *blocks)
+    )(*ready, starts, *operands, *blocks)
 
 
 def project(x, gain, cos, sin, part):
@@ -284,16 +295,16 @@
     )
 
 
-def project_back(dq, dkv, x, gain, dsecond, part):
+def project_back(dq, dkv, x, gain, dsecond, part, ready):
     rows, width = x.shape
     shapes = [jax.ShapeDtypeStruct((rows, width), BF16), jax.ShapeDtypeStruct((1, width), F32)]
     return whole_call(
         project_back_kernel, shapes, part["starts"], (dq, dkv, x, gain, dsecond), part["qkv"],
-        (0, 512), [pltpu.VMEM((rows, width), F32)], 4 * rows * width * width,
-    )
-
-
-def weight_back(normed, dq, dkv, mixed, dbranch, part):
+        (0, 512), [pltpu.VMEM((rows, width), F32)], 4 * rows * width * width, ready,
+    )
+
+
+def weight_back(normed, dq, dkv, mixed, dbranch, part, ready=()):
     rows, width = normed.shape
     nblocks = len(part["qkv"])
     nrow, cut = part["qkv"][0].shape[:2]
@@ -301,8 +312,9 @@
     shapes += [jax.ShapeDtypeStruct((nrow, 256, width // nrow), BF16)] * nblocks
     operands = (normed, dq, dkv, mixed, dbranch)
     grads = pl.pallas_call(
-        functools.partial(weight_back_kernel, nblocks),
-        in_specs=[pl.BlockSpec(memory_space=pltpu.SMEM)]
+        behind(functools.partial(weight_back_kernel, nblocks), len(ready)),
+        in_specs=[pl.BlockSpec(memory_space=pl.ANY)] * len(ready)
+        + [pl.BlockSpec(memory_space=pltpu.SMEM)]
         + [pl.BlockSpec(memory_space=pltpu.VMEM)] * len(operands),
         out_specs=[pl.BlockSpec(memory_space=pltpu.VMEM)] * len(shapes),
         out_shape=shapes,
@@ -310,7 +322,7 @@
         cost_estimate=pl.CostEstimate(
             flops=6 * rows * width * width, bytes_accessed=8 * 1024 * 1024, transcendentals=0
         ),
-    )(part["starts"], *operands)
+    )(*ready, part["starts_back"], *operands)
     return grads[:nblocks], grads[nblocks:]
 
 
@@ -432,12 +444,13 @@
     )(qkv, kv, kv, bias, grad, o, lse, cos, sin, kcos, ksin)
 
 
-def chosen_rows(place_ref, weight_ref, m, cap, tokens):
+def chosen_rows(place_ref, m, cap, tokens):
     slots = lax.broadcasted_iota(jnp.int32, (cap, tokens), 0)
-    hit = slots == place_ref[0, m : m + 1, :]
-    pick = jnp.where(hit, 1.0, 0.0)
-    weight = jnp.sum(pick * weight_ref[0, m : m + 1, :], axis=1, keepdims=True)
-    return pick.astype(BF16), weight
+    return jnp.where(slots == place_ref[0, m : m + 1, :], 1.0, 0.0).astype(BF16)
+
+
+def slot_weights(pick, weight_ref, m):
+    return jnp.sum(pick.astype(F32) * weight_ref[0, m : m + 1, :], axis=1, keepdims=True)
 
 
 def load_tokens(pieces, scratch):
@@ -463,184 +476,216 @@
         pl.when(most == 0)(empty)
 
 
-def experts_kernel(ncol, counts_ref, place_ref, weight_ref, *refs):
+def expert_call(kernel, local, operands, specs, outs, scratch, flops, moved, ready=()):
+    def spec(shape, own):
+        zeros = (0,) * (len(shape) - 1)
+        if own:
+            return pl.BlockSpec((1, *shape[1:]), lambda e: (e, *zeros))
+        return pl.BlockSpec(shape, lambda e: (0, *zeros))
+
+    return pl.pallas_call(
+        behind(kernel, len(ready)),
+        grid=(local,),
+        in_specs=[pl.BlockSpec(memory_space=pl.ANY) for _ in ready]
+        + [
+            pl.BlockSpec(memory_space=pltpu.SMEM) if own is None else spec(o.shape, own)
+            for o, own in zip(operands, specs)
+        ],
+        out_specs=[spec(shape, own) for shape, own in outs],
+        out_shape=[jax.ShapeDtypeStruct(shape, BF16) for shape, _ in outs],
+        scratch_shapes=scratch,
+        compiler_params=pltpu.CompilerParams(vmem_limit_bytes=VMEM_LIMIT),
+        cost_estimate=pl.CostEstimate(flops=flops, bytes_accessed=moved, transcendentals=0),
+    )(*ready, *operands)
+
+
+def expert_hidden_kernel(ncol, counts_ref, place_ref, *refs):
     pieces, refs = refs[:ncol], refs[ncol:]
-    gate_ref, up_ref, down_ref, y_ref, chosen_ref, hidden_ref, tokens_ref, total_ref, rows_ref, out_ref = refs
+    gate_ref, up_ref, chosen_ref, hidden_ref, active_ref, tokens_ref, rows_ref = refs
     micro, tokens, _ = tokens_ref.shape
     hidden = gate_ref.shape[2]
-    e = pl.program_id(0)
-
-    @pl.when(e == 0)
+
+    @pl.when(pl.program_id(0) == 0)
+    def _():
+        load_tokens(pieces, tokens_ref)
+
+    def body(cap):
+        for m in range(micro):
+            chosen = dot_nn(chosen_rows(place_ref, m, cap, tokens), tokens_ref[m]).astype(BF16)
+            rows_ref[m * cap : (m + 1) * cap, :] = chosen
+            chosen_ref[0, m, :cap, :] = chosen
+        gate = dot_nn(rows_ref[: micro * cap, :], gate_ref[0])
+        up = dot_nn(rows_ref[: micro * cap, :], up_ref[0])
+        active = (gate * jax.nn.sigmoid(gate) * up).astype(BF16)
+        for m in range(micro):
+            slots = slice(m * cap, (m + 1) * cap)
+            hidden_ref[0, m, :cap, :hidden] = gate[slots].astype(BF16)
+            hidden_ref[0, m, :cap, hidden:] = up[slots].astype(BF16)
+            active_ref[0, m, :cap, :] = active[slots]
+
+    by_load(counts_ref, body)
+
+
+def expert_out_kernel(counts_ref, place_ref, weight_ref, active_ref, down_ref, y_ref, total_ref):
+    micro, tokens, _ = total_ref.shape
+
+    @pl.when(pl.program_id(0) == 0)
+    def _():
+        total_ref[...] = jnp.zeros_like(total_ref)
+
+    def body(cap):
+        active = jnp.concatenate([active_ref[0, m, :cap, :] for m in range(micro)], axis=0)
+        out = dot_nn(active, down_ref[0])
+        for m in range(micro):
+            pick = chosen_rows(place_ref, m, cap, tokens)
+            scaled = (out[m * cap : (m + 1) * cap] * slot_weights(pick, weight_ref, m)).astype(BF16)
+            total_ref[m] += dot_tn(pick, scaled)
+
+    by_load(counts_ref, body)
+
+    @pl.when(pl.program_id(0) == pl.num_programs(0) - 1)
+    def _():
+        store_tokens(y_ref, total_ref)
+
+
+def experts(counts, place, weight, pieces, weights):
+    micro, rows, width = pieces[0].shape
+    gate, up, down = weights
+    local, hidden = gate.shape[0], gate.shape[2]
+    ncol = len(pieces)
+    tokens = ncol * rows
+    slots = local * micro * 256
+    chosen, hid, active = expert_call(
+        functools.partial(expert_hidden_kernel, ncol),
+        local,
+        (counts, place, *pieces, gate, up),
+        (None, True, *[False] * ncol, True, True),
+        [
+            ((local, micro, CAP, width), True),
+            ((local, micro, CAP, 2 * hidden), True),
+            ((local, micro, CAP, hidden), True),
+        ],
+        [pltpu.VMEM((micro, tokens, width), BF16), pltpu.VMEM((micro * CAP, width), BF16)],
+        slots * width * (4 * hidden + 2 * tokens),
+        local * width * (4 * hidden + 4 * micro * CAP),
+    )
+    (y,) = expert_call(
+        expert_out_kernel,
+        local,
+        (counts, place, weight, active, down),
+        (None, True, True, True, True),
+        [((ncol, micro, rows, width), False)],
+        [pltpu.VMEM((micro, tokens, width), F32)],
+        slots * width * (2 * hidden + 2 * tokens),
+        local * width * 2 * hidden + 4 * micro * tokens * width,
+    )
+    return y, chosen, hid
+
+
+def expert_back_kernel(ncol, counts_ref, place_ref, weight_ref, *refs):
+    pieces, refs = refs[:ncol], refs[ncol:]
+    gate_ref, up_ref, down_ref, hidden_ref, dx_ref, dhidden_ref, ddown_ref, *refs = refs
+    tokens_ref, total_ref, rows_ref = refs
+    micro, tokens, _ = tokens_ref.shape
+    hidden = down_ref.shape[1]
+
+    @pl.when(pl.program_id(0) == 0)
     def _():
         load_tokens(pieces, tokens_ref)
         total_ref[...] = jnp.zeros_like(total_ref)
 
     def body(cap):
-        picks, weights = [], []
+        picks = [chosen_rows(place_ref, m, cap, tokens) for m in range(micro)]
         for m in range(micro):
-            pick, weight = chosen_rows(place_ref, weight_ref, m, cap, tokens)
-            chosen = dot_nn(pick, tokens_ref[m]).astype(BF16)
-            rows_ref[m * cap : (m + 1) * cap, :] = chosen
-            chosen_ref[0, m, :cap, :] = chosen
-            picks.append(pick)
-            weights.append(weight)
+            grads = dot_nn(picks[m], tokens_ref[m]) * slot_weights(picks[m], weight_ref, m)
+            rows_ref[m * cap : (m + 1) * cap, :] = grads.astype(BF16)
         used = micro * cap
-        gate = dot_nn(rows_ref[:used, :], gate_ref[0])
-        up = dot_nn(rows_ref[:used, :], up_ref[0])
+        dactive = dot_nt(rows_ref[:used, :], down_ref[0])
+        both = jnp.concatenate([hidden_ref[0, m, :cap, :] for m in range(micro)], axis=0)
+        gate, up = both[:, :hidden].astype(F32), both[:, hidden:].astype(F32)
+        sigmoid = jax.nn.sigmoid(gate)
+        silu = gate * sigmoid
+        dgate = (dactive * up * sigmoid * (1.0 + gate * (1.0 - sigmoid))).astype(BF16)
+        dup = (dactive * silu).astype(BF16)
         for m in range(micro):
-            hidden_ref[0, m, :cap, :hidden] = gate[m * cap : (m + 1) * cap].astype(BF16)
-            hidden_ref[0, m, :cap, hidden:] = up[m * cap : (m + 1) * cap].astype(BF16)
-        active = (gate * jax.nn.sigmoid(gate) * up).astype(BF16)
-        scale = jnp.concatenate(weights, axis=0)
-        out_ref[:used, :] = (dot_nn(active, down_ref[0]) * scale).astype(BF16)
+            dhidden_ref[0, m, :cap, :hidden] = dgate[m * cap : (m + 1) * cap]
+            dhidden_ref[0, m, :cap, hidden:] = dup[m * cap : (m + 1) * cap]
+        ddown_ref[0] = dot_tn((silu * up).astype(BF16), rows_ref[:used, :]).astype(BF16)
+        out = (dot_nt(dgate, gate_ref[0]) + dot_nt(dup, up_ref[0])).astype(BF16)
         for m in range(micro):
-            total_ref[m] += dot_tn(picks[m], out_ref[m * cap : (m + 1) * cap, :])
-
-    by_load(counts_ref, body)
-
-    @pl.when(e == pl.num_programs(0) - 1)
+            total_ref[m] += dot_tn(picks[m], out[m * cap : (m + 1) * cap])
+
+    def empty():
+        ddown_ref[...] = jnp.zeros_like(ddown_ref)
+
+    by_load(counts_ref, body, empty)
+
+    @pl.when(pl.program_id(0) == pl.num_programs(0) - 1)
     def _():
-        store_tokens(y_ref, total_ref)
-
-
-def expert_specs(pieces, weights, slots):
+        store_tokens(dx_ref, total_ref)
+
+
+def expert_weight_back_kernel(counts_ref, chosen_ref, dhidden_ref, dgate_ref, dup_ref):
+    micro = chosen_ref.shape[1]
+    hidden = dgate_ref.shape[2]
+
+    def body(cap):
+        rows = jnp.concatenate([chosen_ref[0, m, :cap, :] for m in range(micro)], axis=0)
+        both = jnp.concatenate([dhidden_ref[0, m, :cap, :] for m in range(micro)], axis=0)
+        grads = dot_tn(rows, both).astype(BF16)
+        dgate_ref[0] = grads[:, :hidden]
+        dup_ref[0] = grads[:, hidden:]
+
+    def empty():
+        dgate_ref[...] = jnp.zeros_like(dgate_ref)
+        dup_ref[...] = jnp.zeros_like(dup_ref)
+
+    by_load(counts_ref, body, empty)
+
+
+def experts_back(counts, place, weight, pieces, weights, hid):
     micro, rows, width = pieces[0].shape
-    at_expert = lambda e: (e, 0, 0)
-    specs = [
-        pl.BlockSpec(memory_space=pltpu.SMEM),
-        pl.BlockSpec((1, *slots.shape[1:]), at_expert),
-        pl.BlockSpec((1, *slots.shape[1:]), at_expert),
-    ]
-    specs += [pl.BlockSpec((micro, rows, width), lambda e: (0, 0, 0)) for _ in pieces]
-    specs += [pl.BlockSpec((1, *w.shape[1:]), at_expert) for w in weights]
-    return specs
-
-
-def experts(counts, place, weight, pieces, weights):
-    micro, rows, width = pieces[0].shape
-    local, hidden = weights[0].shape[0], weights[0].shape[2]
+    gate, up, down = weights
+    local, hidden = gate.shape[0], gate.shape[2]
     ncol = len(pieces)
     tokens = ncol * rows
-    at_expert = lambda e: (e, 0, 0, 0)
-    return pl.pallas_call(
-        functools.partial(experts_kernel, ncol),
-        grid=(local,),
-        in_specs=expert_specs(pieces, weights, place),
-        out_specs=[
-            pl.BlockSpec((ncol, micro, rows, width), lambda e: (0, 0, 0, 0)),
-            pl.BlockSpec((1, micro, CAP, width), at_expert),
-            pl.BlockSpec((1, micro, CAP, 2 * hidden), at_expert),
+    slots = local * micro * 256
+    dx, dhid, ddown = expert_call(
+        functools.partial(expert_back_kernel, ncol),
+        local,
+        (counts, place, weight, *pieces, gate, up, down, hid),
+        (None, True, True, *[False] * ncol, True, True, True, True),
+        [
+            ((ncol, micro, rows, width), False),
+            ((local, micro, CAP, 2 * hidden), True),
+            (down.shape, True),
         ],
-        out_shape=[
-            jax.ShapeDtypeStruct((ncol, micro, rows, width), BF16),
-            jax.ShapeDtypeStruct((local, micro, CAP, width), BF16),
-            jax.ShapeDtypeStruct((local, micro, CAP, 2 * hidden), BF16),
-        ],
-        scratch_shapes=[
+        [
             pltpu.VMEM((micro, tokens, width), BF16),
             pltpu.VMEM((micro, tokens, width), F32),
             pltpu.VMEM((micro * CAP, width), BF16),
-            pltpu.VMEM((micro * CAP, width), BF16),
         ],
-        compiler_params=pltpu.CompilerParams(vmem_limit_bytes=VMEM_LIMIT),
-        cost_estimate=pl.CostEstimate(
-            flops=local * micro * 256 * width * (6 * hidden + 4 * tokens),
-            bytes_accessed=local * width * (6 * hidden + 4 * micro * CAP),
-            transcendentals=local * micro * CAP * hidden,
-        ),
-    )(counts, place, weight, *pieces, *weights)
-
-
-def experts_back_kernel(ncol, counts_ref, place_ref, weight_ref, *refs):
-    pieces, refs = refs[:ncol], refs[ncol:]
-    gate_ref, up_ref, down_ref, chosen_ref, hidden_ref, dx_ref, dgate_ref, dup_ref, ddown_ref, *refs = refs
-    tokens_ref, total_ref, rows_ref, out_ref, dhid_ref = refs
-    micro, tokens, _ = tokens_ref.shape
-    hidden = gate_ref.shape[2]
-    e = pl.program_id(0)
-
-    @pl.when(e == 0)
-    def _():
-        load_tokens(pieces, tokens_ref)
-        total_ref[...] = jnp.zeros_like(total_ref)
-
-    def body(cap):
-        picks = []
-        for m in range(micro):
-            pick, weight = chosen_rows(place_ref, weight_ref, m, cap, tokens)
-            picks.append(pick)
-            rows_ref[m * cap : (m + 1) * cap, :] = (
-                dot_nn(pick, tokens_ref[m]) * weight
-            ).astype(BF16)
-        used = micro * cap
-        dactive = dot_nt(rows_ref[:used, :], down_ref[0])
-        gate = jnp.concatenate([hidden_ref[0, m, :cap, :hidden] for m in range(micro)], axis=0)
-        up = jnp.concatenate([hidden_ref[0, m, :cap, hidden:] for m in range(micro)], axis=0)
-        gate, up = gate.astype(F32), up.astype(F32)
-        sigmoid = jax.nn.sigmoid(gate)
-        silu = gate * sigmoid
-        dhid_ref[:used, :hidden] = (dactive * up * sigmoid * (1.0 + gate * (1.0 - sigmoid))).astype(
-            BF16
-        )
-        dhid_ref[:used, hidden:] = (dactive * silu).astype(BF16)
-        dgate, dup = dhid_ref[:used, :hidden], dhid_ref[:used, hidden:]
-        out_ref[:used, :] = (dot_nt(dgate, gate_ref[0]) + dot_nt(dup, up_ref[0])).astype(BF16)
-        for m in range(micro):
-            total_ref[m] += dot_tn(picks[m], out_ref[m * cap : (m + 1) * cap, :])
-        active = (silu * up).astype(BF16)
-        for m in range(micro):
-            out_ref[m * cap : (m + 1) * cap, :] = chosen_ref[0, m, :cap, :]
-        dgate_ref[0] = dot_tn(out_ref[:used, :], dgate).astype(BF16)
-        dup_ref[0] = dot_tn(out_ref[:used, :], dup).astype(BF16)
-        ddown_ref[0] = dot_tn(active, rows_ref[:used, :]).astype(BF16)
-
-    def empty():
-        for ref in (dgate_ref, dup_ref, ddown_ref):
-            ref[...] = jnp.zeros_like(ref)
-
-    by_load(counts_ref, body, empty)
-
-    @pl.when(e == pl.num_programs(0) - 1)
-    def _():
-        store_tokens(dx_ref, total_ref)
-
-
-def experts_back(counts, place, weight, pieces, weights, chosen, hid):
-    micro, rows, width = pieces[0].shape
-    local, hidden = weights[0].shape[0], weights[0].shape[2]
-    ncol = len(pieces)
-    tokens = ncol * rows
-    at_expert = lambda e: (e, 0, 0, 0)
-    return pl.pallas_call(
-        functools.partial(experts_back_kernel, ncol),
-        grid=(local,),
-        in_specs=[
-            *expert_specs(pieces, weights, place),
-            pl.BlockSpec((1, micro, CAP, width), at_expert),
-            pl.BlockSpec((1, micro, CAP, 2 * hidden), at_expert),
-        ],
-        out_specs=[
-            pl.BlockSpec((ncol, micro, rows, width), lambda e: (0, 0, 0, 0)),
-            *[pl.BlockSpec((1, *w.shape[1:]), lambda e: (e, 0, 0)) for w in weights],
-        ],
-        out_shape=[
-            jax.ShapeDtypeStruct((ncol, micro, rows, width), BF16),
-            *[jax.ShapeDtypeStruct(w.shape, BF16) for w in weights],
-        ],
-        scratch_shapes=[
-            pltpu.VMEM((micro, tokens, width), BF16),
-            pltpu.VMEM((micro, tokens, width), F32),
-            pltpu.VMEM((micro * CAP, width), BF16),
-            pltpu.VMEM((micro * CAP, width), BF16),
-            pltpu.VMEM((micro * CAP, 2 * hidden), BF16),
-        ],
-        compiler_params=pltpu.CompilerParams(vmem_limit_bytes=VMEM_LIMIT),
-        cost_estimate=pl.CostEstimate(
-            flops=local * micro * 256 * width * (12 * hidden + 4 * tokens),
-            bytes_accessed=local * width * (12 * hidden + 4 * micro * CAP),
-            transcendentals=local * micro * CAP * hidden,
-        ),
-    )(counts, place, weight, *pieces, *weights, chosen, hid)
+        slots * width * (8 * hidden + 4 * tokens),
+        local * width * (8 * hidden + 2 * micro * CAP),
+    )
+    return dx, dhid, ddown
+
+
+def expert_weights_back(counts, chosen, dhid, weights, ready):
+    gate, up, _ = weights
+    local, width, hidden = gate.shape
+    micro = chosen.shape[1]
+    return expert_call(
+        expert_weight_back_kernel,
+        local,
+        (counts, chosen, dhid),
+        (None, True, True),
+        [(gate.shape, True), (up.shape, True)],
+        [],
+        local * micro * 256 * width * 4 * hidden,
+        local * width * (4 * hidden + 4 * micro * CAP),
+        ready,
+    )
 
 
 def spread_rows(value):
@@ -648,9 +693,9 @@
     return gather_col(both)
 
 
-def collect_rows(partial):
+def collect_rows(partial, begun=None):
     blocks = [partial[k] for k in range(partial.shape[0])]
-    theirs = exchange(scatter_col([b[1] for b in blocks]).astype(BF16))
+    theirs = exchange(scatter_col([b[1] for b in blocks], begun).astype(BF16))
     return scatter_col([b[0] for b in blocks]) + theirs.astype(F32)
 
 
@@ -675,22 +720,20 @@
         "mixed": mixed,
         "lse": lse,
         "second": second,
-        "pieces": pieces[-1],
         "chosen": chosen,
         "hid": hid,
     }
     return result, keep
 
 
-def backward_layer(grad_result, keep, env, part):
+def backward_layer(grad_result, pieces, keep, env, part, before_projections=()):
     rows, _ = grad_result.shape
     prompt = env["prompt"]
     ncol, nrow = lax.axis_size("col"), lax.axis_size("row")
-    pieces = spread_rows(grad_result.astype(BF16))
-    partial, *expert_grads = experts_back(
-        *part["slots"], pieces, part["experts"], keep["chosen"], keep["hid"]
-    )
-    dn2 = collect_rows(partial)
+    partial, dhid, ddown = experts_back(*part["slots"], pieces, part["experts"], keep["hid"])
+    begun = []
+    dn2 = collect_rows(partial, begun)
+    dgate, dup = expert_weights_back(part["slots"][0], keep["chosen"], dhid, part["experts"], begun)
     dsecond, dbranch, dmixed, gain_second = open_back(
         grad_result, dn2, keep["second"], part["gain_second"], part
     )
@@ -706,12 +749,11 @@
         parts.append(own[at : at + prompt].astype(BF16))
     own = jnp.concatenate([scatter_row(parts), own[prompt:rows]], axis=0).astype(BF16)
     grad_in, gain_first = project_back(
-        dq[0], own, keep["layer_in"], part["gain_first"], dsecond, part
-    )
-    small = weight_back(keep["normed"], dq[0], own, keep["mixed"][0], dbranch, part)
+        dq[0], own, keep["layer_in"], part["gain_first"], dsecond, part, before_projections
+    )
     return grad_in, {
-        "small": small,
-        "experts": expert_grads,
+        "small": (keep["normed"], dq[0], own, keep["mixed"][0], dbranch, part),
+        "experts": (dgate, dup, ddown),
         "gain_first": gain_first[0],
         "gain_second": gain_second[0],
     }
@@ -736,16 +778,16 @@
 
 def to_columns(value, prompt):
     micro, _, width = value.shape
-    ncol = lax.axis_size("col")
-    split = lax.all_to_all(value[:, None], "col", 3, 1, tiled=True)
+    ncol, col = lax.axis_size("col"), lax.axis_index("col")
     shard = width // ncol
-    return jnp.concatenate(
-        [
-            split[:, :, :prompt].reshape(micro, -1, shard),
-            split[:, :, prompt:].reshape(micro, -1, shard),
-        ],
-        axis=1,
-    )
+    blocks = []
+    for k in range(ncol):
+        block = lax.dynamic_slice_in_dim(value, (col ^ k) * shard, shard, 2)
+        blocks.append(flip(block, k) if k else block)
+    blocks = jnp.stack(blocks)
+    blocks = [lax.dynamic_index_in_dim(blocks, col ^ c, 0, False) for c in range(ncol)]
+    parts = [b[:, :prompt] for b in blocks] + [b[:, prompt:] for b in blocks]
+    return jnp.concatenate(parts, axis=1)
 
 
 def turn_tables(positions):
@@ -759,22 +801,24 @@
     )
 
 
-def small_weights(packed, w_rows, early):
-    nrow, ncol = lax.axis_size("row"), lax.axis_size("col")
-    row, col = lax.axis_index("row"), lax.axis_index("col")
-    cut = packed.shape[0]
-    starts = ((row - jnp.arange(nrow, dtype=jnp.int32)) % nrow) * cut
-    if early:
-        pieces = [packed]
-        for _ in range(nrow - 1):
-            pieces.append(ring(pieces[-1]))
-    else:
-        pieces = gather_row(packed)
-    blocks = gather_col(jnp.stack(pieces))
+def small_weights(rows, w_rows):
+    nrow, cut = rows.shape[:2]
+    ncol, row, col = lax.axis_size("col"), lax.axis_index("row"), lax.axis_index("col")
+    index = jnp.arange(nrow, dtype=jnp.int32)
+    blocks = gather_col(rows)
+
+    def result(qkv, out, lanes, order):
+        return {
+            "starts": jnp.concatenate([index * cut, order]),
+            "starts_back": jnp.concatenate([((row - index) % nrow) * cut, order]),
+            "qkv": qkv,
+            "out": out,
+            "out_lanes": lanes,
+        }
+
     if w_rows == 256:
         order = (col ^ jnp.arange(ncol, dtype=jnp.int32)) * 256
-        lanes = (512, 256)
-        return {"starts": jnp.concatenate([starts, order]), "qkv": blocks, "out": blocks, "out_lanes": lanes}
+        return result(blocks, blocks, (512, 256), order)
     blocks = jnp.stack(blocks)
     whole = [lax.dynamic_index_in_dim(blocks, col ^ c, 0, False) for c in range(ncol)]
     qkv, out = [], []
@@ -784,8 +828,7 @@
         qkv.append(jnp.concatenate(heads + others, axis=2))
         a, b = a[..., 256:], b[..., 256:]
         out.append(jnp.concatenate([a[:, :64], b[:, :64], a[:, 64:], b[:, 64:]], axis=1))
-    order = jnp.arange(len(qkv), dtype=jnp.int32) * 256
-    return {"starts": jnp.concatenate([starts, order]), "qkv": qkv, "out": out, "out_lanes": (0, cut)}
+    return result(qkv, out, (0, cut), jnp.arange(len(qkv), dtype=jnp.int32) * 256)
 
 
 def pack_weights(w_query, w_key, w_value, w_out):
@@ -797,9 +840,8 @@
     return jnp.concatenate([w_query, w_key, w_value, w_out], axis=1)
 
 
-def small_gradients(qkv, out, w_rows):
-    nrow, ncol = lax.axis_size("row"), lax.axis_size("col")
-    col = lax.axis_index("col")
+def col_gradients(qkv, out, w_rows, begun=None):
+    ncol, col = lax.axis_size("col"), lax.axis_index("col")
     if w_rows == 256:
         blocks = [jnp.concatenate([a, b], axis=2) for a, b in zip(qkv, out)]
     else:
@@ -814,8 +856,7 @@
                 whole.append(jnp.concatenate([*heads, rows], axis=2))
         whole = jnp.stack(whole)
         blocks = [lax.dynamic_index_in_dim(whole, col ^ k, 0, False) for k in range(ncol)]
-    mine = scatter_col(blocks).astype(BF16)
-    return scatter_row([mine[j] for j in range(nrow)]).astype(BF16)
+    return scatter_col(blocks, begun).astype(BF16)
 
 
 def routing(ids, scale, prompt_rows, first, local):
@@ -874,7 +915,11 @@
     w_rows = w_out.shape[1]
     packed = by_layer(pack_weights(w_query[0], w_key[0], w_value[0], w_out[0]))
     big = [w[0] for w in (w_gate, w_up, w_down)]
-    crossed = [exchange(after(w[half:], packed[0])) for w in big]
+    over_row = lambda v: lax.all_gather(v, "row", axis=0)
+    small_first = over_row(packed[0])
+    crossed = [exchange(after(big[0][half:], packed[0]))]
+    for w in big[1:]:
+        crossed.append(exchange(after(w[half:], crossed[-1])))
     shards = [
         [jnp.where(is_home, w[:half], c) for w, c in zip(big, crossed)] for is_home in home
     ]
@@ -897,10 +942,13 @@
             "slots": routing(ids, scale, prompt_rows, first, half),
         }
 
+    shards[0] = [after(w, small_first) for w in shards[0]]
     parts = [layer_part(0, whole(shards[0]))]
-    parts[0].update(small_weights(packed[0], w_rows, True))
-    later = lax.optimization_barrier((shards[1], parts[0]["experts"][0]))[0]
-    parts.append(layer_part(1, whole(later)))
+    parts[0].update(small_weights(small_first, w_rows))
+    held = parts[0]["experts"]
+    small_later = over_row(after(packed[1], held[0]))
+    parts.append(layer_part(1, whole(lax.optimization_barrier((shards[1], held[2]))[0])))
+    parts[1].update(small_weights(small_later, w_rows))
 
     def prompt_positions(row_index, col_index):
         return row_index * prompt_rows + col_index * prompt + jnp.arange(prompt, dtype=jnp.int32)
@@ -925,7 +973,6 @@
 
     result, keep_first = forward_layer(first_in, env, parts[0])
     mid = result.astype(BF16)
-    parts[1].update(small_weights(after(packed[1], keep_first["pieces"]), w_rows, False))
     final, keep_last = forward_layer(mid, env, parts[1])
 
     count = (micro * prompt_len + jnp.sum(lengths)).astype(F32)
@@ -935,8 +982,18 @@
     loss = jnp.sum(diff * diff) / count
     dfinal = (2.0 / count) * diff
 
-    dmid, last_grads = backward_layer(dfinal, keep_last, env, parts[1])
-    dx, first_grads = backward_layer(dmid, keep_first, env, parts[0])
+    def both_micros(first, last):
+        received = exchange(jnp.where(home[0], last, first))
+        pair = jnp.where(home[0], jnp.stack([first, received]), jnp.stack([received, last]))
+        return to_columns(pair, prompt)
+
+    outputs = both_micros(mid, final.astype(BF16))
+    dfinal_pieces = spread_rows(dfinal.astype(BF16))
+    dmid, last_grads = backward_layer(dfinal, dfinal_pieces, keep_last, env, parts[1])
+    dmid_pieces = spread_rows(dmid)
+    small_last = col_gradients(*weight_back(*last_grads["small"], dmid_pieces[-1:]), w_rows)
+    small_last = small_last, shift(small_last, "section", [(0, 1)])
+    dx, first_grads = backward_layer(dmid, dmid_pieces, keep_first, env, parts[0], small_last)
 
     layer_grads = [first_grads, last_grads]
 
@@ -944,25 +1001,24 @@
         grad = after(layer_grads[layer]["experts"][j], *earlier)
         return lax.psum_scatter(grad, "row", scatter_dimension=(1, 1, 2)[j], tiled=True)
 
-    returned = []
+    order = (2, 0, 1)
+    sums_last = [over_rows(j, 1) for j in order]
+    back_last = [shift(g, "section", [(0, 1)]) for g in sums_last]
+    sums_first = [over_rows(j, 0, back) for j, back in zip(order, back_last)]
+    back_first = [shift(g, "section", [(1, 0)]) for g in sums_first]
 
     def expert_gradient(j):
-        last = over_rows(j, 1)
-        back = shift(last, "section", [(0, 1)])
-        first = over_rows(j, 0, back)
-        returned.append(shift(first, "section", [(1, 0)]))
-        own = jnp.where(home[0], first, last)
-        other = jnp.where(home[0], returned[-1], back)
+        at = order.index(j)
+        own = jnp.where(home[0], sums_first[at], sums_last[at])
+        other = jnp.where(home[0], back_first[at], back_last[at])
         return jnp.concatenate([own, other], axis=0).astype(F32)
 
     grad_gate, grad_up, grad_down = (expert_gradient(j) for j in range(3))
-    small = [small_gradients(*grads["small"], w_rows) for grads in layer_grads]
-
-    def at_home(first, last):
-        received = exchange(jnp.where(home[0], last, first))
-        return jnp.where(home[0], first, last).astype(F32) + received.astype(F32)
-
-    small = at_home(*small)
+    small_first = col_gradients(*weight_back(*first_grads["small"], back_first[:1]), w_rows)
+    small_first = small_first, shift(small_first, "section", [(1, 0)])
+    small = [a.astype(F32) + b.astype(F32) for a, b in (small_first, small_last)]
+    small = jnp.where(home[0], *small).astype(BF16)
+    small = scatter_row([small[j] for j in range(nrow)])
     grad_query, grad_out = small[:, :columns], small[:, columns + 2 * kcols :]
     if w_rows == 256:
         heads = lambda v: [v[:, :64], v[:, 128:192], v[:, 64:128], v[:, 192:]]
@@ -974,19 +1030,13 @@
         [g[name] for g in layer_grads for name in ("gain_first", "gain_second")]
         + [jnp.broadcast_to(loss, (128,))]
     )
-    tally = total_everywhere(after(tally, returned[0]))
+    tally = total_everywhere(tally)
     loss = tally[4 * width]
     gains = tally[: 4 * width].reshape(2, 2, width)
     gains = jnp.where(home[0], gains[0], gains[1])
     gains = lax.dynamic_slice_in_dim(gains, col * shard, shard, 1)
 
-    def both_micros(first, last):
-        received = exchange(jnp.where(home[0], last, first))
-        pair = jnp.where(home[0], jnp.stack([first, received]), jnp.stack([received, last]))
-        return to_columns(pair, prompt)
-
-    outputs = both_micros(mid, final.astype(BF16))
-    input_grads = both_micros(after(dx, returned[1]), dmid)
+    input_grads = both_micros(dx, dmid)
     return (
         outputs[None, :, None],
         loss,

time: 1360 us -> 1290 us (0.949)
  starting transfers between devices: 204 us -> 155 us
  waiting for transfers between devices: 752 us -> 716 us
  Pallas kernels: 215 us -> 234 us
  local copies, waits for them, and re-layouts: 70.6 us -> 53.5 us
    ppermute x119 -> x117, waiting for transfers between devices: 627 us -> 502 us  [shift(): return lax.ppermute(value, axis, pairs)]
    all_gather x6, waiting for transfers between devices: 65.4 us -> 164 us  [whole(): lax.all_gather(w, 'row', axis=axis, tiled=True)]
    ppermute x119 -> x117, starting transfers between devices: 187 us -> 147 us  [shift(): return lax.ppermute(value, axis, pairs)]
    pallas_call x14 -> x18, Pallas kernels: 157 us -> 175 us  [the longest x8 127 us: expert_call(): pl.pallas_call(behind(kernel, len(ready)), grid=(local,), in_specs=[pl.Bl...]
    reduce_scatter x6, waiting for transfers between devices: 52.6 us -> 36.1 us  [over_rows(): lax.psum_scatter(grad, 'row', scatter_dimension=(1, 1, 2)[j], tiled=True)]
  transfers between devices with their start and end apart: 135 -> 133, of which waited for: 66 -> 69; matrix products, arithmetic and copies ran while one was open for 11% -> 10% of each run, Pallas kernels for 12% -> 15%
where the time goes in v4:
time: 1290 us; the launch traced here: 1280 us
  waiting for transfers between devices  716 us (56%)
  Pallas kernels  234 us (18%)
  starting transfers between devices  155 us (12%)
  other arithmetic  105 us (8%)
  local copies, waits for them, and re-layouts  53.5 us (4%)
  between operations  17.2 us (1%)
    ppermute x117, waiting for transfers between devices, shift(): return lax.ppermute(value, axis, pairs)  502 us
    all_gather x6, waiting for transfers between devices, whole(): lax.all_gather(w, 'row', axis=axis, tiled=True)  164 us
    ppermute x117, starting transfers between devices, shift(): return lax.ppermute(value, axis, pairs)  147 us
    pallas_call x8, Pallas kernels, expert_call(): pl.pallas_call(behind(kernel, len(ready)), grid=(local,), in_specs=[pl.Bl...  127 us
    pallas_call x8, Pallas kernels, whole_call(): pl.pallas_call(behind(functools.partial(kernel, len(blocks)), len(ready))...  36.7 us
    reduce_scatter x6, waiting for transfers between devices, over_rows(): lax.psum_scatter(grad, 'row', scatter_dimension=(1, 1, 2)[j], tiled=True)  36.1 us
    pallas_call x2, Pallas kernels, attend_back(): pl.pallas_call(attend_back_kernel, grid=(micro, groups), in_specs=[mine,...  36.1 us
  transfers between devices with their start and end apart: 133, of which 69 were waited for; matrix products, arithmetic and copies ran while one was open for 10% of the time, Pallas kernels for 15%

profile of v4, /device:TPU:0, one launch (start us, length us, event | category | flops | bytes accessed | tf_op | source)
XLA Modules:
  0.0 1281.3 jit_solution(17247926979986580293)
XLA Ops:
  25.3 22.6 %collective-permute-done.20 = bf16[4,256,512]{2,1,0:T(8,128)(2,1)S(1)} collective-permute-done((bf16[4,256,512]{2,1,0:T(8,128)(2,1)S(1)}, bf16[4,256,512]{2,1,0:T(8,128)(2,1)S(1)}, u32[]{:S(2)}, u32[]{:S(2)}) %collective-permute-start.20) | collective-permute-done | bytes 1048608 | tf_op jit(solution)/shard_map/ppermute | solution.py:25
  49.4 12.7 all-gather.23.cloned.1.call-done
  66.3 22.0 %collective-permute-done.21 = bf16[4,256,512]{2,1,0:T(8,128)(2,1)S(1)} collective-permute-done((bf16[4,256,512]{2,1,0:T(8,128)(2,1)S(1)}, bf16[4,256,512]{2,1,0:T(8,128)(2,1)S(1)}, u32[]{:S(2)}, u32[]{:S(2)}) %collective-permute-start.21) | collective-permute-done | bytes 1048608 | tf_op jit(solution)/shard_map/ppermute | solution.py:25
  89.8 22.5 %collective-permute-done.22 = bf16[4,512,256]{2,1,0:T(8,128)(2,1)S(1)} collective-permute-done((bf16[4,512,256]{2,1,0:T(8,128)(2,1)S(1)}, bf16[4,512,256]{2,1,0:T(8,128)(2,1)S(1)}, u32[]{:S(2)}, u32[]{:S(2)}) %collective-permute-start.22) | collective-permute-done | bytes 1048608 | tf_op jit(solution)/shard_map/ppermute | solution.py:25
  113.9 30.0 %all-gather.11.cloned.1.call-done.refs_6_.refs_7_ = bf16[4,1024,512]{2,1,0:T(8,128)(2,1)} async-done(((bf16[4,256,512]{2,1,0:T(8,128)(2,1)}), bf16[4,1024,512]{2,1,0:T(8,128)(2,1)}) %all-gather.11.cloned.1.call-update) | async-done | bytes 4194320 | tf_op jit(solution)/shard_map/all_gather | solution.py:931
  146.7 78.4 %all-gather.15.cloned.1.call-done.refs_4_.refs_9_ = bf16[4,512,1024]{2,1,0:T(8,128)(2,1)} async-done(((bf16[4,512,256]{2,1,0:T(8,128)(2,1)}), bf16[4,512,1024]{2,1,0:T(8,128)(2,1)}) %all-gather.15.cloned.1.call-update) | async-done | bytes 4194320 | tf_op jit(solution)/shard_map/all_gather | solution.py:931
  245.5 27.1 %collective-permute-done.3.refs_7_.refs_6_.refs_10_ = bf16[4,256,768]{2,1,0:T(8,128)(2,1)S(1)} collective-permute-done((bf16[4,256,768]{2,1,0:T(8,128)(2,1)S(1)}, bf16[4,256,768]{2,1,0:T(8,128)(2,1)S(1)}, u32[]{:S(2)}, u32[]{:S(2)}) %collective-permute-start.3) | collective-permute-done | bytes 1572896 | tf_op jit(solution)/shard_map/ppermute | solution.py:25
  330.0 11.4 shard_map.230
  361.9 14.3 %collective-permute-done.18.refs_4_ = bf16[2,192,1024]{2,1,0:T(8,128)(2,1)S(1)} collective-permute-done((bf16[2,192,1024]{2,1,0:T(8,128)(2,1)S(1)}, bf16[2,192,1024]{2,1,0:T(8,128)(2,1)S(1)}, u32[]{:S(2)}, u32[]{:S(2)}) %collective-permute-start.18) | collective-permute-done | bytes 786464 | tf_op jit(solution)/shard_map/ppermute | solution.py:25
  379.5 14.6 %shard_map.232 = (bf16[4,2,384,1024]{3,2,1,0:T(8,128)(2,1)}, bf16[4,2,384,1024]{3,2,1,0:T(8,128)(2,1)}, bf16[4,2,384,512]{3,2,1,0:T(8,128)(2,1)}) custom-call(s32[8]{0:T(128)} %reshape_squeeze.6.refs_0_.refs_1_, s32[4,2,768]{2,1,0:T(2,128)} %add_select_fusion.1.refs_1_, bf16[2,192,1024]{2,1,0:T(8,128)(2,1)} %copy-done.35, ...), custom_call_target="tpu_custom_call" | custom-call | flops 7516192768 | bytes 20971520 | tf_op jit(solution)/shard_map/pallas_call | solution.py:486
  394.0 10.6 shard_map.233
  419.1 10.0 collective-permute-done.28
  487.7 11.7 shard_map.235
  518.8 15.7 %collective-permute-done.44.refs_4_ = bf16[2,192,1024]{2,1,0:T(8,128)(2,1)S(1)} collective-permute-done((bf16[2,192,1024]{2,1,0:T(8,128)(2,1)S(1)}, bf16[2,192,1024]{2,1,0:T(8,128)(2,1)S(1)}, u32[]{:S(2)}, u32[]{:S(2)}) %collective-permute-start.44) | collective-permute-done | bytes 786464 | tf_op jit(solution)/shard_map/ppermute | solution.py:25
  536.9 15.4 %shard_map.237 = (bf16[4,2,384,1024]{3,2,1,0:T(8,128)(2,1)}, bf16[4,2,384,1024]{3,2,1,0:T(8,128)(2,1)}, bf16[4,2,384,512]{3,2,1,0:T(8,128)(2,1)}) custom-call(s32[8]{0:T(128)} %reshape_squeeze.7.refs_0_.refs_1_, s32[4,2,768]{2,1,0:T(2,128)} %add_select_fusion.refs_1_, bf16[2,192,1024]{2,1,0:T(8,128)(2,1)} %copy-done.34, bf16[2,192,1024]{2,1,0:T(8,128)(2,1)} %copy-done.59, ...), custom_call_target="tpu_custom_call" | custom-call | flops 7516192768 | bytes 20971520 | tf_op jit(solution)/shard_map/pallas_call | solution.py:486
  552.2 55.6 %all-gather.21.cloned.1.call-done.refs_4_.refs_9_ = bf16[4,512,1024]{2,1,0:T(8,128)(2,1)} async-done(((bf16[4,512,256]{2,1,0:T(8,128)(2,1)}), bf16[4,512,1024]{2,1,0:T(8,128)(2,1)}) %all-gather.21.cloned.1.call-update) | async-done | bytes 4194320 | tf_op jit(solution)/shard_map/all_gather | solution.py:931
  607.8 11.8 shard_map.238
  666.5 17.1 %collective-permute-done.59.refs_5_ = bf16[2,192,1024]{2,1,0:T(8,128)(2,1)S(1)} collective-permute-done((bf16[2,192,1024]{2,1,0:T(8,128)(2,1)S(1)}, bf16[2,192,1024]{2,1,0:T(8,128)(2,1)S(1)}, u32[]{:S(2)}, u32[]{:S(2)}) %collective-permute-start.59) | collective-permute-done | bytes 786464 | tf_op jit(solution)/shard_map/ppermute | solution.py:25
  686.7 28.6 %shard_map.239 = (bf16[4,2,192,1024]{3,2,1,0:T(8,128)(2,1)}, bf16[4,2,384,1024]{3,2,1,0:T(8,128)(2,1)}, bf16[4,512,1024]{2,1,0:T(8,128)(2,1)}) custom-call(s32[8]{0:T(128)} %reshape_squeeze.7.refs_0_.refs_1_, s32[4,2,768]{2,1,0:T(2,128)} %add_select_fusion.refs_1_, f32[4,2,768]{2,1,0:T(2,128)} %fusion.34.refs_2_, bf16[2,192,1024]{2,1,0:T(8,128)(2,1)} %copy-done.37, ...), custom_call_target="tpu_custom_call" | custom-call | flops 15032385536 | bytes 23068672 | tf_op jit(solution)/shard_map/pallas_call | solution.py:486
  723.0 11.4 collective-permute-done.66
  736.4 10.6 shard_map.250
  773.2 17.9 %shard_map.241 = (bf16[1,192,1024]{2,1,0:T(8,128)(2,1)}, bf16[1,1536,1024]{2,1,0:T(8,128)(2,1)}) custom-call(bf16[1,192,2048]{2,1,0:T(8,128)(2,1)} %bitcast.360, bf16[1,1536,1024]{2,1,0:T(8,128)(2,1)} %bitcast.342, bf16[1,1536,1024]{2,1,0:T(8,128)(2,1)} %bitcast.343, f32[1536,768]{1,0:T(8,128)} %compare_select_fusion.bias_ref, ...), custom_call_target="tpu_custom_call" | custom-call | flops 6039797760 | bytes 11010048 | tf_op jit(solution)/shard_map/pallas_call | solution.py:417
  796.2 18.8 %collective-permute-done.70 = bf16[384,1024]{1,0:T(8,128)(2,1)S(1)} collective-permute-done((bf16[384,1024]{1,0:T(8,128)(2,1)S(1)}, bf16[384,1024]{1,0:T(8,128)(2,1)S(1)}, u32[]{:S(2)}, u32[]{:S(2)}) %collective-permute-start.70) | collective-permute-done | bytes 786464 | tf_op jit(solution)/shard_map/ppermute | solution.py:25
  854.8 18.3 %collective-permute-done.75.refs_5_ = bf16[2,192,1024]{2,1,0:T(8,128)(2,1)} collective-permute-done((bf16[2,192,1024]{2,1,0:T(8,128)(2,1)S(1)}, bf16[2,192,1024]{2,1,0:T(8,128)(2,1)}, u32[]{:S(2)}, u32[]{:S(2)}) %collective-permute-start.75) | collective-permute-done | bytes 786464 | tf_op jit(solution)/shard_map/ppermute | solution.py:25
  877.1 25.4 %shard_map.244 = (bf16[4,2,192,1024]{3,2,1,0:T(8,128)(2,1)}, bf16[4,2,384,1024]{3,2,1,0:T(8,128)(2,1)}, bf16[4,512,1024]{2,1,0:T(8,128)(2,1)}) custom-call(s32[8]{0:T(128)} %reshape_squeeze.6.refs_0_.refs_1_, s32[4,2,768]{2,1,0:T(2,128)} %add_select_fusion.1.refs_1_, f32[4,2,768]{2,1,0:T(2,128)} %fusion.33.refs_2_, bf16[2,192,1024]{2,1,0:T(8,128)(2,1)} %copy-done.36, ...), custom_call_target="tpu_custom_call" | custom-call | flops 15032385536 | bytes 23068672 | tf_op jit(solution)/shard_map/pallas_call | solution.py:486
  927.0 10.4 shard_map.249
  980.7 18.1 %shard_map.246 = (bf16[1,192,1024]{2,1,0:T(8,128)(2,1)}, bf16[1,1536,1024]{2,1,0:T(8,128)(2,1)}) custom-call(bf16[1,192,2048]{2,1,0:T(8,128)(2,1)} %bitcast.358, bf16[1,1536,1024]{2,1,0:T(8,128)(2,1)} %bitcast.346, bf16[1,1536,1024]{2,1,0:T(8,128)(2,1)} %bitcast.347, f32[1536,768]{1,0:T(8,128)} %compare_select_fusion.bias_ref, ...), custom_call_target="tpu_custom_call" | custom-call | flops 6039797760 | bytes 11010048 | tf_op jit(solution)/shard_map/pallas_call | solution.py:417
  1012.1 12.8 collective-permute-done.115
  1138.4 33.1 %collective-permute-done.108 = bf16[4,256,768]{2,1,0:T(8,128)(2,1)S(1)} collective-permute-done((bf16[4,256,768]{2,1,0:T(8,128)(2,1)}, bf16[4,256,768]{2,1,0:T(8,128)(2,1)S(1)}, u32[]{:S(2)}, u32[]{:S(2)}) %collective-permute-start.108) | collective-permute-done | bytes 1572896 | tf_op jit(solution)/shard_map/ppermute | solution.py:25
  1177.2 36.1 %reduce-scatter.17.cloned.1.call-done = bf16[4,256,512]{2,1,0:T(8,128)(2,1)} async-done(((bf16[4,1024,512]{2,1,0:T(8,128)(2,1)}), bf16[4,256,512]{2,1,0:T(8,128)(2,1)}) %reduce-scatter.17.cloned.1.call-update) | async-done | bytes 1048592 | tf_op jit(solution)/shard_map/reduce_scatter | solution.py:1002
  1220.1 20.4 %collective-permute-done.116 = bf16[4,256,512]{2,1,0:T(8,128)(2,1)S(1)} collective-permute-done((bf16[4,256,512]{2,1,0:T(8,128)(2,1)}, bf16[4,256,512]{2,1,0:T(8,128)(2,1)S(1)}, u32[]{:S(2)}, u32[]{:S(2)}) %collective-permute-start.116) | collective-permute-done | bytes 1048608 | tf_op jit(solution)/shard_map/ppermute | solution.py:25
  1257.0 14.8 %collective-permute-done.111 = bf16[256,768]{1,0:T(8,128)(2,1)S(1)} collective-permute-done((bf16[256,768]{1,0:T(8,128)(2,1)S(1)}, bf16[256,768]{1,0:T(8,128)(2,1)S(1)}, u32[]{:S(2)}, u32[]{:S(2)}) %collective-permute-start.111) | collective-permute-done | bytes 393248 | tf_op jit(solution)/shard_map/ppermute | solution.py:25
  (621 shorter events, 584.1 us)
Async XLA Ops:
  7.2 54.9 %all-gather.23.cloned.1.call-start = ((), (), s32[]{:S(2)}) async-start(), calls=%async_computation.20 | async-start | bytes 1966080 | tf_op jit(solution)/shard_map/all_gather | solution.py:918
  23.3 120.5 %all-gather.11.cloned.1.call-start = ((), (), s32[]{:S(2)}) async-start(), calls=%async_computation.8 | async-start | bytes 5242880 | tf_op jit(solution)/shard_map/all_gather | solution.py:931
  62.1 163.0 %all-gather.15.cloned.1.call-start = ((), (), s32[]{:S(2)}) async-start(), calls=%async_computation.10 | async-start | bytes 5242880 | tf_op jit(solution)/shard_map/all_gather | solution.py:931
  113.8 264.0 %all-gather.25.cloned.1.call-start = ((), (), s32[]{:S(2)}) async-start(), calls=%async_computation.21 | async-start | bytes 1966080 | tf_op jit(solution)/shard_map/all_gather | solution.py:918
  143.9 235.5 %all-gather.13.cloned.1.call-start = ((), (), s32[]{:S(2)}) async-start(), calls=%async_computation.9 | async-start | bytes 5242880 | tf_op jit(solution)/shard_map/all_gather | solution.py:931
  146.7 389.3 %all-gather.17.cloned.1.call-start = ((), (), s32[]{:S(2)}) async-start(), calls=%async_computation.11 | async-start | bytes 5242880 | tf_op jit(solution)/shard_map/all_gather | solution.py:931
  227.9 52.6 %all-to-all-start = ((bf16[1,4,192,256]{3,2,0,1:T(8,128)(2,1)}), bf16[1,4,192,256]{3,2,0,1:T(8,128)(2,1)S(1)}, u32[]{:S(2)}, u32[]{:S(2)}) async-start(bf16[1,4,192,256]{3,2,0,1:T(8,128)(2,1)} %maximum_bitcast_fusion), calls=%async_computation | async-start | bytes 786432 | tf_op jit(solution)/shard_map/all_to_all | solution.py:776
  231.4 304.6 %all-gather.19.cloned.1.call-start = ((), (), s32[]{:S(2)}) async-start(), calls=%async_computation.12 | async-start | bytes 5242880 | tf_op jit(solution)/shard_map/all_gather | solution.py:931
  232.1 47.1 %collective-permute-start = (f32[2,1024]{1,0:T(2,128)}, f32[2,1024]{1,0:T(2,128)}, u32[]{:S(2)}, u32[]{:S(2)}) collective-permute-start(f32[2,1024]{1,0:T(2,128)} %maximum_convert_fusion.3), channel_id=1, source_target_pairs={{0,16},{16,0},{1,17},{17,1},{2,18},{18,2},{3,19},{19,3},{4,20},{20... | collective-permute-start | bytes 24584 | tf_op jit(solution)/shard_map/ppermute | solution.py:25
  233.5 76.6 %collective-permute-start.14 = (s32[2,768,8]{1,2,0:T(8,128)}, s32[2,768,8]{1,2,0:T(8,128)}, u32[]{:S(2)}, u32[]{:S(2)}) collective-permute-start(s32[2,768,8]{1,2,0:T(8,128)} %bitcast.17), channel_id=1, source_target_pairs={{0,16},{16,0},{1,17},{17,1},{2,18},{18,2},{3,19},{19,3},{4,20},{20... | collective-permute-start | bytes 147464 | tf_op jit(solution)/shard_map/ppermute | solution.py:25
  234.1 126.2 %collective-permute-start.15 = (f32[2,768,8]{1,2,0:T(8,128)}, f32[2,768,8]{1,2,0:T(8,128)}, u32[]{:S(2)}, u32[]{:S(2)}) collective-permute-start(f32[2,768,8]{1,2,0:T(8,128)} %bitcast.24), channel_id=1, source_target_pairs={{0,16},{16,0},{1,17},{17,1},{2,18},{18,2},{3,19},{19,3},{4,20},{20... | collective-permute-start | bytes 147464 | tf_op jit(solution)/shard_map/ppermute | solution.py:25
  236.7 35.9 %collective-permute-start.3 = (bf16[4,256,768]{2,1,0:T(8,128)(2,1)S(1)}, bf16[4,256,768]{2,1,0:T(8,128)(2,1)S(1)}, u32[]{:S(2)}, u32[]{:S(2)}) collective-permute-start(bf16[4,256,768]{2,1,0:T(8,128)(2,1)S(1)} %bitcast.332), channel_id=1, source_target_pairs={{0,2},{1,3},{2,0},{3,1},{4,6},{5,7},{6,4},{7,5},{8,10},{9,11},{10,... | collective-permute-start | bytes 4718600 | tf_op jit(solution)/shard_map/ppermute | solution.py:25
  245.5 36.2 %collective-permute-start.2 = (bf16[4,256,768]{2,1,0:T(8,128)(2,1)S(1)}, bf16[4,256,768]{2,1,0:T(8,128)(2,1)}, u32[]{:S(2)}, u32[]{:S(2)}) collective-permute-start(bf16[4,256,768]{2,1,0:T(8,128)(2,1)S(1)} %bitcast.333), channel_id=1, source_target_pairs={{0,1},{1,0},{2,3},{3,2},{4,5},{5,4},{6,7},{7,6},{8,9},{9,8},{10,11... | collective-permute-start | bytes 4718600 | tf_op jit(solution)/shard_map/ppermute | solution.py:25
  281.7 326.2 %all-gather.21.cloned.1.call-start = ((), (), s32[]{:S(2)}) async-start(), calls=%async_computation.13 | async-start | bytes 5242880 | tf_op jit(solution)/shard_map/all_gather | solution.py:931
  377.8 37.0 %collective-permute-start.31 = (bf16[4,256,768]{2,1,0:T(8,128)(2,1)}, bf16[4,256,768]{2,1,0:T(8,128)(2,1)S(1)}, u32[]{:S(2)}, u32[]{:S(2)}) collective-permute-start(bf16[4,256,768]{2,1,0:T(8,128)(2,1)} %bitcast.334), channel_id=1, source_target_pairs={{0,2},{1,3},{2,0},{3,1},{4,6},{5,7},{6,4},{7,5},{8,10},{9,11},{10,... | collective-permute-start | bytes 4718600 | tf_op jit(solution)/shard_map/ppermute | solution.py:25
  410.0 31.6 %collective-permute-start.30 = (bf16[4,256,768]{2,1,0:T(8,128)(2,1)S(1)}, bf16[4,256,768]{2,1,0:T(8,128)(2,1)S(1)}, u32[]{:S(2)}, u32[]{:S(2)}) collective-permute-start(bf16[4,256,768]{2,1,0:T(8,128)(2,1)S(1)} %bitcast.339), channel_id=1, source_target_pairs={{0,1},{1,0},{2,3},{3,2},{4,5},{5,4},{6,7},{7,6},{8,9},{9,8},{10,11... | collective-permute-start | bytes 4718600 | tf_op jit(solution)/shard_map/ppermute | solution.py:25
  631.0 242.1 %reduce-scatter.7.cloned.1.call-start = ((), (), s32[]{:S(2)}) async-start(), calls=%async_computation.14 | async-start | bytes 5242880 | tf_op jit(solution)/shard_map/reduce_scatter | solution.py:1002
  715.3 199.9 %reduce-scatter.11.cloned.1.call-start = ((), (), s32[]{:S(2)}) async-start(), calls=%async_computation.16 | async-start | bytes 5242880 | tf_op jit(solution)/shard_map/reduce_scatter | solution.py:1002
  747.0 251.8 %reduce-scatter.15.cloned.1.call-start = ((), (), s32[]{:S(2)}) async-start(), calls=%async_computation.18 | async-start | bytes 5242880 | tf_op jit(solution)/shard_map/reduce_scatter | solution.py:1002
  747.8 331.7 %reduce-scatter.9.cloned.1.call-start = ((), (), s32[]{:S(2)}) async-start(), calls=%async_computation.15 | async-start | bytes 5242880 | tf_op jit(solution)/shard_map/reduce_scatter | solution.py:1002
  873.1 29.4 %collective-permute-start.104 = (bf16[4,512,256]{2,1,0:T(8,128)(2,1)}, bf16[4,512,256]{2,1,0:T(8,128)(2,1)S(1)}, u32[]{:S(2)}, u32[]{:S(2)}) collective-permute-start(bf16[4,512,256]{2,1,0:T(8,128)(2,1)} %reduce-scatter.7.cloned.1.call-done), channel_id=1, source_target_pairs={{0,16},{1,17},{2,18},{3,19},{4,20},{5,21},{6,22},{7,23},{8,24},{9,... | collective-permute-start | bytes 3145736 | tf_op jit(solution)/shard_map/ppermute | solution.py:25
  902.6 234.5 %reduce-scatter.13.cloned.1.call-start = ((), (), s32[]{:S(2)}) async-start(), calls=%async_computation.17 | async-start | bytes 5242880 | tf_op jit(solution)/shard_map/reduce_scatter | solution.py:1002
  941.0 272.2 %reduce-scatter.17.cloned.1.call-start = ((), (), s32[]{:S(2)}) async-start(), calls=%async_computation.19 | async-start | bytes 5242880 | tf_op jit(solution)/shard_map/reduce_scatter | solution.py:1002
  962.0 44.2 %collective-permute-start.56 = (bf16[2,192,256]{2,1,0:T(8,128)(2,1)}, bf16[2,192,256]{2,1,0:T(8,128)(2,1)}, u32[]{:S(2)}, u32[]{:S(2)}) collective-permute-start(bf16[2,192,256]{2,1,0:T(8,128)(2,1)} %get-tuple-element.237), channel_id=1, source_target_pairs={{0,3},{1,2},{2,1},{3,0},{4,7},{5,6},{6,5},{7,4},{8,11},{9,10},{10,... | collective-permute-start | bytes 589832 | tf_op jit(solution)/shard_map/ppermute | solution.py:25
  964.6 41.5 %collective-permute-start.55 = (bf16[2,192,256]{2,1,0:T(8,128)(2,1)}, bf16[2,192,256]{2,1,0:T(8,128)(2,1)}, u32[]{:S(2)}, u32[]{:S(2)}) collective-permute-start(bf16[2,192,256]{2,1,0:T(8,128)(2,1)} %get-tuple-element.238), channel_id=1, source_target_pairs={{0,2},{1,3},{2,0},{3,1},{4,6},{5,7},{6,4},{7,5},{8,10},{9,11},{10,... | collective-permute-start | bytes 589832 | tf_op jit(solution)/shard_map/ppermute | solution.py:25
  965.3 61.6 %collective-permute-start.77 = (bf16[4,256,768]{2,1,0:T(8,128)(2,1)S(1)}, bf16[4,256,768]{2,1,0:T(8,128)(2,1)}, u32[]{:S(2)}, u32[]{:S(2)}) collective-permute-start(bf16[4,256,768]{2,1,0:T(8,128)(2,1)S(1)} %pad_maximum_fusion), channel_id=1, source_target_pairs={{0,1},{1,0},{2,3},{3,2},{4,5},{5,4},{6,7},{7,6},{8,9},{9,8},{10,11... | collective-permute-start | bytes 4718600 | tf_op jit(solution)/shard_map/ppermute | solution.py:25
  978.9 48.0 %collective-permute-start.79 = (bf16[4,256,768]{2,1,0:T(8,128)(2,1)}, bf16[4,256,768]{2,1,0:T(8,128)(2,1)S(1)}, u32[]{:S(2)}, u32[]{:S(2)}) collective-permute-start(bf16[4,256,768]{2,1,0:T(8,128)(2,1)} %add_convert_fusion.4), channel_id=1, source_target_pairs={{0,2},{1,3},{2,0},{3,1},{4,6},{5,7},{6,4},{7,5},{8,10},{9,11},{10,... | collective-permute-start | bytes 4718600 | tf_op jit(solution)/shard_map/ppermute | solution.py:25
  1029.5 42.5 %collective-permute-start.80 = (bf16[4,256,768]{2,1,0:T(8,128)(2,1)S(1)}, bf16[4,256,768]{2,1,0:T(8,128)(2,1)S(1)}, u32[]{:S(2)}, u32[]{:S(2)}) collective-permute-start(bf16[4,256,768]{2,1,0:T(8,128)(2,1)S(1)} %add_convert_fusion.3.refs_0_), channel_id=1, source_target_pairs={{0,16},{1,17},{2,18},{3,19},{4,20},{5,21},{6,22},{7,23},{8,24},{9,... | collective-permute-start | bytes 4718600 | tf_op jit(solution)/shard_map/ppermute | solution.py:25
  1079.5 29.6 %collective-permute-start.105 = (bf16[4,512,256]{2,1,0:T(8,128)(2,1)}, bf16[4,512,256]{2,1,0:T(8,128)(2,1)S(1)}, u32[]{:S(2)}, u32[]{:S(2)}) collective-permute-start(bf16[4,512,256]{2,1,0:T(8,128)(2,1)} %reduce-scatter.9.cloned.1.call-done), channel_id=1, source_target_pairs={{16,0},{17,1},{18,2},{19,3},{20,4},{21,5},{22,6},{23,7},{24,8},{25... | collective-permute-start | bytes 3145736 | tf_op jit(solution)/shard_map/ppermute | solution.py:25
  1134.6 36.9 %collective-permute-start.108 = (bf16[4,256,768]{2,1,0:T(8,128)(2,1)}, bf16[4,256,768]{2,1,0:T(8,128)(2,1)S(1)}, u32[]{:S(2)}, u32[]{:S(2)}) collective-permute-start(bf16[4,256,768]{2,1,0:T(8,128)(2,1)} %add_convert_fusion.1), channel_id=1, source_target_pairs={{0,2},{1,3},{2,0},{3,1},{4,6},{5,7},{6,4},{7,5},{8,10},{9,11},{10,... | collective-permute-start | bytes 4718600 | tf_op jit(solution)/shard_map/ppermute | solution.py:25
  1137.1 81.5 %collective-permute-start.114 = (bf16[4,256,512]{2,1,0:T(8,128)(2,1)}, bf16[4,256,512]{2,1,0:T(8,128)(2,1)}, u32[]{:S(2)}, u32[]{:S(2)}) collective-permute-start(bf16[4,256,512]{2,1,0:T(8,128)(2,1)} %reduce-scatter.13.cloned.1.call-done), channel_id=1, source_target_pairs={{16,0},{17,1},{18,2},{19,3},{20,4},{21,5},{22,6},{23,7},{24,8},{25... | collective-permute-start | bytes 3145736 | tf_op jit(solution)/shard_map/ppermute | solution.py:25
  1175.7 64.9 %collective-permute-start.109 = (bf16[4,256,768]{2,1,0:T(8,128)(2,1)S(1)}, bf16[4,256,768]{2,1,0:T(8,128)(2,1)}, u32[]{:S(2)}, u32[]{:S(2)}) collective-permute-start(bf16[4,256,768]{2,1,0:T(8,128)(2,1)S(1)} %add_convert_fusion), channel_id=1, source_target_pairs={{16,0},{17,1},{18,2},{19,3},{20,4},{21,5},{22,6},{23,7},{24,8},{25... | collective-permute-start | bytes 4718600 | tf_op jit(solution)/shard_map/ppermute | solution.py:25
  (164 other events, 2238.8 us)
Sparse Core Ops, SparseCore 0:
  23.5 38.5 all-gather.22
  64.2 79.6 all-gather.10
  146.0 79.0 all-gather.14
  226.6 35.2 all-gather.24
  263.9 90.6 all-gather.12
  356.0 79.2 all-gather.16
  436.9 90.3 all-gather.18
  528.8 78.9 all-gather.20
  715.4 79.5 reduce-scatter.6
  797.9 85.6 reduce-scatter.10
  885.9 78.6 reduce-scatter.14
  967.4 77.2 reduce-scatter.8
  1047.6 83.7 reduce-scatter.12
  1134.2 78.9 reduce-scatter.16

commit v5 on v4

--- a/solution.py
+++ b/solution.py
@@ -479,8 +479,8 @@
 def expert_call(kernel, local, operands, specs, outs, scratch, flops, moved, ready=()):
     def spec(shape, own):
         zeros = (0,) * (len(shape) - 1)
-        if own:
-            return pl.BlockSpec((1, *shape[1:]), lambda e: (e, *zeros))
+        if own is not False:
+            return pl.BlockSpec((1, *shape[1:]), lambda e: (e + int(own) - 1, *zeros))
         return pl.BlockSpec(shape, lambda e: (0, *zeros))
 
     return pl.pallas_call(
@@ -548,10 +548,16 @@
         store_tokens(y_ref, total_ref)
 
 
+def gate_and_up(weights, local):
+    gate, up = weights[0], weights[-2]
+    return gate, up, True, (local + 1 if len(weights) == 2 else True)
+
+
 def experts(counts, place, weight, pieces, weights):
     micro, rows, width = pieces[0].shape
-    gate, up, down = weights
-    local, hidden = gate.shape[0], gate.shape[2]
+    local, hidden = place.shape[0], weights[0].shape[2]
+    gate, up, at_gate, at_up = gate_and_up(weights, local)
+    down = weights[-1]
     ncol = len(pieces)
     tokens = ncol * rows
     slots = local * micro * 256
@@ -559,7 +565,7 @@
         functools.partial(expert_hidden_kernel, ncol),
         local,
         (counts, place, *pieces, gate, up),
-        (None, True, *[False] * ncol, True, True),
+        (None, True, *[False] * ncol, at_gate, at_up),
         [
             ((local, micro, CAP, width), True),
             ((local, micro, CAP, 2 * hidden), True),
@@ -628,6 +634,7 @@
 def expert_weight_back_kernel(counts_ref, chosen_ref, dhidden_ref, dgate_ref, dup_ref):
     micro = chosen_ref.shape[1]
     hidden = dgate_ref.shape[2]
+    outs = dgate_ref, dup_ref
 
     def body(cap):
         rows = jnp.concatenate([chosen_ref[0, m, :cap, :] for m in range(micro)], axis=0)
@@ -637,16 +644,17 @@
         dup_ref[0] = grads[:, hidden:]
 
     def empty():
-        dgate_ref[...] = jnp.zeros_like(dgate_ref)
-        dup_ref[...] = jnp.zeros_like(dup_ref)
+        for out in outs:
+            out[...] = jnp.zeros_like(out)
 
     by_load(counts_ref, body, empty)
 
 
 def experts_back(counts, place, weight, pieces, weights, hid):
     micro, rows, width = pieces[0].shape
-    gate, up, down = weights
-    local, hidden = gate.shape[0], gate.shape[2]
+    local, hidden = place.shape[0], weights[0].shape[2]
+    gate, up, at_gate, at_up = gate_and_up(weights, local)
+    down = weights[-1]
     ncol = len(pieces)
     tokens = ncol * rows
     slots = local * micro * 256
@@ -654,7 +662,7 @@
         functools.partial(expert_back_kernel, ncol),
         local,
         (counts, place, weight, *pieces, gate, up, down, hid),
-        (None, True, True, *[False] * ncol, True, True, True, True),
+        (None, True, True, *[False] * ncol, at_gate, at_up, True, True),
         [
             ((ncol, micro, rows, width), False),
             ((local, micro, CAP, 2 * hidden), True),
@@ -672,15 +680,15 @@
 
 
 def expert_weights_back(counts, chosen, dhid, weights, ready):
-    gate, up, _ = weights
-    local, width, hidden = gate.shape
-    micro = chosen.shape[1]
+    local, micro = chosen.shape[:2]
+    width, hidden = weights[0].shape[1:]
+    shapes = [(local, width, hidden)] * 2
     return expert_call(
         expert_weight_back_kernel,
         local,
         (counts, chosen, dhid),
         (None, True, True),
-        [(gate.shape, True), (up.shape, True)],
+        [(shape, True) for shape in shapes],
         [],
         local * micro * 256 * width * 4 * hidden,
         local * width * (4 * hidden + 4 * micro * CAP),
@@ -726,14 +734,14 @@
     return result, keep
 
 
-def backward_layer(grad_result, pieces, keep, env, part, before_projections=()):
+def backward_layer(grad_result, pieces, keep, env, part, before_projections=None):
     rows, _ = grad_result.shape
     prompt = env["prompt"]
     ncol, nrow = lax.axis_size("col"), lax.axis_size("row")
     partial, dhid, ddown = experts_back(*part["slots"], pieces, part["experts"], keep["hid"])
     begun = []
     dn2 = collect_rows(partial, begun)
-    dgate, dup = expert_weights_back(part["slots"][0], keep["chosen"], dhid, part["experts"], begun)
+    dhidden = expert_weights_back(part["slots"][0], keep["chosen"], dhid, part["experts"], begun)
     dsecond, dbranch, dmixed, gain_second = open_back(
         grad_result, dn2, keep["second"], part["gain_second"], part
     )
@@ -748,12 +756,17 @@
         at = rows + (j - 1) * prompt
         parts.append(own[at : at + prompt].astype(BF16))
     own = jnp.concatenate([scatter_row(parts), own[prompt:rows]], axis=0).astype(BF16)
+    small = keep["normed"], dq[0], own, keep["mixed"][0], dbranch, part
+    ready = ()
+    if before_projections is not None:
+        small = weight_back(*small)
+        ready = (*before_projections, small[0][0])
     grad_in, gain_first = project_back(
-        dq[0], own, keep["layer_in"], part["gain_first"], dsecond, part, before_projections
+        dq[0], own, keep["layer_in"], part["gain_first"], dsecond, part, ready
     )
     return grad_in, {
-        "small": (keep["normed"], dq[0], own, keep["mixed"][0], dbranch, part),
-        "experts": (dgate, dup, ddown),
+        "small": small,
+        "experts": (*dhidden, ddown),
         "gain_first": gain_first[0],
         "gain_second": gain_second[0],
     }
@@ -923,13 +936,14 @@
     shards = [
         [jnp.where(is_home, w[:half], c) for w, c in zip(big, crossed)] for is_home in home
     ]
+    gate, up, down = shards[1]
+    shards[1] = [jnp.concatenate([gate, up], axis=0), down]
     ids_layer, gates_layer = by_layer(expert_ids[0, :, 0]), by_layer(gates[0, :, 0])
     gains = by_layer(jnp.concatenate([gain_attn, gain_ffn]).astype(F32))
 
     def whole(pieces):
-        return [
-            lax.all_gather(w, "row", axis=axis, tiled=True) for w, axis in zip(pieces, (1, 1, 2))
-        ]
+        axes = (1,) * (len(pieces) - 1) + (2,)
+        return [lax.all_gather(w, "row", axis=axis, tiled=True) for w, axis in zip(pieces, axes)]
 
     def layer_part(layer, held):
         own_first = lambda v: jnp.where(home[0], v, v[::-1])
@@ -1005,7 +1019,16 @@
     sums_last = [over_rows(j, 1) for j in order]
     back_last = [shift(g, "section", [(0, 1)]) for g in sums_last]
     sums_first = [over_rows(j, 0, back) for j, back in zip(order, back_last)]
-    back_first = [shift(g, "section", [(1, 0)]) for g in sums_first]
+    back_first = [shift(g, "section", [(1, 0)]) for g in sums_first[:2]]
+    small_first = col_gradients(*first_grads["small"], w_rows)
+    small = [None] * nrow
+    for j in (*range(1, nrow), 0):
+        pair = small_first[j], shift(small_first[j], "section", [(1, 0)])
+        first, last = (a.astype(F32) + b.astype(F32) for a, b in (pair, (small_last[0][j], small_last[1][j])))
+        small[j] = jnp.where(home[0], first, last).astype(BF16)
+    small[0] = needing(small[0], back_first[0])
+    small = scatter_row(small)
+    back_first.append(shift(needing(sums_first[2], small), "section", [(1, 0)]))
 
     def expert_gradient(j):
         at = order.index(j)
@@ -1014,11 +1037,6 @@
         return jnp.concatenate([own, other], axis=0).astype(F32)
 
     grad_gate, grad_up, grad_down = (expert_gradient(j) for j in range(3))
-    small_first = col_gradients(*weight_back(*first_grads["small"], back_first[:1]), w_rows)
-    small_first = small_first, shift(small_first, "section", [(1, 0)])
-    small = [a.astype(F32) + b.astype(F32) for a, b in (small_first, small_last)]
-    small = jnp.where(home[0], *small).astype(BF16)
-    small = scatter_row([small[j] for j in range(nrow)])
     grad_query, grad_out = small[:, :columns], small[:, columns + 2 * kcols :]
     if w_rows == 256:
         heads = lambda v: [v[:, :64], v[:, 128:192], v[:, 64:128], v[:, 192:]]

time: 1290 us -> 1280 us (level)
  waiting for transfers between devices: 716 us -> 692 us
    reduce_scatter x6, waiting for transfers between devices: 36.1 us -> 0.03 us  [over_rows(): lax.psum_scatter(grad, 'row', scatter_dimension=(1, 1, 2)[j], tiled=True)]
    ppermute x117 -> x120, waiting for transfers between devices: 502 us -> 530 us  [shift(): return lax.ppermute(value, axis, pairs)]
    all_gather x6 -> x5, waiting for transfers between devices: 164 us -> 148 us  [whole(): lax.all_gather(w, 'row', axis=axis, tiled=True)]
    ppermute x117 -> x120, starting transfers between devices: 147 us -> 136 us  [shift(): return lax.ppermute(value, axis, pairs)]
  transfers between devices with their start and end apart: 133 -> 135, of which waited for: 69 -> 72; matrix products, arithmetic and copies ran while one was open for 10% -> 13% of each run, Pallas kernels for 15% -> 15%
where the time goes in v5:
time: 1280 us; the launch traced here: 1270 us
  waiting for transfers between devices  692 us (54%)
  Pallas kernels  234 us (18%)
  starting transfers between devices  144 us (11%)
  other arithmetic  116 us (9%)
  local copies, waits for them, and re-layouts  61.4 us (5%)
  between operations  18.4 us (1%)
    ppermute x120, waiting for transfers between devices, shift(): return lax.ppermute(value, axis, pairs)  530 us
    all_gather x5, waiting for transfers between devices, whole(): lax.all_gather(w, 'row', axis=axis, tiled=True)  148 us
    ppermute x120, starting transfers between devices, shift(): return lax.ppermute(value, axis, pairs)  136 us
    pallas_call x8, Pallas kernels, expert_call(): pl.pallas_call(behind(kernel, len(ready)), grid=(local,), in_specs=[pl.Bl...  127 us
    pallas_call x8, Pallas kernels, whole_call(): pl.pallas_call(behind(functools.partial(kernel, len(blocks)), len(ready))...  36.2 us
    pallas_call x2, Pallas kernels, attend_back(): pl.pallas_call(attend_back_kernel, grid=(micro, groups), in_specs=[mine,...  35.8 us
  transfers between devices with their start and end apart: 135, of which 72 were waited for; matrix products, arithmetic and copies ran while one was open for 13% of the time, Pallas kernels for 15%

profile of v5, /device:TPU:0, one launch (start us, length us, event | category | flops | bytes accessed | tf_op | source)
XLA Modules:
  0.0 1266.1 jit_solution(16495184278931214143)
XLA Ops:
  25.3 22.6 %collective-permute-done.20 = bf16[4,256,512]{2,1,0:T(8,128)(2,1)S(1)} collective-permute-done((bf16[4,256,512]{2,1,0:T(8,128)(2,1)S(1)}, bf16[4,256,512]{2,1,0:T(8,128)(2,1)S(1)}, u32[]{:S(2)}, u32[]{:S(2)}) %collective-permute-start.20) | collective-permute-done | bytes 1048608 | tf_op jit(solution)/shard_map/ppermute | solution.py:25
  49.0 13.1 %all-gather.20.cloned.1.call-done = bf16[1024,768]{1,0:T(8,128)(2,1)} async-done(((bf16[256,768]{1,0:T(8,128)(2,1)}), bf16[1024,768]{1,0:T(8,128)(2,1)}) %all-gather.20.cloned.1.call-update) | async-done | bytes 1572880 | tf_op jit(solution)/shard_map/all_gather | solution.py:931
  66.3 22.1 %collective-permute-done.21 = bf16[4,256,512]{2,1,0:T(8,128)(2,1)} collective-permute-done((bf16[4,256,512]{2,1,0:T(8,128)(2,1)S(1)}, bf16[4,256,512]{2,1,0:T(8,128)(2,1)}, u32[]{:S(2)}, u32[]{:S(2)}) %collective-permute-start.21) | collective-permute-done | bytes 1048608 | tf_op jit(solution)/shard_map/ppermute | solution.py:25
  89.9 22.4 %collective-permute-done.22 = bf16[4,512,256]{2,1,0:T(8,128)(2,1)S(1)} collective-permute-done((bf16[4,512,256]{2,1,0:T(8,128)(2,1)S(1)}, bf16[4,512,256]{2,1,0:T(8,128)(2,1)S(1)}, u32[]{:S(2)}, u32[]{:S(2)}) %collective-permute-start.22) | collective-permute-done | bytes 1048608 | tf_op jit(solution)/shard_map/ppermute | solution.py:25
  113.9 30.0 %all-gather.10.cloned.1.call-done.refs_6_.refs_7_ = bf16[4,1024,512]{2,1,0:T(8,128)(2,1)} async-done(((bf16[4,256,512]{2,1,0:T(8,128)(2,1)}), bf16[4,1024,512]{2,1,0:T(8,128)(2,1)}) %all-gather.10.cloned.1.call-update) | async-done | bytes 4194320 | tf_op jit(solution)/shard_map/all_gather | solution.py:946
  148.3 76.9 %all-gather.14.cloned.1.call-done.refs_4_.refs_9_ = bf16[4,512,1024]{2,1,0:T(8,128)(2,1)} async-done(((bf16[4,512,256]{2,1,0:T(8,128)(2,1)}), bf16[4,512,1024]{2,1,0:T(8,128)(2,1)}) %all-gather.14.cloned.1.call-update) | async-done | bytes 4194320 | tf_op jit(solution)/shard_map/all_gather | solution.py:946
  245.3 27.1 %collective-permute-done.3.refs_7_.refs_6_.refs_11_ = bf16[4,256,768]{2,1,0:T(8,128)(2,1)S(1)} collective-permute-done((bf16[4,256,768]{2,1,0:T(8,128)(2,1)S(1)}, bf16[4,256,768]{2,1,0:T(8,128)(2,1)S(1)}, u32[]{:S(2)}, u32[]{:S(2)}) %collective-permute-start.3) | collective-permute-done | bytes 1572896 | tf_op jit(solution)/shard_map/ppermute | solution.py:25
  329.7 11.3 shard_map.230
  361.6 14.3 %collective-permute-done.18.refs_4_ = bf16[2,192,1024]{2,1,0:T(8,128)(2,1)S(1)} collective-permute-done((bf16[2,192,1024]{2,1,0:T(8,128)(2,1)S(1)}, bf16[2,192,1024]{2,1,0:T(8,128)(2,1)S(1)}, u32[]{:S(2)}, u32[]{:S(2)}) %collective-permute-start.18) | collective-permute-done | bytes 786464 | tf_op jit(solution)/shard_map/ppermute | solution.py:25
  379.2 14.4 %shard_map.232 = (bf16[4,2,384,1024]{3,2,1,0:T(8,128)(2,1)}, bf16[4,2,384,1024]{3,2,1,0:T(8,128)(2,1)}, bf16[4,2,384,512]{3,2,1,0:T(8,128)(2,1)}) custom-call(s32[8]{0:T(128)} %reshape_squeeze.6.refs_0_.refs_1_, s32[4,2,768]{2,1,0:T(2,128)} %add_select_fusion.1.refs_1_, bf16[2,192,1024]{2,1,0:T(8,128)(2,1)} %copy-done.35, ...), custom_call_target="tpu_custom_call" | custom-call | flops 7516192768 | bytes 20971520 | tf_op jit(solution)/shard_map/pallas_call | solution.py:486
  393.6 10.8 shard_map.233
  489.8 11.6 shard_map.235
  506.4 10.0 collective-permute-done.42
  520.8 15.5 %collective-permute-done.44.refs_4_ = bf16[2,192,1024]{2,1,0:T(8,128)(2,1)S(1)} collective-permute-done((bf16[2,192,1024]{2,1,0:T(8,128)(2,1)S(1)}, bf16[2,192,1024]{2,1,0:T(8,128)(2,1)S(1)}, u32[]{:S(2)}, u32[]{:S(2)}) %collective-permute-start.44) | collective-permute-done | bytes 786464 | tf_op jit(solution)/shard_map/ppermute | solution.py:25
  538.8 15.6 %shard_map.237 = (bf16[4,2,384,1024]{3,2,1,0:T(8,128)(2,1)}, bf16[4,2,384,1024]{3,2,1,0:T(8,128)(2,1)}, bf16[4,2,384,512]{3,2,1,0:T(8,128)(2,1)}) custom-call(s32[8]{0:T(128)} %reshape_squeeze.7.refs_0_.refs_1_, s32[4,2,768]{2,1,0:T(2,128)} %add_select_fusion.refs_1_, bf16[2,192,1024]{2,1,0:T(8,128)(2,1)} %copy-done.34, bf16[2,192,1024]{2,1,0:T(8,128)(2,1)} %copy-done.61, ...), custom_call_target="tpu_custom_call" | custom-call | flops 7516192768 | bytes 20971520 | tf_op jit(solution)/shard_map/pallas_call | solution.py:486
  554.4 41.3 %all-gather.18.cloned.1.call-done.refs_4_.refs_9_ = bf16[4,512,1024]{2,1,0:T(8,128)(2,1)} async-done(((bf16[4,512,256]{2,1,0:T(8,128)(2,1)}), bf16[4,512,1024]{2,1,0:T(8,128)(2,1)}) %all-gather.18.cloned.1.call-update) | async-done | bytes 4194320 | tf_op jit(solution)/shard_map/all_gather | solution.py:946
  595.7 11.6 shard_map.238
  653.5 16.7 %collective-permute-done.59.refs_5_ = bf16[2,192,1024]{2,1,0:T(8,128)(2,1)S(1)} collective-permute-done((bf16[2,192,1024]{2,1,0:T(8,128)(2,1)S(1)}, bf16[2,192,1024]{2,1,0:T(8,128)(2,1)S(1)}, u32[]{:S(2)}, u32[]{:S(2)}) %collective-permute-start.59) | collective-permute-done | bytes 786464 | tf_op jit(solution)/shard_map/ppermute | solution.py:25
  673.4 27.4 %shard_map.239 = (bf16[4,2,192,1024]{3,2,1,0:T(8,128)(2,1)}, bf16[4,2,384,1024]{3,2,1,0:T(8,128)(2,1)}, bf16[4,512,1024]{2,1,0:T(8,128)(2,1)}) custom-call(s32[8]{0:T(128)} %reshape_squeeze.7.refs_0_.refs_1_, s32[4,2,768]{2,1,0:T(2,128)} %add_select_fusion.refs_1_, f32[4,2,768]{2,1,0:T(2,128)} %fusion.37.refs_2_, bf16[2,192,1024]{2,1,0:T(8,128)(2,1)} %copy-done.37, ...), custom_call_target="tpu_custom_call" | custom-call | flops 15032385536 | bytes 23068672 | tf_op jit(solution)/shard_map/pallas_call | solution.py:486
  722.9 11.0 shard_map.250
  757.1 17.9 %shard_map.241 = (bf16[1,192,1024]{2,1,0:T(8,128)(2,1)}, bf16[1,1536,1024]{2,1,0:T(8,128)(2,1)}) custom-call(bf16[1,192,2048]{2,1,0:T(8,128)(2,1)} %bitcast.389, bf16[1,1536,1024]{2,1,0:T(8,128)(2,1)} %bitcast.371, bf16[1,1536,1024]{2,1,0:T(8,128)(2,1)} %bitcast.372, f32[1536,768]{1,0:T(8,128)} %compare_select_fusion.bias_ref, ...), custom_call_target="tpu_custom_call" | custom-call | flops 6039797760 | bytes 11010048 | tf_op jit(solution)/shard_map/pallas_call | solution.py:417
  780.1 18.8 %collective-permute-done.70 = bf16[384,1024]{1,0:T(8,128)(2,1)S(1)} collective-permute-done((bf16[384,1024]{1,0:T(8,128)(2,1)S(1)}, bf16[384,1024]{1,0:T(8,128)(2,1)S(1)}, u32[]{:S(2)}, u32[]{:S(2)}) %collective-permute-start.70) | collective-permute-done | bytes 786464 | tf_op jit(solution)/shard_map/ppermute | solution.py:25
  836.9 16.6 %collective-permute-done.75.refs_5_ = bf16[2,192,1024]{2,1,0:T(8,128)(2,1)} collective-permute-done((bf16[2,192,1024]{2,1,0:T(8,128)(2,1)S(1)}, bf16[2,192,1024]{2,1,0:T(8,128)(2,1)}, u32[]{:S(2)}, u32[]{:S(2)}) %collective-permute-start.75) | collective-permute-done | bytes 786464 | tf_op jit(solution)/shard_map/ppermute | solution.py:25
  856.2 26.0 %shard_map.244 = (bf16[4,2,192,1024]{3,2,1,0:T(8,128)(2,1)}, bf16[4,2,384,1024]{3,2,1,0:T(8,128)(2,1)}, bf16[4,512,1024]{2,1,0:T(8,128)(2,1)}) custom-call(s32[8]{0:T(128)} %reshape_squeeze.6.refs_0_.refs_1_, s32[4,2,768]{2,1,0:T(2,128)} %add_select_fusion.1.refs_1_, f32[4,2,768]{2,1,0:T(2,128)} %fusion.36.refs_2_, bf16[2,192,1024]{2,1,0:T(8,128)(2,1)} %copy-done.36, ...), custom_call_target="tpu_custom_call" | custom-call | flops 15032385536 | bytes 23068672 | tf_op jit(solution)/shard_map/pallas_call | solution.py:486
  907.8 10.6 shard_map.249
  950.9 17.9 %shard_map.246 = (bf16[1,192,1024]{2,1,0:T(8,128)(2,1)}, bf16[1,1536,1024]{2,1,0:T(8,128)(2,1)}) custom-call(bf16[1,192,2048]{2,1,0:T(8,128)(2,1)} %bitcast.387, bf16[1,1536,1024]{2,1,0:T(8,128)(2,1)} %bitcast.375, bf16[1,1536,1024]{2,1,0:T(8,128)(2,1)} %bitcast.376, f32[1536,768]{1,0:T(8,128)} %compare_select_fusion.bias_ref, ...), custom_call_target="tpu_custom_call" | custom-call | flops 6039797760 | bytes 11010048 | tf_op jit(solution)/shard_map/pallas_call | solution.py:417
  988.0 14.6 %collective-permute-done.118 = bf16[4,256,512]{2,1,0:T(8,128)(2,1)} collective-permute-done((bf16[4,256,512]{2,1,0:T(8,128)(2,1)}, bf16[4,256,512]{2,1,0:T(8,128)(2,1)}, u32[]{:S(2)}, u32[]{:S(2)}) %collective-permute-start.118) | collective-permute-done | bytes 1048608 | tf_op jit(solution)/shard_map/ppermute | solution.py:25
  1015.0 10.7 collective-permute-done.91
  1027.8 10.0 collective-permute-start.94
  1103.7 35.8 %collective-permute-done.103 = bf16[2,192,256]{2,1,0:T(8,128)(2,1)S(1)} collective-permute-done((bf16[2,192,256]{2,1,0:T(8,128)(2,1)S(1)}, bf16[2,192,256]{2,1,0:T(8,128)(2,1)S(1)}, u32[]{:S(2)}, u32[]{:S(2)}) %collective-permute-start.103) | collective-permute-done | bytes 196640 | tf_op jit(solution)/shard_map/ppermute | solution.py:25
  1193.5 12.2 collective-permute-done.109
  1240.5 16.4 %collective-permute-done.119 = bf16[4,256,512]{2,1,0:T(8,128)(2,1)S(1)} collective-permute-done((bf16[4,256,512]{2,1,0:T(8,128)(2,1)S(1)}, bf16[4,256,512]{2,1,0:T(8,128)(2,1)S(1)}, u32[]{:S(2)}, u32[]{:S(2)}) %collective-permute-start.119) | collective-permute-done | bytes 1048608 | tf_op jit(solution)/shard_map/ppermute | solution.py:25
  (633 shorter events, 614.1 us)
Async XLA Ops:
  7.2 54.9 %all-gather.20.cloned.1.call-start = ((), (), s32[]{:S(2)}) async-start(), calls=%async_computation.19 | async-start | bytes 1966080 | tf_op jit(solution)/shard_map/all_gather | solution.py:931
  23.3 120.5 %all-gather.10.cloned.1.call-start = ((), (), s32[]{:S(2)}) async-start(), calls=%async_computation.8 | async-start | bytes 5242880 | tf_op jit(solution)/shard_map/all_gather | solution.py:946
  62.1 163.0 %all-gather.14.cloned.1.call-start = ((), (), s32[]{:S(2)}) async-start(), calls=%async_computation.10 | async-start | bytes 5242880 | tf_op jit(solution)/shard_map/all_gather | solution.py:946
  113.8 263.6 %all-gather.22.cloned.1.call-start = ((), (), s32[]{:S(2)}) async-start(), calls=%async_computation.20 | async-start | bytes 1966080 | tf_op jit(solution)/shard_map/all_gather | solution.py:931
  143.9 235.2 %all-gather.12.cloned.1.call-start = ((), (), s32[]{:S(2)}) async-start(), calls=%async_computation.9 | async-start | bytes 5242880 | tf_op jit(solution)/shard_map/all_gather | solution.py:946
  146.6 392.1 %all-gather.16.cloned.1.call-start = ((), (), s32[]{:S(2)}) async-start(), calls=%async_computation.11 | async-start | bytes 10485760 | tf_op jit(solution)/shard_map/all_gather | solution.py:946
  227.8 52.7 %all-to-all-start = ((bf16[1,4,192,256]{3,2,0,1:T(8,128)(2,1)}), bf16[1,4,192,256]{3,2,0,1:T(8,128)(2,1)S(1)}, u32[]{:S(2)}, u32[]{:S(2)}) async-start(bf16[1,4,192,256]{3,2,0,1:T(8,128)(2,1)} %maximum_bitcast_fusion), calls=%async_computation | async-start | bytes 786432 | tf_op jit(solution)/shard_map/all_to_all | solution.py:789
  231.3 364.4 %all-gather.18.cloned.1.call-start = ((), (), s32[]{:S(2)}) async-start(), calls=%async_computation.12 | async-start | bytes 5242880 | tf_op jit(solution)/shard_map/all_gather | solution.py:946
  232.0 47.2 %collective-permute-start = (f32[2,1024]{1,0:T(2,128)}, f32[2,1024]{1,0:T(2,128)}, u32[]{:S(2)}, u32[]{:S(2)}) collective-permute-start(f32[2,1024]{1,0:T(2,128)} %maximum_convert_fusion.3), channel_id=1, source_target_pairs={{0,16},{16,0},{1,17},{17,1},{2,18},{18,2},{3,19},{19,3},{4,20},{20... | collective-permute-start | bytes 24584 | tf_op jit(solution)/shard_map/ppermute | solution.py:25
  233.4 76.4 %collective-permute-start.14 = (s32[2,768,8]{1,2,0:T(8,128)}, s32[2,768,8]{1,2,0:T(8,128)}, u32[]{:S(2)}, u32[]{:S(2)}) collective-permute-start(s32[2,768,8]{1,2,0:T(8,128)} %bitcast.17), channel_id=1, source_target_pairs={{0,16},{16,0},{1,17},{17,1},{2,18},{18,2},{3,19},{19,3},{4,20},{20... | collective-permute-start | bytes 147464 | tf_op jit(solution)/shard_map/ppermute | solution.py:25
  234.0 126.0 %collective-permute-start.15 = (f32[2,768,8]{1,2,0:T(8,128)}, f32[2,768,8]{1,2,0:T(8,128)}, u32[]{:S(2)}, u32[]{:S(2)}) collective-permute-start(f32[2,768,8]{1,2,0:T(8,128)} %bitcast.24), channel_id=1, source_target_pairs={{0,16},{16,0},{1,17},{17,1},{2,18},{18,2},{3,19},{19,3},{4,20},{20... | collective-permute-start | bytes 147464 | tf_op jit(solution)/shard_map/ppermute | solution.py:25
  377.5 37.0 %collective-permute-start.31 = (bf16[4,256,768]{2,1,0:T(8,128)(2,1)}, bf16[4,256,768]{2,1,0:T(8,128)(2,1)S(1)}, u32[]{:S(2)}, u32[]{:S(2)}) collective-permute-start(bf16[4,256,768]{2,1,0:T(8,128)(2,1)} %bitcast.363), channel_id=1, source_target_pairs={{0,2},{1,3},{2,0},{3,1},{4,6},{5,7},{6,4},{7,5},{8,10},{9,11},{10,... | collective-permute-start | bytes 4718600 | tf_op jit(solution)/shard_map/ppermute | solution.py:25
  620.4 233.2 %reduce-scatter.7.cloned.1.call-start = ((), (), s32[]{:S(2)}) async-start(), calls=%async_computation.13 | async-start | bytes 5242880 | tf_op jit(solution)/shard_map/reduce_scatter | solution.py:1016
  700.9 195.1 %reduce-scatter.11.cloned.1.call-start = ((), (), s32[]{:S(2)}) async-start(), calls=%async_computation.15 | async-start | bytes 5242880 | tf_op jit(solution)/shard_map/reduce_scatter | solution.py:1016
  733.9 242.6 %reduce-scatter.15.cloned.1.call-start = ((), (), s32[]{:S(2)}) async-start(), calls=%async_computation.17 | async-start | bytes 5242880 | tf_op jit(solution)/shard_map/reduce_scatter | solution.py:1016
  734.5 422.1 %reduce-scatter.9.cloned.1.call-start = ((), (), s32[]{:S(2)}) async-start(), calls=%async_computation.14 | async-start | bytes 5242880 | tf_op jit(solution)/shard_map/reduce_scatter | solution.py:1016
  882.3 308.9 %reduce-scatter.13.cloned.1.call-start = ((), (), s32[]{:S(2)}) async-start(), calls=%async_computation.16 | async-start | bytes 5242880 | tf_op jit(solution)/shard_map/reduce_scatter | solution.py:1016
  920.3 307.7 %reduce-scatter.17.cloned.1.call-start = ((), (), s32[]{:S(2)}) async-start(), calls=%async_computation.18 | async-start | bytes 5242880 | tf_op jit(solution)/shard_map/reduce_scatter | solution.py:1016
  931.3 37.5 %collective-permute-start.78 = (bf16[4,256,768]{2,1,0:T(8,128)(2,1)}, bf16[4,256,768]{2,1,0:T(8,128)(2,1)}, u32[]{:S(2)}, u32[]{:S(2)}) collective-permute-start(bf16[4,256,768]{2,1,0:T(8,128)(2,1)} %pad_maximum_fusion.2), channel_id=1, source_target_pairs={{0,1},{1,0},{2,3},{3,2},{4,5},{5,4},{6,7},{7,6},{8,9},{9,8},{10,11... | collective-permute-start | bytes 4718600 | tf_op jit(solution)/shard_map/ppermute | solution.py:25
  933.9 39.9 %collective-permute-start.56 = (bf16[2,192,256]{2,1,0:T(8,128)(2,1)}, bf16[2,192,256]{2,1,0:T(8,128)(2,1)}, u32[]{:S(2)}, u32[]{:S(2)}) collective-permute-start(bf16[2,192,256]{2,1,0:T(8,128)(2,1)} %get-tuple-element.241), channel_id=1, source_target_pairs={{0,3},{1,2},{2,1},{3,0},{4,7},{5,6},{6,5},{7,4},{8,11},{9,10},{10,... | collective-permute-start | bytes 589832 | tf_op jit(solution)/shard_map/ppermute | solution.py:25
  935.5 39.0 %collective-permute-start.55 = (bf16[2,192,256]{2,1,0:T(8,128)(2,1)}, bf16[2,192,256]{2,1,0:T(8,128)(2,1)}, u32[]{:S(2)}, u32[]{:S(2)}) collective-permute-start(bf16[2,192,256]{2,1,0:T(8,128)(2,1)} %get-tuple-element.242), channel_id=1, source_target_pairs={{0,2},{1,3},{2,0},{3,1},{4,6},{5,7},{6,4},{7,5},{8,10},{9,11},{10,... | collective-permute-start | bytes 589832 | tf_op jit(solution)/shard_map/ppermute | solution.py:25
  944.0 58.7 %collective-permute-start.77 = (bf16[4,256,768]{2,1,0:T(8,128)(2,1)}, bf16[4,256,768]{2,1,0:T(8,128)(2,1)}, u32[]{:S(2)}, u32[]{:S(2)}) collective-permute-start(bf16[4,256,768]{2,1,0:T(8,128)(2,1)} %pad_maximum_fusion.1), channel_id=1, source_target_pairs={{0,1},{1,0},{2,3},{3,2},{4,5},{5,4},{6,7},{7,6},{8,9},{9,8},{10,11... | collective-permute-start | bytes 4718600 | tf_op jit(solution)/shard_map/ppermute | solution.py:25
  972.2 37.6 %collective-permute-start.79 = (bf16[4,256,768]{2,1,0:T(8,128)(2,1)}, bf16[4,256,768]{2,1,0:T(8,128)(2,1)}, u32[]{:S(2)}, u32[]{:S(2)}) collective-permute-start(bf16[4,256,768]{2,1,0:T(8,128)(2,1)} %add_convert_fusion.4), channel_id=1, source_target_pairs={{0,2},{1,3},{2,0},{3,1},{4,6},{5,7},{6,4},{7,5},{8,10},{9,11},{10,... | collective-permute-start | bytes 4718600 | tf_op jit(solution)/shard_map/ppermute | solution.py:25
  985.8 39.9 %collective-permute-start.91 = (bf16[384,1024]{1,0:T(8,128)(2,1)}, bf16[384,1024]{1,0:T(8,128)(2,1)}, u32[]{:S(2)}, u32[]{:S(2)}) collective-permute-start(bf16[384,1024]{1,0:T(8,128)(2,1)} %fusion.2), channel_id=1, source_target_pairs={{0,2},{1,3},{2,0},{3,1},{4,6},{5,7},{6,4},{7,5},{8,10},{9,11},{10,... | collective-permute-start | bytes 2359304 | tf_op jit(solution)/shard_map/ppermute | solution.py:25
  1012.7 51.2 %collective-permute-start.80 = (bf16[4,256,768]{2,1,0:T(8,128)(2,1)S(1)}, bf16[4,256,768]{2,1,0:T(8,128)(2,1)S(1)}, u32[]{:S(2)}, u32[]{:S(2)}) collective-permute-start(bf16[4,256,768]{2,1,0:T(8,128)(2,1)S(1)} %add_convert_fusion.3.refs_0_), channel_id=1, source_target_pairs={{0,16},{1,17},{2,18},{3,19},{4,20},{5,21},{6,22},{7,23},{8,24},{9,... | collective-permute-start | bytes 4718600 | tf_op jit(solution)/shard_map/ppermute | solution.py:25
  1090.9 57.4 %collective-permute-start.104 = (bf16[4,256,768]{2,1,0:T(8,128)(2,1)}, bf16[4,256,768]{2,1,0:T(8,128)(2,1)}, u32[]{:S(2)}, u32[]{:S(2)}) collective-permute-start(bf16[4,256,768]{2,1,0:T(8,128)(2,1)} %pad_maximum_fusion.3), channel_id=1, source_target_pairs={{0,1},{1,0},{2,3},{3,2},{4,5},{5,4},{6,7},{7,6},{8,9},{9,8},{10,11... | collective-permute-start | bytes 4718600 | tf_op jit(solution)/shard_map/ppermute | solution.py:25
  1099.5 48.8 %collective-permute-start.106 = (bf16[4,256,768]{2,1,0:T(8,128)(2,1)}, bf16[4,256,768]{2,1,0:T(8,128)(2,1)}, u32[]{:S(2)}, u32[]{:S(2)}) collective-permute-start(bf16[4,256,768]{2,1,0:T(8,128)(2,1)} %add_convert_fusion.1), channel_id=1, source_target_pairs={{0,2},{1,3},{2,0},{3,1},{4,6},{5,7},{6,4},{7,5},{8,10},{9,11},{10,... | collective-permute-start | bytes 4718600 | tf_op jit(solution)/shard_map/ppermute | solution.py:25
  1100.6 38.9 %collective-permute-start.103 = (bf16[2,192,256]{2,1,0:T(8,128)(2,1)S(1)}, bf16[2,192,256]{2,1,0:T(8,128)(2,1)S(1)}, u32[]{:S(2)}, u32[]{:S(2)}) collective-permute-start(bf16[2,192,256]{2,1,0:T(8,128)(2,1)S(1)} %get-tuple-element.226), channel_id=1, source_target_pairs={{0,3},{1,2},{2,1},{3,0},{4,7},{5,6},{6,5},{7,4},{8,11},{9,10},{10,... | collective-permute-start | bytes 589832 | tf_op jit(solution)/shard_map/ppermute | solution.py:25
  1101.0 43.2 %collective-permute-start.102 = (bf16[2,192,256]{2,1,0:T(8,128)(2,1)S(1)}, bf16[2,192,256]{2,1,0:T(8,128)(2,1)S(1)}, u32[]{:S(2)}, u32[]{:S(2)}) collective-permute-start(bf16[2,192,256]{2,1,0:T(8,128)(2,1)S(1)} %get-tuple-element.227), channel_id=1, source_target_pairs={{0,2},{1,3},{2,0},{3,1},{4,6},{5,7},{6,4},{7,5},{8,10},{9,11},{10,... | collective-permute-start | bytes 589832 | tf_op jit(solution)/shard_map/ppermute | solution.py:25
  1101.9 42.3 %collective-permute-start.101 = (bf16[2,192,256]{2,1,0:T(8,128)(2,1)S(1)}, bf16[2,192,256]{2,1,0:T(8,128)(2,1)S(1)}, u32[]{:S(2)}, u32[]{:S(2)}) collective-permute-start(bf16[2,192,256]{2,1,0:T(8,128)(2,1)S(1)} %get-tuple-element.228), channel_id=1, source_target_pairs={{0,1},{1,0},{2,3},{3,2},{4,5},{5,4},{6,7},{7,6},{8,9},{9,8},{10,11... | collective-permute-start | bytes 589832 | tf_op jit(solution)/shard_map/ppermute | solution.py:25
  1156.6 49.0 %collective-permute-start.109 = (bf16[4,512,256]{2,1,0:T(8,128)(2,1)}, bf16[4,512,256]{2,1,0:T(8,128)(2,1)}, u32[]{:S(2)}, u32[]{:S(2)}) collective-permute-start(bf16[4,512,256]{2,1,0:T(8,128)(2,1)} %reduce-scatter.9.cloned.1.call-done), channel_id=1, source_target_pairs={{16,0},{17,1},{18,2},{19,3},{20,4},{21,5},{22,6},{23,7},{24,8},{25... | collective-permute-start | bytes 3145736 | tf_op jit(solution)/shard_map/ppermute | solution.py:25
  1158.7 55.4 %collective-permute-start.107 = (bf16[256,768]{1,0:T(8,128)(2,1)}, bf16[256,768]{1,0:T(8,128)(2,1)}, u32[]{:S(2)}, u32[]{:S(2)}) collective-permute-start(bf16[256,768]{1,0:T(8,128)(2,1)} %get-tuple-element.205), channel_id=1, source_target_pairs={{16,0},{17,1},{18,2},{19,3},{20,4},{21,5},{22,6},{23,7},{24,8},{25... | collective-permute-start | bytes 1179656 | tf_op jit(solution)/shard_map/ppermute | solution.py:25
  (168 other events, 2733.9 us)
Sparse Core Ops, SparseCore 0:
  23.5 38.5 all-gather.19
  64.2 79.6 all-gather.9
  146.0 79.0 all-gather.13
  226.6 35.2 all-gather.21
  263.9 90.6 all-gather.11
  356.0 159.2 all-gather.15
  516.9 78.7 all-gather.17
  701.0 78.4 reduce-scatter.6
  782.4 85.6 reduce-scatter.10
  870.3 78.6 reduce-scatter.14
  952.0 77.2 reduce-scatter.8
  1032.0 83.8 reduce-scatter.12
  1118.9 91.4 reduce-scatter.16

commit v6 on v5

--- a/solution.py
+++ b/solution.py
@@ -1028,7 +1028,7 @@
         small[j] = jnp.where(home[0], first, last).astype(BF16)
     small[0] = needing(small[0], back_first[0])
     small = scatter_row(small)
-    back_first.append(shift(needing(sums_first[2], small), "section", [(1, 0)]))
+    back_first.append(shift(sums_first[2], "section", [(1, 0)]))
 
     def expert_gradient(j):
         at = order.index(j)

time: 1280 us -> 1290 us (level)
  Pallas kernels: 234 us -> 251 us
  waiting for transfers between devices: 692 us -> 705 us
    reduce_scatter x6, waiting for transfers between devices: 0.03 us -> 17.8 us  [over_rows(): lax.psum_scatter(grad, 'row', scatter_dimension=(1, 1, 2)[j], tiled=True)]
    pallas_call x8, Pallas kernels: 127 us -> 144 us  [expert_call(): pl.pallas_call(behind(kernel, len(ready)), grid=(local,), in_specs=[pl.Bl...]
  transfers between devices with their start and end apart: 135 -> 135, of which waited for: 72 -> 72; matrix products, arithmetic and copies ran while one was open for 13% -> 11% of each run, Pallas kernels for 15% -> 16%
where the time goes in v6:
time: 1290 us; the launch traced here: 1280 us
  waiting for transfers between devices  705 us (55%)
  Pallas kernels  251 us (19%)
  starting transfers between devices  137 us (11%)
  other arithmetic  114 us (9%)
  local copies, waits for them, and re-layouts  51.7 us (4%)
  between operations  17.8 us (1%)
    ppermute x120, waiting for transfers between devices, shift(): return lax.ppermute(value, axis, pairs)  527 us
    all_gather x5, waiting for transfers between devices, whole(): lax.all_gather(w, 'row', axis=axis, tiled=True)  147 us
    pallas_call x8, Pallas kernels, expert_call(): pl.pallas_call(behind(kernel, len(ready)), grid=(local,), in_specs=[pl.Bl...  144 us
    ppermute x120, starting transfers between devices, shift(): return lax.ppermute(value, axis, pairs)  130 us
    pallas_call x2, Pallas kernels, attend_back(): pl.pallas_call(attend_back_kernel, grid=(micro, groups), in_specs=[mine,...  36.5 us
    pallas_call x8, Pallas kernels, whole_call(): pl.pallas_call(behind(functools.partial(kernel, len(blocks)), len(ready))...  36.2 us
  transfers between devices with their start and end apart: 135, of which 72 were waited for; matrix products, arithmetic and copies ran while one was open for 11% of the time, Pallas kernels for 16%

profile of v6, /device:TPU:0, one launch (start us, length us, event | category | flops | bytes accessed | tf_op | source)
XLA Modules:
  0.0 1277.5 jit_solution(3701363709493607477)
XLA Ops:
  25.3 22.6 %collective-permute-done.20 = bf16[4,256,512]{2,1,0:T(8,128)(2,1)S(1)} collective-permute-done((bf16[4,256,512]{2,1,0:T(8,128)(2,1)S(1)}, bf16[4,256,512]{2,1,0:T(8,128)(2,1)S(1)}, u32[]{:S(2)}, u32[]{:S(2)}) %collective-permute-start.20) | collective-permute-done | bytes 1048608 | tf_op jit(solution)/shard_map/ppermute | solution.py:25
  49.0 13.1 %all-gather.20.cloned.1.call-done = bf16[1024,768]{1,0:T(8,128)(2,1)} async-done(((bf16[256,768]{1,0:T(8,128)(2,1)}), bf16[1024,768]{1,0:T(8,128)(2,1)}) %all-gather.20.cloned.1.call-update) | async-done | bytes 1572880 | tf_op jit(solution)/shard_map/all_gather | solution.py:931
  66.3 22.1 %collective-permute-done.21 = bf16[4,256,512]{2,1,0:T(8,128)(2,1)} collective-permute-done((bf16[4,256,512]{2,1,0:T(8,128)(2,1)S(1)}, bf16[4,256,512]{2,1,0:T(8,128)(2,1)}, u32[]{:S(2)}, u32[]{:S(2)}) %collective-permute-start.21) | collective-permute-done | bytes 1048608 | tf_op jit(solution)/shard_map/ppermute | solution.py:25
  89.9 22.4 %collective-permute-done.22 = bf16[4,512,256]{2,1,0:T(8,128)(2,1)S(1)} collective-permute-done((bf16[4,512,256]{2,1,0:T(8,128)(2,1)S(1)}, bf16[4,512,256]{2,1,0:T(8,128)(2,1)S(1)}, u32[]{:S(2)}, u32[]{:S(2)}) %collective-permute-start.22) | collective-permute-done | bytes 1048608 | tf_op jit(solution)/shard_map/ppermute | solution.py:25
  113.9 30.0 %all-gather.10.cloned.1.call-done.refs_6_.refs_7_ = bf16[4,1024,512]{2,1,0:T(8,128)(2,1)} async-done(((bf16[4,256,512]{2,1,0:T(8,128)(2,1)}), bf16[4,1024,512]{2,1,0:T(8,128)(2,1)}) %all-gather.10.cloned.1.call-update) | async-done | bytes 4194320 | tf_op jit(solution)/shard_map/all_gather | solution.py:946
  148.3 76.9 %all-gather.14.cloned.1.call-done.refs_4_.refs_9_ = bf16[4,512,1024]{2,1,0:T(8,128)(2,1)} async-done(((bf16[4,512,256]{2,1,0:T(8,128)(2,1)}), bf16[4,512,1024]{2,1,0:T(8,128)(2,1)}) %all-gather.14.cloned.1.call-update) | async-done | bytes 4194320 | tf_op jit(solution)/shard_map/all_gather | solution.py:946
  245.2 27.2 %collective-permute-done.3.refs_7_.refs_6_.refs_11_ = bf16[4,256,768]{2,1,0:T(8,128)(2,1)S(1)} collective-permute-done((bf16[4,256,768]{2,1,0:T(8,128)(2,1)S(1)}, bf16[4,256,768]{2,1,0:T(8,128)(2,1)S(1)}, u32[]{:S(2)}, u32[]{:S(2)}) %collective-permute-start.3) | collective-permute-done | bytes 1572896 | tf_op jit(solution)/shard_map/ppermute | solution.py:25
  329.7 11.4 shard_map.230
  361.6 14.3 %collective-permute-done.18.refs_4_ = bf16[2,192,1024]{2,1,0:T(8,128)(2,1)S(1)} collective-permute-done((bf16[2,192,1024]{2,1,0:T(8,128)(2,1)S(1)}, bf16[2,192,1024]{2,1,0:T(8,128)(2,1)S(1)}, u32[]{:S(2)}, u32[]{:S(2)}) %collective-permute-start.18) | collective-permute-done | bytes 786464 | tf_op jit(solution)/shard_map/ppermute | solution.py:25
  379.1 15.3 %shard_map.232 = (bf16[4,2,384,1024]{3,2,1,0:T(8,128)(2,1)}, bf16[4,2,384,1024]{3,2,1,0:T(8,128)(2,1)}, bf16[4,2,384,512]{3,2,1,0:T(8,128)(2,1)}) custom-call(s32[8]{0:T(128)} %reshape_squeeze.6.refs_0_.refs_1_, s32[4,2,768]{2,1,0:T(2,128)} %add_select_fusion.1.refs_1_, bf16[2,192,1024]{2,1,0:T(8,128)(2,1)} %copy-done.36, ...), custom_call_target="tpu_custom_call" | custom-call | flops 7516192768 | bytes 20971520 | tf_op jit(solution)/shard_map/pallas_call | solution.py:486
  394.4 11.9 shard_map.233
  489.8 11.7 shard_map.235
  520.8 15.5 %collective-permute-done.44.refs_4_ = bf16[2,192,1024]{2,1,0:T(8,128)(2,1)S(1)} collective-permute-done((bf16[2,192,1024]{2,1,0:T(8,128)(2,1)S(1)}, bf16[2,192,1024]{2,1,0:T(8,128)(2,1)S(1)}, u32[]{:S(2)}, u32[]{:S(2)}) %collective-permute-start.44) | collective-permute-done | bytes 786464 | tf_op jit(solution)/shard_map/ppermute | solution.py:25
  538.8 17.2 %shard_map.237 = (bf16[4,2,384,1024]{3,2,1,0:T(8,128)(2,1)}, bf16[4,2,384,1024]{3,2,1,0:T(8,128)(2,1)}, bf16[4,2,384,512]{3,2,1,0:T(8,128)(2,1)}) custom-call(s32[8]{0:T(128)} %reshape_squeeze.7.refs_0_.refs_1_, s32[4,2,768]{2,1,0:T(2,128)} %add_select_fusion.refs_1_, bf16[2,192,1024]{2,1,0:T(8,128)(2,1)} %copy-done.35, bf16[2,192,1024]{2,1,0:T(8,128)(2,1)} %copy-done.66, ...), custom_call_target="tpu_custom_call" | custom-call | flops 7516192768 | bytes 20971520 | tf_op jit(solution)/shard_map/pallas_call | solution.py:486
  556.0 39.6 %all-gather.18.cloned.1.call-done.refs_4_.refs_9_ = bf16[4,512,1024]{2,1,0:T(8,128)(2,1)} async-done(((bf16[4,512,256]{2,1,0:T(8,128)(2,1)}), bf16[4,512,1024]{2,1,0:T(8,128)(2,1)}) %all-gather.18.cloned.1.call-update) | async-done | bytes 4194320 | tf_op jit(solution)/shard_map/all_gather | solution.py:946
  595.6 14.1 %shard_map.238 = bf16[4,2,192,1024]{3,2,1,0:T(8,128)(2,1)} custom-call(s32[8]{0:T(128)} %reshape_squeeze.7.refs_0_.refs_1_, s32[4,2,768]{2,1,0:T(2,128)} %add_select_fusion.refs_1_, f32[4,2,768]{2,1,0:T(2,128)} %fusion.37.refs_2_, bf16[4,2,384,512]{3,2,1,0:T(8,128)(2,1)} %get-tuple-element.101.refs_3_, ...), custom_call_target="tpu_custom_call" | custom-call | flops 5368709120 | bytes 10485760 | tf_op jit(solution)/shard_map/pallas_call | solution.py:486
  653.7 17.2 %collective-permute-done.59.refs_5_ = bf16[2,192,1024]{2,1,0:T(8,128)(2,1)S(1)} collective-permute-done((bf16[2,192,1024]{2,1,0:T(8,128)(2,1)S(1)}, bf16[2,192,1024]{2,1,0:T(8,128)(2,1)S(1)}, u32[]{:S(2)}, u32[]{:S(2)}) %collective-permute-start.59) | collective-permute-done | bytes 786464 | tf_op jit(solution)/shard_map/ppermute | solution.py:25
  674.1 33.7 %shard_map.239 = (bf16[4,2,192,1024]{3,2,1,0:T(8,128)(2,1)}, bf16[4,2,384,1024]{3,2,1,0:T(8,128)(2,1)}, bf16[4,512,1024]{2,1,0:T(8,128)(2,1)}) custom-call(s32[8]{0:T(128)} %reshape_squeeze.7.refs_0_.refs_1_, s32[4,2,768]{2,1,0:T(2,128)} %add_select_fusion.refs_1_, f32[4,2,768]{2,1,0:T(2,128)} %fusion.37.refs_2_, bf16[2,192,1024]{2,1,0:T(8,128)(2,1)} %copy-done.38, ...), custom_call_target="tpu_custom_call" | custom-call | flops 15032385536 | bytes 23068672 | tf_op jit(solution)/shard_map/pallas_call | solution.py:486
  726.3 11.6 shard_map.250
  759.6 17.9 %shard_map.241 = (bf16[1,192,1024]{2,1,0:T(8,128)(2,1)}, bf16[1,1536,1024]{2,1,0:T(8,128)(2,1)}) custom-call(bf16[1,192,2048]{2,1,0:T(8,128)(2,1)} %bitcast.388, bf16[1,1536,1024]{2,1,0:T(8,128)(2,1)} %bitcast.370, bf16[1,1536,1024]{2,1,0:T(8,128)(2,1)} %bitcast.371, f32[1536,768]{1,0:T(8,128)} %compare_select_fusion.bias_ref, ...), custom_call_target="tpu_custom_call" | custom-call | flops 6039797760 | bytes 11010048 | tf_op jit(solution)/shard_map/pallas_call | solution.py:417
  783.6 17.8 %collective-permute-done.70 = bf16[384,1024]{1,0:T(8,128)(2,1)S(1)} collective-permute-done((bf16[384,1024]{1,0:T(8,128)(2,1)S(1)}, bf16[384,1024]{1,0:T(8,128)(2,1)S(1)}, u32[]{:S(2)}, u32[]{:S(2)}) %collective-permute-start.70) | collective-permute-done | bytes 786464 | tf_op jit(solution)/shard_map/ppermute | solution.py:25
  828.8 11.2 collective-permute-done.74
  842.7 17.2 %collective-permute-done.75.refs_5_ = bf16[2,192,1024]{2,1,0:T(8,128)(2,1)} collective-permute-done((bf16[2,192,1024]{2,1,0:T(8,128)(2,1)S(1)}, bf16[2,192,1024]{2,1,0:T(8,128)(2,1)}, u32[]{:S(2)}, u32[]{:S(2)}) %collective-permute-start.75) | collective-permute-done | bytes 786464 | tf_op jit(solution)/shard_map/ppermute | solution.py:25
  862.5 28.6 %shard_map.244 = (bf16[4,2,192,1024]{3,2,1,0:T(8,128)(2,1)}, bf16[4,2,384,1024]{3,2,1,0:T(8,128)(2,1)}, bf16[4,512,1024]{2,1,0:T(8,128)(2,1)}) custom-call(s32[8]{0:T(128)} %reshape_squeeze.6.refs_0_.refs_1_, s32[4,2,768]{2,1,0:T(2,128)} %add_select_fusion.1.refs_1_, f32[4,2,768]{2,1,0:T(2,128)} %fusion.36.refs_2_, bf16[2,192,1024]{2,1,0:T(8,128)(2,1)} %copy-done.37, ...), custom_call_target="tpu_custom_call" | custom-call | flops 15032385536 | bytes 23068672 | tf_op jit(solution)/shard_map/pallas_call | solution.py:486
  911.7 11.1 shard_map.249
  958.2 18.7 %shard_map.246 = (bf16[1,192,1024]{2,1,0:T(8,128)(2,1)}, bf16[1,1536,1024]{2,1,0:T(8,128)(2,1)}) custom-call(bf16[1,192,2048]{2,1,0:T(8,128)(2,1)} %bitcast.386, bf16[1,1536,1024]{2,1,0:T(8,128)(2,1)} %bitcast.374, bf16[1,1536,1024]{2,1,0:T(8,128)(2,1)} %bitcast.375, f32[1536,768]{1,0:T(8,128)} %compare_select_fusion.bias_ref, ...), custom_call_target="tpu_custom_call" | custom-call | flops 6039797760 | bytes 11010048 | tf_op jit(solution)/shard_map/pallas_call | solution.py:417
  992.0 16.3 %collective-permute-done.118 = bf16[4,256,512]{2,1,0:T(8,128)(2,1)} collective-permute-done((bf16[4,256,512]{2,1,0:T(8,128)(2,1)}, bf16[4,256,512]{2,1,0:T(8,128)(2,1)}, u32[]{:S(2)}, u32[]{:S(2)}) %collective-permute-start.118) | collective-permute-done | bytes 1048608 | tf_op jit(solution)/shard_map/ppermute | solution.py:25
  1022.4 11.6 collective-permute-done.91
  1113.0 35.0 %collective-permute-done.103 = bf16[2,192,256]{2,1,0:T(8,128)(2,1)S(1)} collective-permute-done((bf16[2,192,256]{2,1,0:T(8,128)(2,1)S(1)}, bf16[2,192,256]{2,1,0:T(8,128)(2,1)S(1)}, u32[]{:S(2)}, u32[]{:S(2)}) %collective-permute-start.103) | collective-permute-done | bytes 196640 | tf_op jit(solution)/shard_map/ppermute | solution.py:25
  1198.9 17.7 %reduce-scatter.17.cloned.1.call-done = bf16[4,256,512]{2,1,0:T(8,128)(2,1)} async-done(((bf16[4,1024,512]{2,1,0:T(8,128)(2,1)}), bf16[4,256,512]{2,1,0:T(8,128)(2,1)}) %reduce-scatter.17.cloned.1.call-update) | async-done | bytes 1048592 | tf_op jit(solution)/shard_map/reduce_scatter | solution.py:1016
  1234.7 12.5 collective-permute-done.117
  1249.6 18.7 %collective-permute-done.119 = bf16[4,256,512]{2,1,0:T(8,128)(2,1)S(1)} collective-permute-done((bf16[4,256,512]{2,1,0:T(8,128)(2,1)S(1)}, bf16[4,256,512]{2,1,0:T(8,128)(2,1)S(1)}, u32[]{:S(2)}, u32[]{:S(2)}) %collective-permute-start.119) | collective-permute-done | bytes 1048608 | tf_op jit(solution)/shard_map/ppermute | solution.py:25
  (641 shorter events, 597.4 us)
Async XLA Ops:
  7.2 54.9 %all-gather.20.cloned.1.call-start = ((), (), s32[]{:S(2)}) async-start(), calls=%async_computation.19 | async-start | bytes 1966080 | tf_op jit(solution)/shard_map/all_gather | solution.py:931
  23.3 120.5 %all-gather.10.cloned.1.call-start = ((), (), s32[]{:S(2)}) async-start(), calls=%async_computation.8 | async-start | bytes 5242880 | tf_op jit(solution)/shard_map/all_gather | solution.py:946
  62.1 163.0 %all-gather.14.cloned.1.call-start = ((), (), s32[]{:S(2)}) async-start(), calls=%async_computation.10 | async-start | bytes 5242880 | tf_op jit(solution)/shard_map/all_gather | solution.py:946
  113.8 263.6 %all-gather.22.cloned.1.call-start = ((), (), s32[]{:S(2)}) async-start(), calls=%async_computation.20 | async-start | bytes 1966080 | tf_op jit(solution)/shard_map/all_gather | solution.py:931
  143.9 235.2 %all-gather.12.cloned.1.call-start = ((), (), s32[]{:S(2)}) async-start(), calls=%async_computation.9 | async-start | bytes 5242880 | tf_op jit(solution)/shard_map/all_gather | solution.py:946
  146.6 392.1 %all-gather.16.cloned.1.call-start = ((), (), s32[]{:S(2)}) async-start(), calls=%async_computation.11 | async-start | bytes 10485760 | tf_op jit(solution)/shard_map/all_gather | solution.py:946
  227.8 52.6 %all-to-all-start = ((bf16[1,4,192,256]{3,2,0,1:T(8,128)(2,1)}), bf16[1,4,192,256]{3,2,0,1:T(8,128)(2,1)S(1)}, u32[]{:S(2)}, u32[]{:S(2)}) async-start(bf16[1,4,192,256]{3,2,0,1:T(8,128)(2,1)} %maximum_bitcast_fusion), calls=%async_computation | async-start | bytes 786432 | tf_op jit(solution)/shard_map/all_to_all | solution.py:789
  231.3 364.3 %all-gather.18.cloned.1.call-start = ((), (), s32[]{:S(2)}) async-start(), calls=%async_computation.12 | async-start | bytes 5242880 | tf_op jit(solution)/shard_map/all_gather | solution.py:946
  232.0 47.1 %collective-permute-start = (f32[2,1024]{1,0:T(2,128)}, f32[2,1024]{1,0:T(2,128)}, u32[]{:S(2)}, u32[]{:S(2)}) collective-permute-start(f32[2,1024]{1,0:T(2,128)} %maximum_convert_fusion.3), channel_id=1, source_target_pairs={{0,16},{16,0},{1,17},{17,1},{2,18},{18,2},{3,19},{19,3},{4,20},{20... | collective-permute-start | bytes 24584 | tf_op jit(solution)/shard_map/ppermute | solution.py:25
  233.4 76.4 %collective-permute-start.14 = (s32[2,768,8]{1,2,0:T(8,128)}, s32[2,768,8]{1,2,0:T(8,128)}, u32[]{:S(2)}, u32[]{:S(2)}) collective-permute-start(s32[2,768,8]{1,2,0:T(8,128)} %bitcast.17), channel_id=1, source_target_pairs={{0,16},{16,0},{1,17},{17,1},{2,18},{18,2},{3,19},{19,3},{4,20},{20... | collective-permute-start | bytes 147464 | tf_op jit(solution)/shard_map/ppermute | solution.py:25
  234.0 125.9 %collective-permute-start.15 = (f32[2,768,8]{1,2,0:T(8,128)}, f32[2,768,8]{1,2,0:T(8,128)}, u32[]{:S(2)}, u32[]{:S(2)}) collective-permute-start(f32[2,768,8]{1,2,0:T(8,128)} %bitcast.24), channel_id=1, source_target_pairs={{0,16},{16,0},{1,17},{17,1},{2,18},{18,2},{3,19},{19,3},{4,20},{20... | collective-permute-start | bytes 147464 | tf_op jit(solution)/shard_map/ppermute | solution.py:25
  620.0 239.9 %reduce-scatter.7.cloned.1.call-start = ((), (), s32[]{:S(2)}) async-start(), calls=%async_computation.13 | async-start | bytes 5242880 | tf_op jit(solution)/shard_map/reduce_scatter | solution.py:1016
  707.8 190.6 %reduce-scatter.11.cloned.1.call-start = ((), (), s32[]{:S(2)}) async-start(), calls=%async_computation.15 | async-start | bytes 5242880 | tf_op jit(solution)/shard_map/reduce_scatter | solution.py:1016
  738.0 245.3 %reduce-scatter.15.cloned.1.call-start = ((), (), s32[]{:S(2)}) async-start(), calls=%async_computation.17 | async-start | bytes 5242880 | tf_op jit(solution)/shard_map/reduce_scatter | solution.py:1016
  738.6 423.7 %reduce-scatter.9.cloned.1.call-start = ((), (), s32[]{:S(2)}) async-start(), calls=%async_computation.14 | async-start | bytes 5242880 | tf_op jit(solution)/shard_map/reduce_scatter | solution.py:1016
  891.2 305.4 %reduce-scatter.13.cloned.1.call-start = ((), (), s32[]{:S(2)}) async-start(), calls=%async_computation.16 | async-start | bytes 5242880 | tf_op jit(solution)/shard_map/reduce_scatter | solution.py:1016
  927.6 289.0 %reduce-scatter.17.cloned.1.call-start = ((), (), s32[]{:S(2)}) async-start(), calls=%async_computation.18 | async-start | bytes 5242880 | tf_op jit(solution)/shard_map/reduce_scatter | solution.py:1016
  938.6 38.3 %collective-permute-start.78 = (bf16[4,256,768]{2,1,0:T(8,128)(2,1)}, bf16[4,256,768]{2,1,0:T(8,128)(2,1)}, u32[]{:S(2)}, u32[]{:S(2)}) collective-permute-start(bf16[4,256,768]{2,1,0:T(8,128)(2,1)} %pad_maximum_fusion.2), channel_id=1, source_target_pairs={{0,1},{1,0},{2,3},{3,2},{4,5},{5,4},{6,7},{7,6},{8,9},{9,8},{10,11... | collective-permute-start | bytes 4718600 | tf_op jit(solution)/shard_map/ppermute | solution.py:25
  942.0 41.3 %collective-permute-start.56 = (bf16[2,192,256]{2,1,0:T(8,128)(2,1)}, bf16[2,192,256]{2,1,0:T(8,128)(2,1)}, u32[]{:S(2)}, u32[]{:S(2)}) collective-permute-start(bf16[2,192,256]{2,1,0:T(8,128)(2,1)} %get-tuple-element.239), channel_id=1, source_target_pairs={{0,3},{1,2},{2,1},{3,0},{4,7},{5,6},{6,5},{7,4},{8,11},{9,10},{10,... | collective-permute-start | bytes 589832 | tf_op jit(solution)/shard_map/ppermute | solution.py:25
  943.3 40.0 %collective-permute-start.55 = (bf16[2,192,256]{2,1,0:T(8,128)(2,1)}, bf16[2,192,256]{2,1,0:T(8,128)(2,1)}, u32[]{:S(2)}, u32[]{:S(2)}) collective-permute-start(bf16[2,192,256]{2,1,0:T(8,128)(2,1)} %get-tuple-element.240), channel_id=1, source_target_pairs={{0,2},{1,3},{2,0},{3,1},{4,6},{5,7},{6,4},{7,5},{8,10},{9,11},{10,... | collective-permute-start | bytes 589832 | tf_op jit(solution)/shard_map/ppermute | solution.py:25
  951.6 58.0 %collective-permute-start.77 = (bf16[4,256,768]{2,1,0:T(8,128)(2,1)}, bf16[4,256,768]{2,1,0:T(8,128)(2,1)}, u32[]{:S(2)}, u32[]{:S(2)}) collective-permute-start(bf16[4,256,768]{2,1,0:T(8,128)(2,1)} %pad_maximum_fusion.1), channel_id=1, source_target_pairs={{0,1},{1,0},{2,3},{3,2},{4,5},{5,4},{6,7},{7,6},{8,9},{9,8},{10,11... | collective-permute-start | bytes 4718600 | tf_op jit(solution)/shard_map/ppermute | solution.py:25
  980.3 37.5 %collective-permute-start.79 = (bf16[4,256,768]{2,1,0:T(8,128)(2,1)}, bf16[4,256,768]{2,1,0:T(8,128)(2,1)}, u32[]{:S(2)}, u32[]{:S(2)}) collective-permute-start(bf16[4,256,768]{2,1,0:T(8,128)(2,1)} %add_convert_fusion.4), channel_id=1, source_target_pairs={{0,2},{1,3},{2,0},{3,1},{4,6},{5,7},{6,4},{7,5},{8,10},{9,11},{10,... | collective-permute-start | bytes 4718600 | tf_op jit(solution)/shard_map/ppermute | solution.py:25
  991.8 42.3 %collective-permute-start.91 = (bf16[384,1024]{1,0:T(8,128)(2,1)}, bf16[384,1024]{1,0:T(8,128)(2,1)}, u32[]{:S(2)}, u32[]{:S(2)}) collective-permute-start(bf16[384,1024]{1,0:T(8,128)(2,1)} %fusion.2), channel_id=1, source_target_pairs={{0,2},{1,3},{2,0},{3,1},{4,6},{5,7},{6,4},{7,5},{8,10},{9,11},{10,... | collective-permute-start | bytes 2359304 | tf_op jit(solution)/shard_map/ppermute | solution.py:25
  1020.8 50.1 %collective-permute-start.80 = (bf16[4,256,768]{2,1,0:T(8,128)(2,1)S(1)}, bf16[4,256,768]{2,1,0:T(8,128)(2,1)S(1)}, u32[]{:S(2)}, u32[]{:S(2)}) collective-permute-start(bf16[4,256,768]{2,1,0:T(8,128)(2,1)S(1)} %add_convert_fusion.3.refs_0_), channel_id=1, source_target_pairs={{0,16},{1,17},{2,18},{3,19},{4,20},{5,21},{6,22},{7,23},{8,24},{9,... | collective-permute-start | bytes 4718600 | tf_op jit(solution)/shard_map/ppermute | solution.py:25
  1103.8 48.8 %collective-permute-start.104 = (bf16[4,256,768]{2,1,0:T(8,128)(2,1)}, bf16[4,256,768]{2,1,0:T(8,128)(2,1)}, u32[]{:S(2)}, u32[]{:S(2)}) collective-permute-start(bf16[4,256,768]{2,1,0:T(8,128)(2,1)} %pad_maximum_fusion.3), channel_id=1, source_target_pairs={{0,1},{1,0},{2,3},{3,2},{4,5},{5,4},{6,7},{7,6},{8,9},{9,8},{10,11... | collective-permute-start | bytes 4718600 | tf_op jit(solution)/shard_map/ppermute | solution.py:25
  1109.1 43.5 %collective-permute-start.106 = (bf16[4,256,768]{2,1,0:T(8,128)(2,1)}, bf16[4,256,768]{2,1,0:T(8,128)(2,1)}, u32[]{:S(2)}, u32[]{:S(2)}) collective-permute-start(bf16[4,256,768]{2,1,0:T(8,128)(2,1)} %add_convert_fusion.1), channel_id=1, source_target_pairs={{0,2},{1,3},{2,0},{3,1},{4,6},{5,7},{6,4},{7,5},{8,10},{9,11},{10,... | collective-permute-start | bytes 4718600 | tf_op jit(solution)/shard_map/ppermute | solution.py:25
  1109.9 38.1 %collective-permute-start.103 = (bf16[2,192,256]{2,1,0:T(8,128)(2,1)S(1)}, bf16[2,192,256]{2,1,0:T(8,128)(2,1)S(1)}, u32[]{:S(2)}, u32[]{:S(2)}) collective-permute-start(bf16[2,192,256]{2,1,0:T(8,128)(2,1)S(1)} %get-tuple-element.224), channel_id=1, source_target_pairs={{0,3},{1,2},{2,1},{3,0},{4,7},{5,6},{6,5},{7,4},{8,11},{9,10},{10,... | collective-permute-start | bytes 589832 | tf_op jit(solution)/shard_map/ppermute | solution.py:25
  1109.9 42.4 %collective-permute-start.102 = (bf16[2,192,256]{2,1,0:T(8,128)(2,1)S(1)}, bf16[2,192,256]{2,1,0:T(8,128)(2,1)S(1)}, u32[]{:S(2)}, u32[]{:S(2)}) collective-permute-start(bf16[2,192,256]{2,1,0:T(8,128)(2,1)S(1)} %get-tuple-element.225), channel_id=1, source_target_pairs={{0,2},{1,3},{2,0},{3,1},{4,6},{5,7},{6,4},{7,5},{8,10},{9,11},{10,... | collective-permute-start | bytes 589832 | tf_op jit(solution)/shard_map/ppermute | solution.py:25
  1111.6 40.7 %collective-permute-start.101 = (bf16[2,192,256]{2,1,0:T(8,128)(2,1)S(1)}, bf16[2,192,256]{2,1,0:T(8,128)(2,1)S(1)}, u32[]{:S(2)}, u32[]{:S(2)}) collective-permute-start(bf16[2,192,256]{2,1,0:T(8,128)(2,1)S(1)} %get-tuple-element.226), channel_id=1, source_target_pairs={{0,1},{1,0},{2,3},{3,2},{4,5},{5,4},{6,7},{7,6},{8,9},{9,8},{10,11... | collective-permute-start | bytes 589832 | tf_op jit(solution)/shard_map/ppermute | solution.py:25
  1161.0 62.0 %collective-permute-start.107 = (bf16[256,768]{1,0:T(8,128)(2,1)S(1)}, bf16[256,768]{1,0:T(8,128)(2,1)}, u32[]{:S(2)}, u32[]{:S(2)}) collective-permute-start(bf16[256,768]{1,0:T(8,128)(2,1)S(1)} %get-tuple-element.205), channel_id=1, source_target_pairs={{16,0},{17,1},{18,2},{19,3},{20,4},{21,5},{22,6},{23,7},{24,8},{25... | collective-permute-start | bytes 1179656 | tf_op jit(solution)/shard_map/ppermute | solution.py:25
  1162.3 55.8 %collective-permute-start.109 = (bf16[4,512,256]{2,1,0:T(8,128)(2,1)}, bf16[4,512,256]{2,1,0:T(8,128)(2,1)}, u32[]{:S(2)}, u32[]{:S(2)}) collective-permute-start(bf16[4,512,256]{2,1,0:T(8,128)(2,1)} %reduce-scatter.9.cloned.1.call-done), channel_id=1, source_target_pairs={{16,0},{17,1},{18,2},{19,3},{20,4},{21,5},{22,6},{23,7},{24,8},{25... | collective-permute-start | bytes 3145736 | tf_op jit(solution)/shard_map/ppermute | solution.py:25
  1223.0 45.3 %collective-permute-start.119 = (bf16[4,256,512]{2,1,0:T(8,128)(2,1)S(1)}, bf16[4,256,512]{2,1,0:T(8,128)(2,1)S(1)}, u32[]{:S(2)}, u32[]{:S(2)}) collective-permute-start(bf16[4,256,512]{2,1,0:T(8,128)(2,1)S(1)} %copy-done.33), channel_id=1, source_target_pairs={{16,0},{17,1},{18,2},{19,3},{20,4},{21,5},{22,6},{23,7},{24,8},{25... | collective-permute-start | bytes 3145736 | tf_op jit(solution)/shard_map/ppermute | solution.py:25
  (173 other events, 2827.7 us)
Sparse Core Ops, SparseCore 0:
  23.5 38.5 all-gather.19
  64.2 79.6 all-gather.9
  146.0 79.0 all-gather.13
  226.6 35.2 all-gather.21
  263.9 90.6 all-gather.11
  356.0 159.2 all-gather.15
  516.9 78.6 all-gather.17
  707.9 73.0 reduce-scatter.6
  783.9 85.6 reduce-scatter.10
  871.8 78.6 reduce-scatter.14
  953.4 77.2 reduce-scatter.8
  1033.5 86.5 reduce-scatter.12
  1123.0 93.5 reduce-scatter.16
